TPU v7x, 32 devices: a whole 2x2x4 slice. The times are simulated.
32 devices in a mesh: section: 8 (over z, x), ctx: 4 (over y, core).
Axes of the slice: x: 2, y: 2, z: 4, core: 2. Of those that a mesh axis runs over, the one named last changes fastest.
Arguments:
- queries: bfloat16 [8, 1024, 16, 128], P('section', 'ctx'), may hold values from -12 to 12
- keys: bfloat16 [8, 1024, 128], P('section', 'ctx'), may hold values from -6 to 6
- values: bfloat16 [8, 1024, 128], P('section', 'ctx'), may hold values from -6 to 6
- outputs: bfloat16 [8, 1024, 16, 128], P('section', 'ctx'), may hold values from -6 to 6, as said below
- grad_held: bfloat16 [8, 1024, 16, 128], P('section', 'ctx'), may hold values from -24 to 24
- lse: float32 [8, 16, 1024], P('section', None, 'ctx'), as said below
- span_start: int32 [8], replicated, may hold values from 0 to 896, as said below
Outputs:
- query_grad: bfloat16 [8, 1024, 16, 128], P('section', 'ctx')
- key_grad: bfloat16 [8, 1024, 128], P('section', 'ctx')
- value_grad: bfloat16 [8, 1024, 128], P('section', 'ctx')
Inputs may be any that keep to these rules, and one draw needn't show every extreme that they name: `span_start`: each multiple of 128 below 1024 appears once. Entries 2 k and 2 k + 1 are the spans held by index k of ctx; they add up to 896, the smaller first. lse[s, h, i] is the log of the sum of exp(scores[s, h, i, j]) over the j with positions[j] <= positions[i]. outputs[s, i, h] is the sum over j of probs[s, h, i, j] values[s, j], rounded once.
All inputs are finite; a program needn't handle non-finite values.
Results may differ from a plain program's by a relative error of at most 0.014.
Values may be sent and summed in bfloat16 or wider, within the bound.
No kernel may reach another device: no remote copies, remote signals or barrier semaphores. Data moves between devices by JAX's collectives and lax.ppermute only.
A program may use at most 64 MiB of HBM per device.

v0:
```python
import jax
import jax.numpy as jnp
from jax import lax
from jax.sharding import PartitionSpec as P


def from_behind(shard, axis, by):
    length = lax.axis_size(axis)
    return lax.ppermute(shard, axis, [(i, (i + by) % length) for i in range(length)])


def tile_grads(
    query_rows, grad_rows, lse_rows, delta_rows, query_pos, key_rows, value_rows, key_pos
):
    score_scale = query_rows.shape[-1] ** (-0.5)
    scores = (
        jnp.einsum("rhd,cd->hrc", query_rows, key_rows, preferred_element_type=jnp.float32)
        * score_scale
    )
    allowed = key_pos[None, :] <= query_pos[:, None]
    probs = jnp.where(allowed[None], jnp.exp(scores - lse_rows[:, :, None]), 0.0)
    probs_low = probs.astype(jnp.bfloat16)
    grad_probs = jnp.einsum(
        "rhd,cd->hrc", grad_rows, value_rows, preferred_element_type=jnp.float32
    )
    grad_scores = (probs * (grad_probs - delta_rows[:, :, None])).astype(jnp.bfloat16)
    query_grad = (
        jnp.einsum("hrc,cd->rhd", grad_scores, key_rows, preferred_element_type=jnp.float32)
        * score_scale
    )
    key_grad = (
        jnp.einsum("hrc,rhd->cd", grad_scores, query_rows, preferred_element_type=jnp.float32)
        * score_scale
    )
    value_grad = jnp.einsum("hrc,rhd->cd", probs_low, grad_rows, preferred_element_type=jnp.float32)
    return (query_grad, key_grad, value_grad)


def sweep_keys(query_side, key_rows, value_rows):
    queries, grad_out, lse_rows, delta_rows, query_pos, own_starts, span_start = query_side
    row_count = queries.shape[0]
    span_rows = row_count // 2
    head_size = key_rows.shape[1]
    block_count = key_rows.shape[0] // row_count
    offsets = jnp.arange(span_rows, dtype=jnp.int32)
    query_init = jnp.zeros(queries.shape, jnp.float32)
    keys_init = jnp.zeros((key_rows.shape[0], 2 * head_size), jnp.float32)

    def sweep_turn(block_index, totals):
        query_total, key_total = totals
        key_block = lax.dynamic_slice_in_dim(key_rows, block_index * row_count, row_count, 0)
        value_block = lax.dynamic_slice_in_dim(value_rows, block_index * row_count, row_count, 0)
        block_starts = lax.dynamic_slice_in_dim(
            span_start, block_index * row_count // span_rows, 2, 0
        )
        key_pos = (block_starts[:, None] + offsets[None, :]).reshape(row_count)
        query_grad, key_grad, value_grad = tile_grads(
            queries, grad_out, lse_rows, delta_rows, query_pos, key_block, value_block, key_pos
        )
        query_total = query_total + query_grad
        key_total = lax.dynamic_update_slice_in_dim(
            key_total, jnp.concatenate([key_grad, value_grad], axis=1), block_index * row_count, 0
        )
        return (query_total, key_total)

    return lax.fori_loop(0, block_count, sweep_turn, (query_init, keys_init))


def body(queries, keys, values, outputs, grad_held, lse, span_start):
    grad_next = from_behind(grad_held, "section", -1)
    query_block = queries[0]
    key_block = keys[0]
    value_block = values[0]
    row_count = query_block.shape[0]
    span_rows = row_count // 2
    head_size = key_block.shape[1]
    context = lax.axis_index("ctx")
    own_starts = lax.dynamic_slice_in_dim(span_start, 2 * context, 2, 0)
    offsets = jnp.arange(span_rows, dtype=jnp.int32)
    query_pos = (own_starts[:, None] + offsets[None, :]).reshape(row_count)
    grad_out = grad_next[0]
    delta_rows = jnp.sum(grad_out.astype(jnp.float32) * outputs[0].astype(jnp.float32), axis=-1).T
    query_side = (query_block, grad_out, lse[0], delta_rows, query_pos, own_starts, span_start)
    query_add, key_value_part = sweep_keys(
        query_side,
        lax.all_gather(key_block, "ctx", axis=0, tiled=True),
        lax.all_gather(value_block, "ctx", axis=0, tiled=True),
    )
    key_value_full = key_value_part
    query_total, key_value_full = (query_add, key_value_full)
    summed = lax.psum_scatter(
        key_value_full.astype(jnp.bfloat16), "ctx", scatter_dimension=0, tiled=True
    ).astype(jnp.float32)
    query_out = query_total.astype(jnp.bfloat16)[None]
    key_out = summed[:, :head_size].astype(jnp.bfloat16)[None]
    value_out = summed[:, head_size:].astype(jnp.bfloat16)[None]
    return (query_out, key_out, value_out)


def solution(mesh):
    placed = (
        P("section", "ctx", None, None),
        P("section", "ctx", None),
        P("section", "ctx", None),
        P("section", "ctx", None, None),
        P("section", "ctx", None, None),
        P("section", None, "ctx"),
        P(),
    )
    return jax.shard_map(
        body,
        mesh=mesh,
        in_specs=placed,
        out_specs=(
            P("section", "ctx", None, None),
            P("section", "ctx", None),
            P("section", "ctx", None),
        ),
        check_vma=False,
    )
```

profile of v0, /device:TPU:0, one launch (start us, length us, event | category | flops | bytes accessed | tf_op | source)
XLA Modules:
  0.0 113.7 jit_solution(14910457138318509913)
XLA Ops:
  7.2 2.4 %copy.17 = bf16[1,256,16,128]{1,3,2,0:T(8,128)(2,1)} copy(bf16[1,256,16,128]{3,2,1,0:T(8,128)(2,1)} %param.13) | data formatting | bytes 2097152 | tf_op args[4]
  9.6 6.0 %collective-permute-start = (bf16[1,256,16,128]{1,3,2,0:T(8,128)(2,1)}, bf16[1,256,16,128]{1,3,2,0:T(8,128)(2,1)}, u32[]{:S(2)}, u32[]{:S(2)}) collective-permute-start(bf16[1,256,16,128]{1,3,2,0:T(8,128)(2,1)} %copy.17), channel_id=1, source_target_pairs={{0,28},{4,0},{8,4},{12,8},{16,12},{20,16},{24,20},{28,24},{1,29},{... | collective-permute-start | bytes 3145736 | tf_op jit(solution)/shard_map/ppermute | solution.py:9
  15.6 1.7 %copy.16 = bf16[1,256,16,128]{1,3,2,0:T(8,128)(2,1)S(1)} copy(bf16[1,256,16,128]{3,2,1,0:T(8,128)(2,1)} %param.9) | data formatting | bytes 2097152 | tf_op args[0]
  17.3 2.4 %copy.18 = bf16[1,256,16,128]{1,3,2,0:T(8,128)(2,1)} copy(bf16[1,256,16,128]{3,2,1,0:T(8,128)(2,1)} %param.12) | data formatting | bytes 2097152 | tf_op args[3]
  19.8 6.2 %all-gather = bf16[1,1024,128]{2,1,0:T(8,128)(2,1)} all-gather(bf16[1,256,128]{2,1,0:T(8,128)(2,1)S(1)} %copy-done), channel_id=2, replica_groups=mesh['section'=8,'ctx'=4] {'ctx'}, dimensions={1}, use_global_device_ids=true | all-gather | bytes 327680 | tf_op jit(solution)/shard_map/all_gather | solution.py:86
  26.0 6.3 %all-gather.1 = bf16[1,1024,128]{2,1,0:T(8,128)(2,1)} all-gather(bf16[1,256,128]{2,1,0:T(8,128)(2,1)S(1)} %copy-done.1), channel_id=3, replica_groups=mesh['section'=8,'ctx'=4] {'ctx'}, dimensions={1}, use_global_device_ids=true | all-gather | bytes 327680 | tf_op jit(solution)/shard_map/all_gather | solution.py:87
  32.3 6.0 %collective-permute-done = bf16[1,256,16,128]{1,3,2,0:T(8,128)(2,1)} collective-permute-done((bf16[1,256,16,128]{1,3,2,0:T(8,128)(2,1)}, bf16[1,256,16,128]{1,3,2,0:T(8,128)(2,1)}, u32[]{:S(2)}, u32[]{:S(2)}) %collective-permute-start) | collective-permute-done | bytes 1048608 | tf_op jit(solution)/shard_map/ppermute | solution.py:9
  38.3 1.8 %fusion.29 = f32[256,16]{0,1:T(8,128)S(1)} fusion(bf16[1,256,16,128]{1,3,2,0:T(8,128)(2,1)} %copy.18, bf16[1,256,16,128]{1,3,2,0:T(8,128)(2,1)} %collective-permute-done), kind=kLoop, calls=%fused_computation.34 | loop fusion | flops 2093056 | bytes 2113536 | tf_op jit(solution)/shard_map/reduce_sum | solution.py:82
  40.2 0.8 broadcast_in_dim.63.clone
  41.0 40.6 %while.18 = (s32[]{:T(128)}, f32[256,16,128]{0,2,1:T(8,128)S(1)}, bf16[1024,256]{1,0:T(8,128)(2,1)}, bf16[1024,128]{1,0:T(8,128)(2,1)}, s32[8]{0:T(128)S(1)}, /*...) while((s32[]{:T(128)}, f32[256,16,128]{0,2,1:T(8,128)S(1)}, ...), condition=%wide.region_2.3_spmd.clone, body=%wide.region_1.2_spmd.clone.sunk | while | flops 1354629632 | bytes 28627408 | solution.py:66
  41.3 1.5 %fusion.61 = f32[256,256,16]{1,0,2:T(8,128)S(1)} fusion(bf16[256,16,128]{0,2,1:T(8,128)(2,1)S(1)} %get-tuple-element.474, bf16[1024,128]{1,0:T(8,128)(2,1)} %get-tuple-element.472, s32[]{:T(128)S(6)} %select_n.68), kind=kOutput, calls=%fused_computation.18.clone.1 | convolution fusion | flops 268435456 | bytes 5308420 | tf_op jit(solution)/shard_map/while/body/eval_jaxpr/rhd,cd->hrc/dot_general | solution.py:17
  42.8 2.2 %fusion.64 = bf16[256,128]{0,1:T(8,128)(2,1)S(1)} fusion(bf16[256,16,128]{0,2,1:T(8,128)(2,1)} %get-tuple-element.477, f32[256,256,16]{1,0,2:T(8,128)S(1)} %fusion.61, f32[16,256]{1,0:T(8,128)S(1)} %bitcast.100, pred[256,256]{0,1:T(8,128)(4,1)S(1)} %broadcast_compare_fusion.2), kind=kOutput, calls=%fused_computation.12.clone.1 | convolution fusion | flops 272629760 | bytes 5390336 | tf_op jit(solution)/shard_map/while/body/eval_jaxpr/hrc,rhd->cd/dot_general | solution.py:35
  45.0 2.7 %fusion.63 = bf16[16,256,256]{1,2,0:T(8,128)(2,1)S(1)} fusion(f32[256,256,16]{1,0,2:T(8,128)S(1)} %fusion.61, bf16[256,16,128]{0,2,1:T(8,128)(2,1)} %get-tuple-element.477, f32[16,256]{1,0:T(8,128)S(1)} %get-tuple-element.478, f32[16,256]{1,0:T(8,128)S(1)} %bitcast.101, pred[256,256]{0,1:T(8,128)(4,1)S(1)} %broadcast_compare_fusion.2, ...), kind=kOutput, calls=%fused_computation.4.clone.1 | convolution fusion | flops 274726912 | bytes 7503876 | tf_op jit(solution)/shard_map/while/body/eval_jaxpr/rhd,cd->hrc/dot_general | solution.py:23
  47.7 0.8 fusion.65
  48.5 1.8 %bitcast_add_fusion.2 = f32[256,16,128]{0,2,1:T(8,128)S(1)} fusion(f32[256,16,128]{0,2,1:T(8,128)S(1)} %get-tuple-element.451, bf16[16,256,256]{1,2,0:T(8,128)(2,1)S(1)} %fusion.63, pred[]{:T(512)S(6)} %compare.11, bf16[1024,128]{1,0:T(8,128)(2,1)} %get-tuple-element.472, s32[]{:T(128)S(6)} %select_n.68), kind=kOutput, calls=%fused_computation.9.clone.1 | convolution fusion | flops 270008320 | bytes 6356997 | tf_op jit(solution)/shard_map/while/body/eval_jaxpr/hrc,cd->rhd/dot_general | solution.py:28
  51.4 1.5 %fusion.61 = f32[256,256,16]{1,0,2:T(8,128)S(1)} fusion(bf16[256,16,128]{0,2,1:T(8,128)(2,1)S(1)} %get-tuple-element.474, bf16[1024,128]{1,0:T(8,128)(2,1)} %get-tuple-element.472, s32[]{:T(128)S(6)} %select_n.68), kind=kOutput, calls=%fused_computation.18.clone.1 | convolution fusion | flops 268435456 | bytes 5308420 | tf_op jit(solution)/shard_map/while/body/eval_jaxpr/rhd,cd->hrc/dot_general | solution.py:17
  53.0 2.2 %fusion.64 = bf16[256,128]{0,1:T(8,128)(2,1)S(1)} fusion(bf16[256,16,128]{0,2,1:T(8,128)(2,1)} %get-tuple-element.477, f32[256,256,16]{1,0,2:T(8,128)S(1)} %fusion.61, f32[16,256]{1,0:T(8,128)S(1)} %bitcast.100, pred[256,256]{0,1:T(8,128)(4,1)S(1)} %broadcast_compare_fusion.2), kind=kOutput, calls=%fused_computation.12.clone.1 | convolution fusion | flops 272629760 | bytes 5390336 | tf_op jit(solution)/shard_map/while/body/eval_jaxpr/hrc,rhd->cd/dot_general | solution.py:35
  55.2 2.7 %fusion.63 = bf16[16,256,256]{1,2,0:T(8,128)(2,1)S(1)} fusion(f32[256,256,16]{1,0,2:T(8,128)S(1)} %fusion.61, bf16[256,16,128]{0,2,1:T(8,128)(2,1)} %get-tuple-element.477, f32[16,256]{1,0:T(8,128)S(1)} %get-tuple-element.478, f32[16,256]{1,0:T(8,128)S(1)} %bitcast.101, pred[256,256]{0,1:T(8,128)(4,1)S(1)} %broadcast_compare_fusion.2, ...), kind=kOutput, calls=%fused_computation.4.clone.1 | convolution fusion | flops 274726912 | bytes 7503876 | tf_op jit(solution)/shard_map/while/body/eval_jaxpr/rhd,cd->hrc/dot_general | solution.py:23
  57.8 0.8 fusion.65
  58.7 1.8 %bitcast_add_fusion.2 = f32[256,16,128]{0,2,1:T(8,128)S(1)} fusion(f32[256,16,128]{0,2,1:T(8,128)S(1)} %get-tuple-element.451, bf16[16,256,256]{1,2,0:T(8,128)(2,1)S(1)} %fusion.63, pred[]{:T(512)S(6)} %compare.11, bf16[1024,128]{1,0:T(8,128)(2,1)} %get-tuple-element.472, s32[]{:T(128)S(6)} %select_n.68), kind=kOutput, calls=%fused_computation.9.clone.1 | convolution fusion | flops 270008320 | bytes 6356997 | tf_op jit(solution)/shard_map/while/body/eval_jaxpr/hrc,cd->rhd/dot_general | solution.py:28
  61.6 1.5 %fusion.61 = f32[256,256,16]{1,0,2:T(8,128)S(1)} fusion(bf16[256,16,128]{0,2,1:T(8,128)(2,1)S(1)} %get-tuple-element.474, bf16[1024,128]{1,0:T(8,128)(2,1)} %get-tuple-element.472, s32[]{:T(128)S(6)} %select_n.68), kind=kOutput, calls=%fused_computation.18.clone.1 | convolution fusion | flops 268435456 | bytes 5308420 | tf_op jit(solution)/shard_map/while/body/eval_jaxpr/rhd,cd->hrc/dot_general | solution.py:17
  63.1 2.2 %fusion.64 = bf16[256,128]{0,1:T(8,128)(2,1)S(1)} fusion(bf16[256,16,128]{0,2,1:T(8,128)(2,1)} %get-tuple-element.477, f32[256,256,16]{1,0,2:T(8,128)S(1)} %fusion.61, f32[16,256]{1,0:T(8,128)S(1)} %bitcast.100, pred[256,256]{0,1:T(8,128)(4,1)S(1)} %broadcast_compare_fusion.2), kind=kOutput, calls=%fused_computation.12.clone.1 | convolution fusion | flops 272629760 | bytes 5390336 | tf_op jit(solution)/shard_map/while/body/eval_jaxpr/hrc,rhd->cd/dot_general | solution.py:35
  65.3 2.7 %fusion.63 = bf16[16,256,256]{1,2,0:T(8,128)(2,1)S(1)} fusion(f32[256,256,16]{1,0,2:T(8,128)S(1)} %fusion.61, bf16[256,16,128]{0,2,1:T(8,128)(2,1)} %get-tuple-element.477, f32[16,256]{1,0:T(8,128)S(1)} %get-tuple-element.478, f32[16,256]{1,0:T(8,128)S(1)} %bitcast.101, pred[256,256]{0,1:T(8,128)(4,1)S(1)} %broadcast_compare_fusion.2, ...), kind=kOutput, calls=%fused_computation.4.clone.1 | convolution fusion | flops 274726912 | bytes 7503876 | tf_op jit(solution)/shard_map/while/body/eval_jaxpr/rhd,cd->hrc/dot_general | solution.py:23
  68.8 1.8 %bitcast_add_fusion.2 = f32[256,16,128]{0,2,1:T(8,128)S(1)} fusion(f32[256,16,128]{0,2,1:T(8,128)S(1)} %get-tuple-element.451, bf16[16,256,256]{1,2,0:T(8,128)(2,1)S(1)} %fusion.63, pred[]{:T(512)S(6)} %compare.11, bf16[1024,128]{1,0:T(8,128)(2,1)} %get-tuple-element.472, s32[]{:T(128)S(6)} %select_n.68), kind=kOutput, calls=%fused_computation.9.clone.1 | convolution fusion | flops 270008320 | bytes 6356997 | tf_op jit(solution)/shard_map/while/body/eval_jaxpr/hrc,cd->rhd/dot_general | solution.py:28
  71.7 1.5 %fusion.61 = f32[256,256,16]{1,0,2:T(8,128)S(1)} fusion(bf16[256,16,128]{0,2,1:T(8,128)(2,1)S(1)} %get-tuple-element.474, bf16[1024,128]{1,0:T(8,128)(2,1)} %get-tuple-element.472, s32[]{:T(128)S(6)} %select_n.68), kind=kOutput, calls=%fused_computation.18.clone.1 | convolution fusion | flops 268435456 | bytes 5308420 | tf_op jit(solution)/shard_map/while/body/eval_jaxpr/rhd,cd->hrc/dot_general | solution.py:17
  73.2 2.2 %fusion.64 = bf16[256,128]{0,1:T(8,128)(2,1)S(1)} fusion(bf16[256,16,128]{0,2,1:T(8,128)(2,1)} %get-tuple-element.477, f32[256,256,16]{1,0,2:T(8,128)S(1)} %fusion.61, f32[16,256]{1,0:T(8,128)S(1)} %bitcast.100, pred[256,256]{0,1:T(8,128)(4,1)S(1)} %broadcast_compare_fusion.2), kind=kOutput, calls=%fused_computation.12.clone.1 | convolution fusion | flops 272629760 | bytes 5390336 | tf_op jit(solution)/shard_map/while/body/eval_jaxpr/hrc,rhd->cd/dot_general | solution.py:35
  75.5 2.7 %fusion.63 = bf16[16,256,256]{1,2,0:T(8,128)(2,1)S(1)} fusion(f32[256,256,16]{1,0,2:T(8,128)S(1)} %fusion.61, bf16[256,16,128]{0,2,1:T(8,128)(2,1)} %get-tuple-element.477, f32[16,256]{1,0:T(8,128)S(1)} %get-tuple-element.478, f32[16,256]{1,0:T(8,128)S(1)} %bitcast.101, pred[256,256]{0,1:T(8,128)(4,1)S(1)} %broadcast_compare_fusion.2, ...), kind=kOutput, calls=%fused_computation.4.clone.1 | convolution fusion | flops 274726912 | bytes 7503876 | tf_op jit(solution)/shard_map/while/body/eval_jaxpr/rhd,cd->hrc/dot_general | solution.py:23
  78.1 0.8 fusion.65
  78.9 1.9 %bitcast_add_fusion.2 = f32[256,16,128]{0,2,1:T(8,128)S(1)} fusion(f32[256,16,128]{0,2,1:T(8,128)S(1)} %get-tuple-element.451, bf16[16,256,256]{1,2,0:T(8,128)(2,1)S(1)} %fusion.63, pred[]{:T(512)S(6)} %compare.11, bf16[1024,128]{1,0:T(8,128)(2,1)} %get-tuple-element.472, s32[]{:T(128)S(6)} %select_n.68), kind=kOutput, calls=%fused_computation.9.clone.1 | convolution fusion | flops 270008320 | bytes 6356997 | tf_op jit(solution)/shard_map/while/body/eval_jaxpr/hrc,cd->rhd/dot_general | solution.py:28
  81.6 1.9 %copy.19 = bf16[256,16,128]{2,1,0:T(8,128)(2,1)} copy(f32[256,16,128]{0,2,1:T(8,128)S(1)} %get-tuple-element.291) | data formatting | bytes 3145728 | tf_op jit(solution)/shard_map/while | solution.py:66
  83.5 21.8 %reduce-scatter.2.cloned.1.call-done = bf16[256,256]{1,0:T(8,128)(2,1)} async-done(((bf16[1024,256]{1,0:T(8,128)(2,1)}), bf16[256,256]{1,0:T(8,128)(2,1)}) %reduce-scatter.2.cloned.1.call-update) | async-done | bytes 131088 | tf_op jit(solution)/shard_map/reduce_scatter | solution.py:91
  105.3 1.5 %slice_bitcast_fusion = (bf16[1,256,128]{2,1,0:T(8,128)(2,1)}, bf16[1,256,128]{2,1,0:T(8,128)(2,1)}) fusion(bf16[256,256]{1,0:T(8,128)(2,1)} %reduce-scatter.2.cloned.1.call-done), kind=kLoop, calls=%fused_computation.36 | loop fusion | bytes 262144 | tf_op jit(solution)/shard_map/broadcast_in_dim | solution.py:96
  (37 shorter events, 5.1 us)
Async XLA Ops:
  7.2 98.1 %reduce-scatter.2.cloned.1.call-start = ((), (), s32[]{:S(2)}) async-start(), calls=%async_computation.1 | async-start | bytes 655360 | tf_op jit(solution)/shard_map/reduce_scatter | solution.py:91
  9.6 28.7 %collective-permute-start = (bf16[1,256,16,128]{1,3,2,0:T(8,128)(2,1)}, bf16[1,256,16,128]{1,3,2,0:T(8,128)(2,1)}, u32[]{:S(2)}, u32[]{:S(2)}) collective-permute-start(bf16[1,256,16,128]{1,3,2,0:T(8,128)(2,1)} %copy.17), channel_id=1, source_target_pairs={{0,28},{4,0},{8,4},{12,8},{16,12},{20,16},{24,20},{28,24},{1,29},{... | collective-permute-start | bytes 3145736 | tf_op jit(solution)/shard_map/ppermute | solution.py:9
  15.6 4.1 %copy-start.3 = (s32[8]{0:T(128)S(1)}, s32[8]{0:T(128)}, u32[]{:S(2)}) copy-start(s32[8]{0:T(128)} %param.15) | copy-start | bytes 100
  15.6 4.2 %copy-start = (bf16[1,256,128]{2,1,0:T(8,128)(2,1)S(1)}, bf16[1,256,128]{2,1,0:T(8,128)(2,1)}, u32[]{:S(2)}) copy-start(bf16[1,256,128]{2,1,0:T(8,128)(2,1)} %param.10) | copy-start | bytes 196612
  15.6 10.4 %copy-start.1 = (bf16[1,256,128]{2,1,0:T(8,128)(2,1)S(1)}, bf16[1,256,128]{2,1,0:T(8,128)(2,1)}, u32[]{:S(2)}) copy-start(bf16[1,256,128]{2,1,0:T(8,128)(2,1)} %param.11) | copy-start | bytes 196612
  19.7 21.3 %copy-start.2 = (f32[1,16,256]{2,1,0:T(8,128)S(1)}, f32[1,16,256]{2,1,0:T(8,128)}, u32[]{:S(2)}) copy-start(f32[1,16,256]{2,1,0:T(8,128)} %param.14) | copy-start | bytes 49156
Sparse Core Ops, SparseCore 0:
  81.7 23.5 reduce-scatter.1
where the time goes:
time: 115 us; the launch traced here: 114 us
  matrix products  36.2 us (31%)
  waiting for transfers between devices  27.9 us (24%)
  local copies, waits for them, and re-layouts  14.1 us (12%)
  between operations  14 us (12%)
  blocking collectives  12.5 us (11%)
  starting transfers between devices  6.01 us (5%)
  other arithmetic  2.61 us (2%)
    reduce_scatter x1, waiting for transfers between devices, body(): lax.psum_scatter(key_value_full.astype(jnp.bfloat16), 'ctx', scatter_dime...  21.8 us
    dot_general x4, matrix products, tile_grads(): jnp.einsum('rhd,cd->hrc', grad_rows, value_rows, preferred_element_type=j...  10.7 us
    dot_general x4, matrix products, tile_grads(): jnp.einsum('hrc,rhd->cd', probs_low, grad_rows, preferred_element_type=jn...  8.79 us
    dot_general x4, matrix products, tile_grads(): jnp.einsum('hrc,cd->rhd', grad_scores, key_rows, preferred_element_type=j...  7.4 us
    unnamed x11, local copies, waits for them, and re-layouts  6.5 us
    all_gather x1, blocking collectives, body(): lax.all_gather(value_block, 'ctx', axis=0, tiled=True)  6.3 us
    all_gather x1, blocking collectives, body(): lax.all_gather(key_block, 'ctx', axis=0, tiled=True)  6.22 us
    dot_general x4, matrix products, tile_grads(): jnp.einsum('rhd,cd->hrc', query_rows, key_rows, preferred_element_type=jn...  6.14 us
  transfers between devices with their start and end apart: 2, of which 2 were waited for; matrix products, arithmetic and copies ran while one was open for 5% of the time, Pallas kernels for 0%

commit v1 on v0

v1 whole, which is shorter than its diff:
```python
import functools
import math

import jax
import jax.numpy as jnp
from jax import lax
from jax.experimental import pallas as pl
from jax.experimental.pallas import tpu as pltpu
from jax.sharding import PartitionSpec as P

KEY_BLOCK = 256
ROW_TILE = 1024
VMEM_LIMIT = 48 * 1024 * 1024

WHOLE = pl.BlockSpec(memory_space=pltpu.VMEM)
SCALARS = pl.BlockSpec(memory_space=pltpu.SMEM)


def from_behind(shard, axis, by):
    length = lax.axis_size(axis)
    return lax.ppermute(shard, axis, [(i, (i + by) % length) for i in range(length)])


def params():
    return pltpu.CompilerParams(vmem_limit_bytes=VMEM_LIMIT)


def sort_keys_kernel(count, span_rows, head_size, starts_ref, *refs):
    blocks = refs[:count]
    keys_ref, values_ref, keys_t_ref = refs[count:]
    me = lax.axis_index("ctx")
    values_ref[:, head_size:] = jnp.full(
        (values_ref.shape[0], values_ref.shape[1] - head_size), -1.0, values_ref.dtype
    )
    for step in range(count):
        owner = lax.rem(me - step + count, count)
        for half in range(2):
            start = pl.multiple_of(starts_ref[2 * owner + half], span_rows)
            rows = pl.ds(start, span_rows)
            part = blocks[step][half * span_rows : (half + 1) * span_rows, :]
            keys_ref[rows, :] = part[:, :head_size]
            values_ref[rows, :head_size] = part[:, head_size:]
            keys_t_ref[:, rows] = part[:, :head_size].astype(jnp.float32).T.astype(jnp.bfloat16)


def sort_keys(span_start, blocks, span_rows, head_size):
    count = len(blocks)
    total = count * 2 * span_rows
    return pl.pallas_call(
        functools.partial(sort_keys_kernel, count, span_rows, head_size),
        out_shape=(
            jax.ShapeDtypeStruct((total, head_size), jnp.bfloat16),
            jax.ShapeDtypeStruct((total, 2 * head_size), jnp.bfloat16),
            jax.ShapeDtypeStruct((head_size, total), jnp.bfloat16),
        ),
        in_specs=[SCALARS] + [WHOLE] * count,
        out_specs=(WHOLE,) * 3,
        compiler_params=params(),
    )(span_start, *blocks)


def span_grads(
    half, heads, span_rows, head_size, starts_ref, q_ref, g_ref, o_ref, lse_ref, keys_ref, values_ref,
    keys_t_ref, dq_ref, total_ref, dq_acc,
):
    scale = head_size**-0.5
    to_log2 = math.log2(math.e)
    me = lax.axis_index("ctx")
    start = starts_ref[2 * me + half]
    rows_all = span_rows * heads
    row_tile = min(ROW_TILE, rows_all)
    full_blocks = start // KEY_BLOCK

    for tile in range(rows_all // row_tile):
        rows = slice(tile * row_tile, (tile + 1) * row_tile)
        q = q_ref[rows, :]
        g = g_ref[rows, :]
        products = (g.astype(jnp.float32) * o_ref[rows, :].astype(jnp.float32)).astype(jnp.bfloat16)
        g_wide = jnp.concatenate([g, products], axis=1)
        lse2 = lse_ref[0:1, rows] * to_log2
        dq_acc[...] = jnp.zeros_like(dq_acc)
        query_pos = (
            start
            + tile * (row_tile // heads)
            + lax.broadcasted_iota(jnp.int32, (KEY_BLOCK, row_tile), 1) // heads
        )

        def block(index, masked):
            base = pl.multiple_of(index * KEY_BLOCK, KEY_BLOCK)
            at = pl.ds(base, KEY_BLOCK)
            nt = (((1,), (1,)), ((), ()))
            scores = lax.dot_general(keys_ref[at, :], q, nt, preferred_element_type=jnp.float32)
            probs = jnp.exp2(scores * (scale * to_log2) - lse2)
            if masked:
                key_pos = base + lax.broadcasted_iota(jnp.int32, (KEY_BLOCK, row_tile), 0)
                probs = jnp.where(key_pos <= query_pos, probs, 0.0)
            centred = lax.dot_general(
                values_ref[at, :], g_wide, nt, preferred_element_type=jnp.float32
            )
            grad_scores = (probs * centred).astype(jnp.bfloat16)
            probs_low = probs.astype(jnp.bfloat16)
            total_ref[at, :head_size] += jnp.dot(
                grad_scores, q, preferred_element_type=jnp.float32
            )
            total_ref[at, head_size:] += jnp.dot(probs_low, g, preferred_element_type=jnp.float32)
            dq_acc[...] += jnp.dot(
                keys_t_ref[:, at], grad_scores, preferred_element_type=jnp.float32
            )

        def dense(index, carry):
            block(index, False)
            return carry

        lax.fori_loop(0, full_blocks, dense, 0)
        block(full_blocks, True)
        dq_ref[rows, :] = (dq_acc[...] * scale).T.astype(jnp.bfloat16)


def hand_out(half, count, span_rows, head_size, starts_ref, total_ref, own_ref, send_refs):
    scale = head_size**-0.5
    me = lax.axis_index("ctx")
    for step in range(count):
        owner = lax.rem(me + step, count)
        start = pl.multiple_of(starts_ref[2 * owner + half], span_rows)
        rows = pl.ds(start, span_rows)
        target = own_ref if step == 0 else send_refs[step - 1]
        target[:, :head_size] = (total_ref[rows, :head_size] * scale).astype(target.dtype)
        target[:, head_size:] = total_ref[rows, head_size:].astype(target.dtype)


def upper_kernel(
    count, heads, span_rows, head_size, starts_ref, q_ref, g_ref, o_ref, lse_ref, keys_ref, values_ref,
    keys_t_ref, dq_ref, lower_ref, own_ref, *rest,
):
    send_refs, (total_ref, dq_acc) = rest[: count - 1], rest[count - 1 :]
    total_ref[...] = jnp.zeros_like(total_ref)
    span_grads(
        1, heads, span_rows, head_size, starts_ref, q_ref, g_ref, o_ref, lse_ref, keys_ref, values_ref,
        keys_t_ref, dq_ref, total_ref, dq_acc,
    )
    lower_ref[...] = total_ref[: lower_ref.shape[0], :]
    hand_out(1, count, span_rows, head_size, starts_ref, total_ref, own_ref, send_refs)


def lower_kernel(
    count, heads, span_rows, head_size, starts_ref, q_ref, g_ref, o_ref, lse_ref, keys_ref, values_ref,
    keys_t_ref, lower_ref, dq_in_ref, dq_ref, own_ref, *rest,
):
    send_refs, (total_ref, dq_acc) = rest[: count - 1], rest[count - 1 :]
    total_ref[...] = lower_ref[...]
    span_grads(
        0, heads, span_rows, head_size, starts_ref, q_ref, g_ref, o_ref, lse_ref, keys_ref, values_ref,
        keys_t_ref, dq_ref, total_ref, dq_acc,
    )
    hand_out(0, count, span_rows, head_size, starts_ref, total_ref, own_ref, send_refs)


def add_kernel(count, span_rows, head_size, *refs):
    key_ref, value_ref = refs[2 * count :]
    for half in range(2):
        own_ref, *term_refs = refs[half * count : (half + 1) * count]
        total = own_ref[...]
        for term_ref in term_refs:
            total = total + term_ref[...].astype(jnp.float32)
        rows = slice(half * span_rows, (half + 1) * span_rows)
        key_ref[rows, :] = total[:, :head_size].astype(jnp.bfloat16)
        value_ref[rows, :] = total[:, head_size:].astype(jnp.bfloat16)


def body(queries, keys, values, outputs, grad_held, lse, span_start):
    count = lax.axis_size("ctx")
    row_count, heads, head_size = queries.shape[1:]
    span_rows = row_count // 2
    total = count * row_count
    rows_span = span_rows * heads

    upper_grad = from_behind(grad_held[0, span_rows:], "section", -1)
    lower_grad = from_behind(grad_held[0, :span_rows], "section", -1)

    pair = jnp.concatenate([keys[0], values[0]], axis=1)
    blocks = [pair] + [from_behind(pair, "ctx", step) for step in range(1, count)]
    sorted_keys = sort_keys(span_start, blocks, span_rows, head_size)

    q_flat = queries.reshape(row_count * heads, head_size)
    o_flat = outputs.reshape(row_count * heads, head_size)
    lse_flat = lse[0].T.reshape(1, row_count * heads)
    row_spec = lambda half: pl.BlockSpec((rows_span, head_size), lambda i: (half, 0))
    lse_spec = lambda half: pl.BlockSpec((1, rows_span), lambda i: (0, half))
    fixed = lambda shape: pl.BlockSpec(shape, lambda i: (0,) * len(shape))
    sorted_specs = [
        fixed((total, head_size)), fixed((total, 2 * head_size)), fixed((head_size, total))
    ]
    span_wide = (span_rows, 2 * head_size)
    dq_shape = jax.ShapeDtypeStruct((row_count * heads, head_size), jnp.bfloat16)
    own_shape = jax.ShapeDtypeStruct(span_wide, jnp.float32)
    send_shape = jax.ShapeDtypeStruct(span_wide, jnp.bfloat16)
    row_tile = min(ROW_TILE, rows_span)

    def cost(blocks_seen):
        pairs = rows_span * blocks_seen * KEY_BLOCK
        return pl.CostEstimate(
            flops=10 * pairs * head_size, bytes_accessed=4 * 2**20, transcendentals=pairs
        )

    dq, lower_total, own_upper, *send_upper = pl.pallas_call(
        functools.partial(upper_kernel, count, heads, span_rows, head_size),
        grid=(1,),
        out_shape=(
            dq_shape,
            jax.ShapeDtypeStruct((total // 2, 2 * head_size), jnp.float32),
            own_shape,
            *[send_shape] * (count - 1),
        ),
        in_specs=[SCALARS, row_spec(1), fixed((rows_span, head_size)), row_spec(1), lse_spec(1)]
        + sorted_specs,
        out_specs=(
            row_spec(1), fixed((total // 2, 2 * head_size)), *[fixed(span_wide)] * count
        ),
        scratch_shapes=[
            pltpu.VMEM((total, 2 * head_size), jnp.float32),
            pltpu.VMEM((head_size, row_tile), jnp.float32),
        ],
        compiler_params=params(),
        cost_estimate=cost(3 * total // (4 * KEY_BLOCK)),
    )(
        span_start, q_flat, upper_grad.reshape(rows_span, head_size), o_flat, lse_flat, *sorted_keys
    )
    got_upper = [from_behind(send_upper[step - 1], "ctx", step) for step in range(1, count)]

    dq, own_lower, *send_lower = pl.pallas_call(
        functools.partial(lower_kernel, count, heads, span_rows, head_size),
        grid=(1,),
        out_shape=(dq_shape, own_shape, *[send_shape] * (count - 1)),
        in_specs=[SCALARS, row_spec(0), fixed((rows_span, head_size)), row_spec(0), lse_spec(0)]
        + sorted_specs
        + [fixed((total // 2, 2 * head_size)), pl.BlockSpec(memory_space=pl.ANY)],
        out_specs=(row_spec(0), *[fixed(span_wide)] * count),
        scratch_shapes=[
            pltpu.VMEM((total // 2, 2 * head_size), jnp.float32),
            pltpu.VMEM((head_size, row_tile), jnp.float32),
        ],
        input_output_aliases={9: 0},
        compiler_params=params(),
        cost_estimate=cost(total // (4 * KEY_BLOCK)),
    )(
        span_start, q_flat, lower_grad.reshape(rows_span, head_size), o_flat, lse_flat, *sorted_keys,
        lower_total, dq,
    )
    got_lower = [from_behind(send_lower[step - 1], "ctx", step) for step in range(1, count)]

    key_out, value_out = pl.pallas_call(
        functools.partial(add_kernel, count, span_rows, head_size),
        out_shape=(jax.ShapeDtypeStruct((row_count, head_size), jnp.bfloat16),) * 2,
        in_specs=[WHOLE] * (2 * count),
        out_specs=(WHOLE,) * 2,
        compiler_params=params(),
    )(own_lower, *got_lower, own_upper, *got_upper)
    return (dq.reshape(queries.shape), key_out[None], value_out[None])


def solution(mesh):
    placed = (
        P("section", "ctx", None, None),
        P("section", "ctx", None),
        P("section", "ctx", None),
        P("section", "ctx", None, None),
        P("section", "ctx", None, None),
        P("section", None, "ctx"),
        P(),
    )
    return jax.shard_map(
        body,
        mesh=mesh,
        in_specs=placed,
        out_specs=(
            P("section", "ctx", None, None),
            P("section", "ctx", None),
            P("section", "ctx", None),
        ),
        check_vma=False,
    )
```

time: 115 us -> 45.3 us (0.39); the launches traced: 114 us -> 45.6 us
  matrix products: 36.2 us -> 0 us
  Pallas kernels: 0 us -> 13.9 us
  between operations: 14 us -> 0.71 us
  waiting for transfers between devices: 27.9 us -> 15.3 us
  blocking collectives: 12.5 us -> 0 us
  local copies, waits for them, and re-layouts: 14.1 us -> 2.69 us
  starting transfers between devices: 6.01 us -> 13 us
  other arithmetic: 2.61 us -> 0.02 us
    dot_general x20 -> x0, matrix products: 36.2 us -> none  [the longest x4 10.7 us: tile_grads(): jnp.einsum('rhd,cd->hrc', grad_rows, value_rows, preferred_element_type=j...]
    reduce_scatter x1 -> x0, waiting for transfers between devices: 21.8 us -> none  [body(): lax.psum_scatter(key_value_full.astype(jnp.bfloat16), 'ctx', scatter_dime...]
    pallas_call x0 -> x4, Pallas kernels: none -> 13.9 us  [the longest x1 7.29 us: body(): pl.pallas_call(functools.partial(upper_kernel, count, heads, span_rows, h...]
    all_gather x2 -> x0, blocking collectives: 12.5 us -> none  [the longest x1 6.3 us: body(): lax.all_gather(value_block, 'ctx', axis=0, tiled=True)]
    ppermute x1 -> x11, waiting for transfers between devices: 6.04 us -> 15.3 us  [from_behind(): lax.ppermute(shard, axis, [(i, (i + by) % length) for i in range(length)])]
    ppermute x1 -> x11, starting transfers between devices: 5.98 us -> 13 us  [from_behind(): lax.ppermute(shard, axis, [(i, (i + by) % length) for i in range(length)])]
    unnamed x11 -> x12, local copies, waits for them, and re-layouts: 6.5 us -> 0.02 us
    dynamic_update_slice x8 -> x0, local copies, waits for them, and re-layouts: 3.03 us -> none  [sweep_turn(): lax.dynamic_update_slice_in_dim(key_total, jnp.concatenate([key_grad, val...]
  transfers between devices with their start and end apart: 2 -> 11, of which waited for: 2 -> 7; matrix products, arithmetic and copies ran while one was open for 5% -> 0% of each run, Pallas kernels for 0% -> 18%
where the time goes in v1:
time: 45.3 us; the launch traced here: 45.6 us
  waiting for transfers between devices  15.3 us (34%)
  Pallas kernels  13.9 us (31%)
  starting transfers between devices  13 us (29%)
  local copies, waits for them, and re-layouts  2.69 us (6%)
  between operations  0.71 us (2%)
    ppermute x11, waiting for transfers between devices, from_behind(): lax.ppermute(shard, axis, [(i, (i + by) % length) for i in range(length)])  15.3 us
    ppermute x11, starting transfers between devices, from_behind(): lax.ppermute(shard, axis, [(i, (i + by) % length) for i in range(length)])  13 us
    pallas_call x1, Pallas kernels, body(): pl.pallas_call(functools.partial(upper_kernel, count, heads, span_rows, h...  7.29 us
    pallas_call x1, Pallas kernels, body(): pl.pallas_call(functools.partial(lower_kernel, count, heads, span_rows, h...  5.12 us
    squeeze x1, local copies, waits for them, and re-layouts, body(): upper_grad = from_behind(grad_held[0, span_rows:], 'section', -1)  2.45 us
  transfers between devices with their start and end apart: 11, of which 7 were waited for; matrix products, arithmetic and copies ran while one was open for 0% of the time, Pallas kernels for 18%

profile of v1, /device:TPU:0, one launch (start us, length us, event | category | flops | bytes accessed | tf_op | source)
XLA Modules:
  0.0 45.6 jit_solution(14926492439483839359)
XLA Ops:
  0.6 0.0 copy-start.3
  0.6 0.0 copy-start.4
  0.7 0.0 copy-start.5
  0.7 2.4 %slice_bitcast_fusion = (bf16[128,16,128]{2,1,0:T(8,128)(2,1)}, bf16[128,16,128]{2,1,0:T(8,128)(2,1)}) fusion(bf16[1,256,16,128]{3,2,1,0:T(8,128)(2,1)} %param.11), kind=kLoop, calls=%fused_computation | loop fusion | bytes 2097152 | tf_op jit(solution)/shard_map/squeeze | solution.py:177
  3.1 6.0 %collective-permute-start.4 = (bf16[128,16,128]{2,1,0:T(8,128)(2,1)}, bf16[128,16,128]{2,1,0:T(8,128)(2,1)}, u32[]{:S(2)}, u32[]{:S(2)}) collective-permute-start(bf16[128,16,128]{2,1,0:T(8,128)(2,1)} %get-tuple-element.35), channel_id=1, source_target_pairs={{0,28},{4,0},{8,4},{12,8},{16,12},{20,16},{24,20},{28,24},{1,29},{... | collective-permute-start | bytes 1572872 | tf_op jit(solution)/shard_map/ppermute | solution.py:21
  9.1 0.5 %collective-permute-start = (bf16[128,16,128]{2,1,0:T(8,128)(2,1)}, bf16[128,16,128]{2,1,0:T(8,128)(2,1)S(1)}, u32[]{:S(2)}, u32[]{:S(2)}) collective-permute-start(bf16[128,16,128]{2,1,0:T(8,128)(2,1)} %get-tuple-element.36), channel_id=1, source_target_pairs={{0,28},{4,0},{8,4},{12,8},{16,12},{20,16},{24,20},{28,24},{1,29},{... | collective-permute-start | bytes 1572872 | tf_op jit(solution)/shard_map/ppermute | solution.py:21
  9.7 0.5 collective-permute-start.3
  10.1 1.2 %collective-permute-start.2 = (bf16[256,256]{1,0:T(8,128)(2,1)S(1)}, bf16[256,256]{1,0:T(8,128)(2,1)S(1)}, u32[]{:S(2)}, u32[]{:S(2)}) collective-permute-start(bf16[256,256]{1,0:T(8,128)(2,1)S(1)} %pad_maximum_fusion.refs_0_), channel_id=1, source_target_pairs={{0,2},{1,3},{2,0},{3,1},{4,6},{5,7},{6,4},{7,5},{8,10},{9,11},{10,... | collective-permute-start | bytes 393224 | tf_op jit(solution)/shard_map/ppermute | solution.py:21
  11.3 0.2 collective-permute-start.1
  11.5 0.1 copy.12
  11.6 0.1 reshape.27.lse_ref
  11.7 1.7 %collective-permute-done.3.refs_3_ = bf16[256,256]{1,0:T(8,128)(2,1)S(1)} collective-permute-done((bf16[256,256]{1,0:T(8,128)(2,1)S(1)}, bf16[256,256]{1,0:T(8,128)(2,1)S(1)}, u32[]{:S(2)}, u32[]{:S(2)}) %collective-permute-start.3) | collective-permute-done | bytes 131104 | tf_op jit(solution)/shard_map/ppermute | solution.py:21
  13.4 5.0 %collective-permute-done.2.refs_2_ = bf16[256,256]{1,0:T(8,128)(2,1)S(1)} collective-permute-done((bf16[256,256]{1,0:T(8,128)(2,1)S(1)}, bf16[256,256]{1,0:T(8,128)(2,1)S(1)}, u32[]{:S(2)}, u32[]{:S(2)}) %collective-permute-start.2) | collective-permute-done | bytes 131104 | tf_op jit(solution)/shard_map/ppermute | solution.py:21
  18.4 0.0 collective-permute-done.1.refs_1_
  18.4 0.8 %shard_map.94 = (bf16[1024,128]{1,0:T(8,128)(2,1)S(1)}, bf16[1024,256]{1,0:T(8,128)(2,1)S(1)}, bf16[128,1024]{1,0:T(8,128)(2,1)S(1)}) custom-call(s32[8]{0:T(128)S(1)} %copy-done.2, bf16[256,256]{1,0:T(8,128)(2,1)S(1)} %pad_maximum_fusion.refs_0_, bf16[256,256]{1,0:T(8,128)(2,1)S(1)} %collective-permute-done.1.refs_1_, ...), custom_call_target="tpu_custom_call" | custom-call | tf_op jit(solution)/shard_map/pallas_call | solution.py:49
  19.2 2.6 %collective-permute-done.4 = bf16[128,16,128]{2,1,0:T(8,128)(2,1)} collective-permute-done((bf16[128,16,128]{2,1,0:T(8,128)(2,1)}, bf16[128,16,128]{2,1,0:T(8,128)(2,1)}, u32[]{:S(2)}, u32[]{:S(2)}) %collective-permute-start.4) | collective-permute-done | bytes 524320 | tf_op jit(solution)/shard_map/ppermute | solution.py:21
  21.8 7.3 %shard_map.95 = (bf16[4096,128]{1,0:T(8,128)(2,1)}, f32[512,256]{1,0:T(8,128)S(1)}, f32[128,256]{1,0:T(8,128)S(1)}, bf16[128,256]{1,0:T(8,128)(2,1)S(1)}, bf16[1...) custom-call(s32[8]{0:T(128)S(1)} %copy-done.2, bf16[4096,128]{1,0:T(8,128)(2,1)S(1)} %bitcast.16, ...), custom_call_target="tpu_custom_call" | custom-call | flops 2013265920 | bytes 4194304 | tf_op jit(solution)/shard_map/pallas_call | solution.py:205
  29.1 2.8 %collective-permute-done = bf16[128,16,128]{2,1,0:T(8,128)(2,1)S(1)} collective-permute-done((bf16[128,16,128]{2,1,0:T(8,128)(2,1)}, bf16[128,16,128]{2,1,0:T(8,128)(2,1)S(1)}, u32[]{:S(2)}, u32[]{:S(2)}) %collective-permute-start) | collective-permute-done | bytes 524320 | tf_op jit(solution)/shard_map/ppermute | solution.py:21
  31.8 5.1 %shard_map.96 = (bf16[4096,128]{1,0:T(8,128)(2,1)}, f32[128,256]{1,0:T(8,128)S(1)}, bf16[128,256]{1,0:T(8,128)(2,1)S(1)}, bf16[128,256]{1,0:T(8,128)(2,1)S(1)}, bf16[128,256]{1,0:T(8,128)(2,1)S(1)}) custom-call(s32[8]{0:T(128)S(1)} %copy-done.2, bf16[4096,128]{1,0:T(8,128)(2,1)S(1)} %bitcast.17, ...), custom_call_target="tpu_custom_call", output_to_operand_aliasing={{0}: (9, {})} | custom-call | flops 671088640 | bytes 4194304 | tf_op jit(solution)/shard_map/pallas_call | solution.py:230
  37.0 0.0 collective-permute-start.5
  37.0 0.5 %collective-permute-start.6 = (bf16[128,256]{1,0:T(8,128)(2,1)S(1)}, bf16[128,256]{1,0:T(8,128)(2,1)S(1)}, u32[]{:S(2)}, u32[]{:S(2)}) collective-permute-start(bf16[128,256]{1,0:T(8,128)(2,1)S(1)} %get-tuple-element.27), channel_id=1, source_target_pairs={{0,2},{1,3},{2,0},{3,1},{4,6},{5,7},{6,4},{7,5},{8,10},{9,11},{10,... | collective-permute-start | bytes 196616 | tf_op jit(solution)/shard_map/ppermute | solution.py:21
  37.5 1.3 %collective-permute-start.7 = (bf16[128,256]{1,0:T(8,128)(2,1)S(1)}, bf16[128,256]{1,0:T(8,128)(2,1)S(1)}, u32[]{:S(2)}, u32[]{:S(2)}) collective-permute-start(bf16[128,256]{1,0:T(8,128)(2,1)S(1)} %get-tuple-element.28), channel_id=1, source_target_pairs={{0,3},{1,0},{2,1},{3,2},{4,7},{5,4},{6,5},{7,6},{8,11},{9,8},{10,9... | collective-permute-start | bytes 196616 | tf_op jit(solution)/shard_map/ppermute | solution.py:21
  38.7 0.1 collective-permute-start.8
  38.8 1.7 %collective-permute-start.9 = (bf16[128,256]{1,0:T(8,128)(2,1)S(1)}, bf16[128,256]{1,0:T(8,128)(2,1)S(1)}, u32[]{:S(2)}, u32[]{:S(2)}) collective-permute-start(bf16[128,256]{1,0:T(8,128)(2,1)S(1)} %get-tuple-element.31), channel_id=1, source_target_pairs={{0,2},{1,3},{2,0},{3,1},{4,6},{5,7},{6,4},{7,5},{8,10},{9,11},{10,... | collective-permute-start | bytes 196616 | tf_op jit(solution)/shard_map/ppermute | solution.py:21
  40.5 0.3 collective-permute-done.5.refs_1_
  40.8 1.1 %collective-permute-start.10 = (bf16[128,256]{1,0:T(8,128)(2,1)S(1)}, bf16[128,256]{1,0:T(8,128)(2,1)S(1)}, u32[]{:S(2)}, u32[]{:S(2)}) collective-permute-start(bf16[128,256]{1,0:T(8,128)(2,1)S(1)} %get-tuple-element.32), channel_id=1, source_target_pairs={{0,3},{1,0},{2,1},{3,2},{4,7},{5,4},{6,5},{7,6},{8,11},{9,8},{10,9... | collective-permute-start | bytes 196616 | tf_op jit(solution)/shard_map/ppermute | solution.py:21
  41.9 0.0 collective-permute-done.6.refs_2_
  41.9 0.0 collective-permute-done.7.refs_3_
  41.9 1.5 %collective-permute-done.8.refs_5_ = bf16[128,256]{1,0:T(8,128)(2,1)S(1)} collective-permute-done((bf16[128,256]{1,0:T(8,128)(2,1)S(1)}, bf16[128,256]{1,0:T(8,128)(2,1)S(1)}, u32[]{:S(2)}, u32[]{:S(2)}) %collective-permute-start.8) | collective-permute-done | bytes 65568 | tf_op jit(solution)/shard_map/ppermute | solution.py:21
  43.5 1.4 %collective-permute-done.9.refs_6_ = bf16[128,256]{1,0:T(8,128)(2,1)S(1)} collective-permute-done((bf16[128,256]{1,0:T(8,128)(2,1)S(1)}, bf16[128,256]{1,0:T(8,128)(2,1)S(1)}, u32[]{:S(2)}, u32[]{:S(2)}) %collective-permute-start.9) | collective-permute-done | bytes 65568 | tf_op jit(solution)/shard_map/ppermute | solution.py:21
  44.9 0.0 collective-permute-done.10.refs_7_
  44.9 0.7 %shard_map.97 = (bf16[256,128]{1,0:T(8,128)(2,1)}, bf16[256,128]{1,0:T(8,128)(2,1)}) custom-call(f32[128,256]{1,0:T(8,128)S(1)} %get-tuple-element.25.refs_0_, bf16[128,256]{1,0:T(8,128)(2,1)S(1)} %collective-permute-done.5.refs_1_, bf16[128,256]{1,0:T(8,128)(2,1)S(1)} %collective-permute-done.6.refs_2_, ...), custom_call_target="tpu_custom_call" | custom-call | tf_op jit(solution)/shard_map/pallas_call | solution.py:251
  (10 shorter events, 0.0 us)
Async XLA Ops:
  0.6 9.0 %copy-start.3 = (bf16[1,256,128]{2,1,0:T(8,128)(2,1)S(1)}, bf16[1,256,128]{2,1,0:T(8,128)(2,1)}, u32[]{:S(2)}) copy-start(bf16[1,256,128]{2,1,0:T(8,128)(2,1)} %param.9) | copy-start | bytes 196612
  0.6 9.0 %copy-start.4 = (bf16[1,256,128]{2,1,0:T(8,128)(2,1)S(1)}, bf16[1,256,128]{2,1,0:T(8,128)(2,1)}, u32[]{:S(2)}) copy-start(bf16[1,256,128]{2,1,0:T(8,128)(2,1)} %param.8) | copy-start | bytes 196612
  0.7 10.8 %copy-start.5 = (f32[1,16,256]{2,1,0:T(8,128)S(1)}, f32[1,16,256]{2,1,0:T(8,128)}, u32[]{:S(2)}) copy-start(f32[1,16,256]{2,1,0:T(8,128)} %param.12) | copy-start | bytes 49156
  0.7 17.7 %copy-start.2 = (s32[8]{0:T(128)S(1)}, s32[8]{0:T(128)}, u32[]{:S(2)}) copy-start(s32[8]{0:T(128)} %starts_ref.5) | copy-start | bytes 100
  0.7 21.1 %copy-start.1 = (bf16[1,256,16,128]{3,2,1,0:T(8,128)(2,1)S(1)}, bf16[1,256,16,128]{3,2,1,0:T(8,128)(2,1)}, u32[]{:S(2)}) copy-start(bf16[1,256,16,128]{3,2,1,0:T(8,128)(2,1)} %param.10) | copy-start | bytes 3145732
  3.1 18.6 %copy-start = (bf16[1,256,16,128]{3,2,1,0:T(8,128)(2,1)S(1)}, bf16[1,256,16,128]{3,2,1,0:T(8,128)(2,1)}, u32[]{:S(2)}) copy-start(bf16[1,256,16,128]{3,2,1,0:T(8,128)(2,1)} %param.7) | copy-start | bytes 3145732
  3.1 18.6 %collective-permute-start.4 = (bf16[128,16,128]{2,1,0:T(8,128)(2,1)}, bf16[128,16,128]{2,1,0:T(8,128)(2,1)}, u32[]{:S(2)}, u32[]{:S(2)}) collective-permute-start(bf16[128,16,128]{2,1,0:T(8,128)(2,1)} %get-tuple-element.35), channel_id=1, source_target_pairs={{0,28},{4,0},{8,4},{12,8},{16,12},{20,16},{24,20},{28,24},{1,29},{... | collective-permute-start | bytes 1572872 | tf_op jit(solution)/shard_map/ppermute | solution.py:21
  9.1 22.7 %collective-permute-start = (bf16[128,16,128]{2,1,0:T(8,128)(2,1)}, bf16[128,16,128]{2,1,0:T(8,128)(2,1)S(1)}, u32[]{:S(2)}, u32[]{:S(2)}) collective-permute-start(bf16[128,16,128]{2,1,0:T(8,128)(2,1)} %get-tuple-element.36), channel_id=1, source_target_pairs={{0,28},{4,0},{8,4},{12,8},{16,12},{20,16},{24,20},{28,24},{1,29},{... | collective-permute-start | bytes 1572872 | tf_op jit(solution)/shard_map/ppermute | solution.py:21
  9.7 3.7 %collective-permute-start.3 = (bf16[256,256]{1,0:T(8,128)(2,1)S(1)}, bf16[256,256]{1,0:T(8,128)(2,1)S(1)}, u32[]{:S(2)}, u32[]{:S(2)}) collective-permute-start(bf16[256,256]{1,0:T(8,128)(2,1)S(1)} %pad_maximum_fusion.refs_0_), channel_id=1, source_target_pairs={{0,3},{1,0},{2,1},{3,2},{4,7},{5,4},{6,5},{7,6},{8,11},{9,8},{10,9... | collective-permute-start | bytes 393224 | tf_op jit(solution)/shard_map/ppermute | solution.py:21
  10.1 8.2 %collective-permute-start.2 = (bf16[256,256]{1,0:T(8,128)(2,1)S(1)}, bf16[256,256]{1,0:T(8,128)(2,1)S(1)}, u32[]{:S(2)}, u32[]{:S(2)}) collective-permute-start(bf16[256,256]{1,0:T(8,128)(2,1)S(1)} %pad_maximum_fusion.refs_0_), channel_id=1, source_target_pairs={{0,2},{1,3},{2,0},{3,1},{4,6},{5,7},{6,4},{7,5},{8,10},{9,11},{10,... | collective-permute-start | bytes 393224 | tf_op jit(solution)/shard_map/ppermute | solution.py:21
  11.3 7.1 %collective-permute-start.1 = (bf16[256,256]{1,0:T(8,128)(2,1)S(1)}, bf16[256,256]{1,0:T(8,128)(2,1)S(1)}, u32[]{:S(2)}, u32[]{:S(2)}) collective-permute-start(bf16[256,256]{1,0:T(8,128)(2,1)S(1)} %pad_maximum_fusion.refs_0_), channel_id=1, source_target_pairs={{0,1},{1,2},{2,3},{3,0},{4,5},{5,6},{6,7},{7,4},{8,9},{9,10},{10,1... | collective-permute-start | bytes 393224 | tf_op jit(solution)/shard_map/ppermute | solution.py:21
  37.0 3.8 %collective-permute-start.5 = (bf16[128,256]{1,0:T(8,128)(2,1)S(1)}, bf16[128,256]{1,0:T(8,128)(2,1)S(1)}, u32[]{:S(2)}, u32[]{:S(2)}) collective-permute-start(bf16[128,256]{1,0:T(8,128)(2,1)S(1)} %get-tuple-element.26), channel_id=1, source_target_pairs={{0,1},{1,2},{2,3},{3,0},{4,5},{5,6},{6,7},{7,4},{8,9},{9,10},{10,1... | collective-permute-start | bytes 196616 | tf_op jit(solution)/shard_map/ppermute | solution.py:21
  37.0 5.0 %collective-permute-start.6 = (bf16[128,256]{1,0:T(8,128)(2,1)S(1)}, bf16[128,256]{1,0:T(8,128)(2,1)S(1)}, u32[]{:S(2)}, u32[]{:S(2)}) collective-permute-start(bf16[128,256]{1,0:T(8,128)(2,1)S(1)} %get-tuple-element.27), channel_id=1, source_target_pairs={{0,2},{1,3},{2,0},{3,1},{4,6},{5,7},{6,4},{7,5},{8,10},{9,11},{10,... | collective-permute-start | bytes 196616 | tf_op jit(solution)/shard_map/ppermute | solution.py:21
  37.5 4.5 %collective-permute-start.7 = (bf16[128,256]{1,0:T(8,128)(2,1)S(1)}, bf16[128,256]{1,0:T(8,128)(2,1)S(1)}, u32[]{:S(2)}, u32[]{:S(2)}) collective-permute-start(bf16[128,256]{1,0:T(8,128)(2,1)S(1)} %get-tuple-element.28), channel_id=1, source_target_pairs={{0,3},{1,0},{2,1},{3,2},{4,7},{5,4},{6,5},{7,6},{8,11},{9,8},{10,9... | collective-permute-start | bytes 196616 | tf_op jit(solution)/shard_map/ppermute | solution.py:21
  38.7 4.7 %collective-permute-start.8 = (bf16[128,256]{1,0:T(8,128)(2,1)S(1)}, bf16[128,256]{1,0:T(8,128)(2,1)S(1)}, u32[]{:S(2)}, u32[]{:S(2)}) collective-permute-start(bf16[128,256]{1,0:T(8,128)(2,1)S(1)} %get-tuple-element.30), channel_id=1, source_target_pairs={{0,1},{1,2},{2,3},{3,0},{4,5},{5,6},{6,7},{7,4},{8,9},{9,10},{10,1... | collective-permute-start | bytes 196616 | tf_op jit(solution)/shard_map/ppermute | solution.py:21
  38.8 6.0 %collective-permute-start.9 = (bf16[128,256]{1,0:T(8,128)(2,1)S(1)}, bf16[128,256]{1,0:T(8,128)(2,1)S(1)}, u32[]{:S(2)}, u32[]{:S(2)}) collective-permute-start(bf16[128,256]{1,0:T(8,128)(2,1)S(1)} %get-tuple-element.31), channel_id=1, source_target_pairs={{0,2},{1,3},{2,0},{3,1},{4,6},{5,7},{6,4},{7,5},{8,10},{9,11},{10,... | collective-permute-start | bytes 196616 | tf_op jit(solution)/shard_map/ppermute | solution.py:21
  40.8 4.1 %collective-permute-start.10 = (bf16[128,256]{1,0:T(8,128)(2,1)S(1)}, bf16[128,256]{1,0:T(8,128)(2,1)S(1)}, u32[]{:S(2)}, u32[]{:S(2)}) collective-permute-start(bf16[128,256]{1,0:T(8,128)(2,1)S(1)} %get-tuple-element.32), channel_id=1, source_target_pairs={{0,3},{1,0},{2,1},{3,2},{4,7},{5,4},{6,5},{7,6},{8,11},{9,8},{10,9... | collective-permute-start | bytes 196616 | tf_op jit(solution)/shard_map/ppermute | solution.py:21

commit v2 on v1

v2 whole, which is shorter than its diff:
```python
import functools
import math

import jax
import jax.numpy as jnp
from jax import lax
from jax.experimental import pallas as pl
from jax.experimental.pallas import tpu as pltpu
from jax.sharding import PartitionSpec as P

KEY_BLOCK = 256
CHUNK_TOKENS = 64
VMEM_LIMIT = 40 * 1024 * 1024

WHOLE = pl.BlockSpec(memory_space=pltpu.VMEM)
SCALARS = pl.BlockSpec(memory_space=pltpu.SMEM)
ANYWHERE = pl.BlockSpec(memory_space=pl.ANY)
NT = (((1,), (1,)), ((), ()))


def from_behind(shard, axis, by):
    length = lax.axis_size(axis)
    return lax.ppermute(shard, axis, [(i, (i + by) % length) for i in range(length)])


def with_partner(shard, axis, step):
    length = lax.axis_size(axis)
    return lax.ppermute(shard, axis, [(i, i ^ step) for i in range(length)])


def params():
    return pltpu.CompilerParams(vmem_limit_bytes=VMEM_LIMIT)


def cut_kernel(cuts, source_ref, *refs):
    out_refs, sems = refs[: len(cuts)], refs[len(cuts)]
    copies = [
        pltpu.make_async_copy(source_ref.at[pl.ds(first, size)], out_ref, sems.at[i])
        for i, ((first, size), out_ref) in enumerate(zip(cuts, out_refs))
    ]
    for copy in copies:
        copy.start()
    for copy in copies:
        copy.wait()


def cut(source, cuts):
    return pl.pallas_call(
        functools.partial(cut_kernel, cuts),
        out_shape=[
            jax.ShapeDtypeStruct((size, *source.shape[1:]), source.dtype) for _, size in cuts
        ],
        in_specs=[pl.BlockSpec(memory_space=pltpu.HBM)],
        out_specs=[ANYWHERE] * len(cuts),
        scratch_shapes=[pltpu.SemaphoreType.DMA((len(cuts),))],
        compiler_params=params(),
        cost_estimate=pl.CostEstimate(
            flops=0, bytes_accessed=2 * source.size * source.dtype.itemsize, transcendentals=0
        ),
    )(source)


def sort_keys_kernel(count, span_rows, head_size, starts_ref, *refs):
    blocks = refs[:count]
    keys_ref, values_ref, keys_t_ref = refs[count:]
    me = lax.axis_index("ctx")
    values_ref[:, head_size:] = jnp.full(
        (values_ref.shape[0], values_ref.shape[1] - head_size), -1.0, values_ref.dtype
    )
    for step in range(count):
        owner = lax.bitwise_xor(me, step)
        for half in range(2):
            start = pl.multiple_of(starts_ref[2 * owner + half], span_rows)
            rows = pl.ds(start, span_rows)
            part = blocks[step][half * span_rows : (half + 1) * span_rows, :]
            keys_ref[rows, :] = part[:, :head_size]
            values_ref[rows, :head_size] = part[:, head_size:]
            keys_t_ref[:, rows] = part[:, :head_size].astype(jnp.float32).T.astype(jnp.bfloat16)


def sort_keys(span_start, blocks, span_rows, head_size):
    count = len(blocks)
    total = count * 2 * span_rows
    return pl.pallas_call(
        functools.partial(sort_keys_kernel, count, span_rows, head_size),
        out_shape=(
            jax.ShapeDtypeStruct((total, head_size), jnp.bfloat16),
            jax.ShapeDtypeStruct((total, 2 * head_size), jnp.bfloat16),
            jax.ShapeDtypeStruct((head_size, total), jnp.bfloat16),
        ),
        in_specs=[SCALARS] + [WHOLE] * count,
        out_specs=(WHOLE,) * 3,
        compiler_params=params(),
    )(span_start, *blocks)


def chunk_grads(
    chunk, heads, span_rows, starts_ref, q_ref, g_ref, o_ref, lse_ref, keys_ref, values_ref,
    keys_t_ref, total_ref, dq_acc,
):
    half, first, tokens = chunk
    head_size = q_ref.shape[1]
    scale = head_size**-0.5
    to_log2 = math.log2(math.e)
    me = lax.axis_index("ctx")
    start = starts_ref[2 * me + half]
    row_count = tokens * heads
    row_first = (half * span_rows + first) * heads
    rows = slice(row_first, row_first + row_count)
    full_blocks = start // KEY_BLOCK

    q = q_ref[rows, :]
    g = g_ref[...]
    products = (g.astype(jnp.float32) * o_ref[rows, :].astype(jnp.float32)).astype(jnp.bfloat16)
    g_wide = jnp.concatenate([g, products], axis=1)
    lse2 = lse_ref[0:1, rows] * to_log2
    dq_acc[...] = jnp.zeros_like(dq_acc)

    def block(index, masked):
        base = pl.multiple_of(index * KEY_BLOCK, KEY_BLOCK)
        at = pl.ds(base, KEY_BLOCK)
        scores = lax.dot_general(keys_ref[at, :], q, NT, preferred_element_type=jnp.float32)
        probs = jnp.exp2(scores * (scale * to_log2) - lse2)
        if masked:
            query_row = lax.broadcasted_iota(jnp.int32, (1, row_count), 1)
            query_pos = start + first + query_row // heads
            key_pos = base + lax.broadcasted_iota(jnp.int32, (KEY_BLOCK, 1), 0)
            probs = jnp.where(key_pos <= query_pos, probs, 0.0)
        centred = lax.dot_general(values_ref[at, :], g_wide, NT, preferred_element_type=jnp.float32)
        grad_scores = (probs * centred).astype(jnp.bfloat16)
        probs_low = probs.astype(jnp.bfloat16)
        total_ref[at, :head_size] += jnp.dot(grad_scores, q, preferred_element_type=jnp.float32)
        total_ref[at, head_size:] += jnp.dot(probs_low, g, preferred_element_type=jnp.float32)
        dq_acc[...] += jnp.dot(keys_t_ref[:, at], grad_scores, preferred_element_type=jnp.float32)

    def dense(index, carry):
        block(index, False)
        return carry

    lax.fori_loop(0, full_blocks, dense, 0)
    block(full_blocks, True)
    return (dq_acc[...] * scale).T.astype(jnp.bfloat16)


def hand_out(half, count, span_rows, starts_ref, total_ref, own_ref, send_refs):
    head_size = total_ref.shape[1] // 2
    scale = head_size**-0.5
    me = lax.axis_index("ctx")
    for step in range(count):
        owner = lax.bitwise_xor(me, step)
        start = pl.multiple_of(starts_ref[2 * owner + half], span_rows)
        rows = pl.ds(start, span_rows)
        target = own_ref if step == 0 else send_refs[step - 1]
        target[:, :head_size] = (total_ref[rows, :head_size] * scale).astype(target.dtype)
        target[:, head_size:] = total_ref[rows, head_size:].astype(target.dtype)


def add_terms(term_refs):
    total = term_refs[0][...]
    for term_ref in term_refs[1:]:
        total = total + term_ref[...].astype(jnp.float32)
    return total


def chunk_kernel(
    chunk, heads, span_rows, count, is_first, hands_out, is_last, starts_ref, q_ref, g_ref, o_ref,
    lse_ref, keys_ref, values_ref, keys_t_ref, *refs,
):
    refs = list(refs)
    take = lambda number: [refs.pop(0) for _ in range(number)]
    total_in = None if is_first else take(1)[0]
    upper_terms = take(count) if is_last else []
    (dq_ref,) = take(1)
    total_out = None if is_last else take(1)[0]
    handed = take(count) if hands_out else []
    upper_out = take(1) if is_last else []
    total_ref, dq_acc = take(2)

    total_ref[...] = jnp.zeros_like(total_ref) if is_first else total_in[...]
    dq_ref[...] = chunk_grads(
        chunk, heads, span_rows, starts_ref, q_ref, g_ref, o_ref, lse_ref, keys_ref, values_ref,
        keys_t_ref, total_ref, dq_acc,
    )
    if hands_out:
        hand_out(chunk[0], count, span_rows, starts_ref, total_ref, handed[0], handed[1:])
    if not is_last:
        total_out[...] = total_ref[: total_out.shape[0], :]
    else:
        upper_out[0][...] = add_terms(upper_terms).astype(jnp.bfloat16)


def add_kernel(count, span_rows, head_size, *refs):
    term_refs, upper_ref, (key_ref, value_ref) = refs[:count], refs[count], refs[count + 1 :]
    lower = add_terms(term_refs).astype(jnp.bfloat16)
    for out_ref, columns in ((key_ref, slice(0, head_size)), (value_ref, slice(head_size, None))):
        out_ref[:span_rows, :] = lower[:, columns]
        out_ref[span_rows:, :] = upper_ref[:, columns]


def join_kernel(places, *refs):
    part_refs, out_ref, sems = refs[: len(places)], refs[len(places)], refs[len(places) + 1]
    copies = [
        pltpu.make_async_copy(part_ref, out_ref.at[pl.ds(first, part_ref.shape[0])], sems.at[i])
        for i, (first, part_ref) in enumerate(zip(places, part_refs))
    ]
    for copy in copies:
        copy.start()
    for copy in copies:
        copy.wait()


def join(parts, places, shape):
    return pl.pallas_call(
        functools.partial(join_kernel, places),
        out_shape=jax.ShapeDtypeStruct(shape, parts[0].dtype),
        in_specs=[ANYWHERE] * len(parts),
        out_specs=ANYWHERE,
        scratch_shapes=[pltpu.SemaphoreType.DMA((len(parts),))],
        compiler_params=params(),
    )(*parts)


def body(queries, keys, values, outputs, grad_held, lse, span_start):
    count = lax.axis_size("ctx")
    row_count, heads, head_size = queries.shape[1:]
    span_rows = row_count // 2
    total = count * row_count
    chunks = [
        (half, first, CHUNK_TOKENS) for half in (1, 0) for first in range(0, span_rows, CHUNK_TOKENS)
    ]
    per_half = len(chunks) // 2

    pieces = cut(grad_held[0], [(half * span_rows + first, size) for half, first, size in chunks])
    grads = [from_behind(piece, "section", -1) for piece in pieces]

    pair = jnp.concatenate([keys[0], values[0]], axis=1)
    blocks = [pair] + [with_partner(pair, "ctx", step) for step in range(1, count)]
    sorted_keys = sort_keys(span_start, blocks, span_rows, head_size)

    q_flat = queries.reshape(row_count * heads, head_size)
    o_flat = outputs.reshape(row_count * heads, head_size)
    lse_flat = lse[0].T.reshape(1, row_count * heads)

    span_wide = (span_rows, 2 * head_size)
    running, received, dq_parts = [], [], []
    for number, chunk in enumerate(chunks):
        half, _, tokens = chunk
        rows = tokens * heads
        is_first, is_last = number == 0, number == len(chunks) - 1
        hands_out = number % per_half == per_half - 1
        held = total if half == 1 else total // 2
        kept = total if half == 1 and not hands_out else total // 2
        out_shape = [jax.ShapeDtypeStruct((rows, head_size), jnp.bfloat16)]
        if not is_last:
            out_shape.append(jax.ShapeDtypeStruct((kept, 2 * head_size), jnp.float32))
        if hands_out:
            out_shape.append(jax.ShapeDtypeStruct(span_wide, jnp.float32))
            out_shape += [jax.ShapeDtypeStruct(span_wide, jnp.bfloat16)] * (count - 1)
        if is_last:
            out_shape.append(jax.ShapeDtypeStruct(span_wide, jnp.bfloat16))
        operands = [
            q_flat, grads[number].reshape(rows, head_size), o_flat, lse_flat, *sorted_keys, *running
        ]
        if is_last:
            operands += received
        pairs = rows * (3 * total // 4 if half == 1 else total // 4)
        results = pl.pallas_call(
            functools.partial(
                chunk_kernel, chunk, heads, span_rows, count, is_first, hands_out, is_last
            ),
            out_shape=out_shape,
            in_specs=[SCALARS] + [WHOLE] * len(operands),
            out_specs=[WHOLE] * len(out_shape),
            scratch_shapes=[
                pltpu.VMEM((held, 2 * head_size), jnp.float32),
                pltpu.VMEM((head_size, rows), jnp.float32),
            ],
            compiler_params=params(),
            cost_estimate=pl.CostEstimate(
                flops=20 * pairs * head_size, bytes_accessed=2 * 2**20, transcendentals=pairs
            ),
        )(span_start, *operands)
        results = list(results)
        dq_parts.append(results.pop(0))
        running = [] if is_last else [results.pop(0)]
        if hands_out:
            own, *sends = results[:count]
            received = [own] + [
                with_partner(send, "ctx", step) for step, send in enumerate(sends, start=1)
            ]
        if is_last:
            upper_sum = results[-1]

    key_out, value_out = pl.pallas_call(
        functools.partial(add_kernel, count, span_rows, head_size),
        out_shape=(jax.ShapeDtypeStruct((row_count, head_size), jnp.bfloat16),) * 2,
        in_specs=[WHOLE] * (count + 1),
        out_specs=(WHOLE,) * 2,
        compiler_params=params(),
    )(*received, upper_sum)
    places = [(half * span_rows + first) * heads for half, first, _ in chunks]
    dq = join(dq_parts, places, q_flat.shape)
    return (dq.reshape(queries.shape), key_out[None], value_out[None])


def solution(mesh):
    placed = (
        P("section", "ctx", None, None),
        P("section", "ctx", None),
        P("section", "ctx", None),
        P("section", "ctx", None, None),
        P("section", "ctx", None, None),
        P("section", None, "ctx"),
        P(),
    )
    return jax.shard_map(
        body,
        mesh=mesh,
        in_specs=placed,
        out_specs=(
            P("section", "ctx", None, None),
            P("section", "ctx", None),
            P("section", "ctx", None),
        ),
        check_vma=False,
    )
```

time: 45.3 us -> 43.5 us (0.960); the launches traced: 45.6 us -> 43.2 us
  waiting for transfers between devices: 15.3 us -> 9.53 us
  Pallas kernels: 13.9 us -> 15.7 us
  other arithmetic: 0.02 us -> 0.89 us
    ppermute x11 -> x4, waiting for transfers between devices: 15.3 us -> 0.01 us  [from_behind(): lax.ppermute(shard, axis, [(i, (i + by) % length) for i in range(length)])]
    ppermute x0 -> x9, waiting for transfers between devices: none -> 9.52 us  [with_partner(): return lax.ppermute(shard, axis, [(i, i ^ step) for i in range(length)])]
    ppermute x0 -> x9, starting transfers between devices: none -> 5.78 us  [with_partner(): return lax.ppermute(shard, axis, [(i, i ^ step) for i in range(length)])]
    ppermute x11 -> x4, starting transfers between devices: 13 us -> 7.65 us  [from_behind(): lax.ppermute(shard, axis, [(i, (i + by) % length) for i in range(length)])]
    squeeze x1 -> x0, local copies, waits for them, and re-layouts: 2.45 us -> none  [body(): upper_grad = from_behind(grad_held[0, span_rows:], 'section', -1)]
    pallas_call x2 -> x6, Pallas kernels: 12.4 us -> 14.3 us  [the longest x4 12.6 us: body(): pl.pallas_call(functools.partial(chunk_kernel, chunk, heads, span_rows, c...]
    unnamed x12 -> x8, local copies, waits for them, and re-layouts: 0.02 us -> 1.88 us
    concatenate x1, other arithmetic: 0.02 us -> 0.89 us  [body(): pair = jnp.concatenate([keys[0], values[0]], axis=1)]
  transfers between devices with their start and end apart: 11 -> 13, of which waited for: 7 -> 6; matrix products, arithmetic and copies ran while one was open for 0% -> 4% of each run, Pallas kernels for 18% -> 29%
where the time goes in v2:
time: 43.5 us; the launch traced here: 43.2 us
  Pallas kernels  15.7 us (36%)
  starting transfers between devices  13.4 us (31%)
  waiting for transfers between devices  9.53 us (22%)
  local copies, waits for them, and re-layouts  2.81 us (6%)
  other arithmetic  0.89 us (2%)
  between operations  0.79 us (2%)
    pallas_call x4, Pallas kernels, body(): pl.pallas_call(functools.partial(chunk_kernel, chunk, heads, span_rows, c...  12.6 us
    ppermute x9, waiting for transfers between devices, with_partner(): return lax.ppermute(shard, axis, [(i, i ^ step) for i in range(length)])  9.52 us
    ppermute x4, starting transfers between devices, from_behind(): lax.ppermute(shard, axis, [(i, (i + by) % length) for i in range(length)])  7.65 us
    ppermute x9, starting transfers between devices, with_partner(): return lax.ppermute(shard, axis, [(i, i ^ step) for i in range(length)])  5.78 us
    unnamed x8, local copies, waits for them, and re-layouts  1.88 us
    pallas_call x1, Pallas kernels, join(): pl.pallas_call(functools.partial(join_kernel, places), out_shape=jax.Shap...  0.99 us
    concatenate x1, other arithmetic, body(): pair = jnp.concatenate([keys[0], values[0]], axis=1)  0.89 us
  transfers between devices with their start and end apart: 13, of which 6 were waited for; matrix products, arithmetic and copies ran while one was open for 4% of the time, Pallas kernels for 29%

profile of v2, /device:TPU:0, one launch (start us, length us, event | category | flops | bytes accessed | tf_op | source)
XLA Modules:
  0.0 43.2 jit_solution(15061045640060234497)
XLA Ops:
  0.6 1.2 %copy-done.2 = bf16[1,256,16,128]{3,2,1,0:T(8,128)(2,1)S(1)} copy-done((bf16[1,256,16,128]{3,2,1,0:T(8,128)(2,1)S(1)}, bf16[1,256,16,128]{3,2,1,0:T(8,128)(2,1)}, u32[]{:S(2)}) %copy-start.2) | copy-done | bytes 1048600
  1.9 0.7 %shard_map.94 = (bf16[64,16,128]{2,1,0:T(8,128)(2,1)}, bf16[64,16,128]{2,1,0:T(8,128)(2,1)S(1)}, bf16[64,16,128]{2,1,0:T(8,128)(2,1)S(1)}, bf16[64,16,128]{2,1,0:T(8,128)(2,1)S(1)}) custom-call(bf16[256,16,128]{2,1,0:T(8,128)(2,1)S(1)} %bitcast.23), custom_call_target="tpu_custom_call" | custom-call | bytes 2097152 | tf_op jit(solution)/shard_map/pallas_call | solution.py:48
  2.6 6.0 %collective-permute-start = (bf16[64,16,128]{2,1,0:T(8,128)(2,1)}, bf16[64,16,128]{2,1,0:T(8,128)(2,1)}, u32[]{:S(2)}, u32[]{:S(2)}) collective-permute-start(bf16[64,16,128]{2,1,0:T(8,128)(2,1)} %get-tuple-element.28), channel_id=1, source_target_pairs={{0,28},{4,0},{8,4},{12,8},{16,12},{20,16},{24,20},{28,24},{1,29},{... | collective-permute-start | bytes 786440 | tf_op jit(solution)/shard_map/ppermute | solution.py:23
  8.6 0.9 %pad_maximum_fusion.refs_0_ = bf16[256,256]{1,0:T(8,128)(2,1)S(1)} fusion(bf16[256,128]{1,0:T(8,128)(2,1)} %bitcast.27, bf16[256,128]{1,0:T(8,128)(2,1)} %bitcast.28), kind=kLoop, calls=%fused_computation | loop fusion | flops 262144 | bytes 262144 | tf_op jit(solution)/shard_map/concatenate | solution.py:236
  9.5 0.7 %collective-permute-start.3 = (bf16[256,256]{1,0:T(8,128)(2,1)S(1)}, bf16[256,256]{1,0:T(8,128)(2,1)S(1)}, u32[]{:S(2)}, u32[]{:S(2)}) collective-permute-start(bf16[256,256]{1,0:T(8,128)(2,1)S(1)} %pad_maximum_fusion.refs_0_), channel_id=1, source_target_pairs={{0,3},{1,2},{2,1},{3,0},{4,7},{5,6},{6,5},{7,4},{8,11},{9,10},{10,... | collective-permute-start | bytes 393224 | tf_op jit(solution)/shard_map/ppermute | solution.py:28
  10.3 0.9 %collective-permute-start.2 = (bf16[256,256]{1,0:T(8,128)(2,1)S(1)}, bf16[256,256]{1,0:T(8,128)(2,1)S(1)}, u32[]{:S(2)}, u32[]{:S(2)}) collective-permute-start(bf16[256,256]{1,0:T(8,128)(2,1)S(1)} %pad_maximum_fusion.refs_0_), channel_id=1, source_target_pairs={{0,2},{1,3},{2,0},{3,1},{4,6},{5,7},{6,4},{7,5},{8,10},{9,11},{10,... | collective-permute-start | bytes 393224 | tf_op jit(solution)/shard_map/ppermute | solution.py:28
  11.2 0.3 collective-permute-start.1
  11.5 0.5 %collective-permute-start.4 = (bf16[64,16,128]{2,1,0:T(8,128)(2,1)S(1)}, bf16[64,16,128]{2,1,0:T(8,128)(2,1)}, u32[]{:S(2)}, u32[]{:S(2)}) collective-permute-start(bf16[64,16,128]{2,1,0:T(8,128)(2,1)S(1)} %get-tuple-element.33), channel_id=1, source_target_pairs={{0,28},{4,0},{8,4},{12,8},{16,12},{20,16},{24,20},{28,24},{1,29},{... | collective-permute-start | bytes 786440 | tf_op jit(solution)/shard_map/ppermute | solution.py:23
  12.0 0.8 %copy.11 = f32[256,16]{1,0:T(8,128)S(1)} copy(f32[256,16]{0,1:T(8,128)} %bitcast.29) | data formatting | bytes 32768 | tf_op jit(solution)/shard_map/transpose | solution.py:242
  12.8 0.1 reshape.33.lse_ref
  12.9 2.4 %collective-permute-done.3.refs_3_ = bf16[256,256]{1,0:T(8,128)(2,1)S(1)} collective-permute-done((bf16[256,256]{1,0:T(8,128)(2,1)S(1)}, bf16[256,256]{1,0:T(8,128)(2,1)S(1)}, u32[]{:S(2)}, u32[]{:S(2)}) %collective-permute-start.3) | collective-permute-done | bytes 131104 | tf_op jit(solution)/shard_map/ppermute | solution.py:28
  15.3 0.5 %collective-permute-start.5 = (bf16[64,16,128]{2,1,0:T(8,128)(2,1)S(1)}, bf16[64,16,128]{2,1,0:T(8,128)(2,1)S(1)}, u32[]{:S(2)}, u32[]{:S(2)}) collective-permute-start(bf16[64,16,128]{2,1,0:T(8,128)(2,1)S(1)} %get-tuple-element.36), channel_id=1, source_target_pairs={{0,28},{4,0},{8,4},{12,8},{16,12},{20,16},{24,20},{28,24},{1,29},{... | collective-permute-start | bytes 786440 | tf_op jit(solution)/shard_map/ppermute | solution.py:23
  15.9 2.3 %collective-permute-done.2.refs_2_ = bf16[256,256]{1,0:T(8,128)(2,1)S(1)} collective-permute-done((bf16[256,256]{1,0:T(8,128)(2,1)S(1)}, bf16[256,256]{1,0:T(8,128)(2,1)S(1)}, u32[]{:S(2)}, u32[]{:S(2)}) %collective-permute-start.2) | collective-permute-done | bytes 131104 | tf_op jit(solution)/shard_map/ppermute | solution.py:28
  18.2 0.5 %collective-permute-start.6 = (bf16[64,16,128]{2,1,0:T(8,128)(2,1)S(1)}, bf16[64,16,128]{2,1,0:T(8,128)(2,1)S(1)}, u32[]{:S(2)}, u32[]{:S(2)}) collective-permute-start(bf16[64,16,128]{2,1,0:T(8,128)(2,1)S(1)} %get-tuple-element.39), channel_id=1, source_target_pairs={{0,28},{4,0},{8,4},{12,8},{16,12},{20,16},{24,20},{28,24},{1,29},{... | collective-permute-start | bytes 786440 | tf_op jit(solution)/shard_map/ppermute | solution.py:23
  18.7 0.7 %copy-done.3 = s32[8]{0:T(128)S(1)} copy-done((s32[8]{0:T(128)S(1)}, s32[8]{0:T(128)}, u32[]{:S(2)}) %copy-start.3) | copy-done | bytes 56
  19.4 0.8 %shard_map.95 = (bf16[1024,128]{1,0:T(8,128)(2,1)S(1)}, bf16[1024,256]{1,0:T(8,128)(2,1)S(1)}, bf16[128,1024]{1,0:T(8,128)(2,1)S(1)}) custom-call(s32[8]{0:T(128)S(1)} %copy-done.3, bf16[256,256]{1,0:T(8,128)(2,1)S(1)} %pad_maximum_fusion.refs_0_, bf16[256,256]{1,0:T(8,128)(2,1)S(1)} %collective-permute-done.1.refs_1_, ...), custom_call_target="tpu_custom_call" | custom-call | tf_op jit(solution)/shard_map/pallas_call | solution.py:84
  20.2 4.6 %shard_map.96 = (bf16[1024,128]{1,0:T(8,128)(2,1)S(1)}, f32[1024,256]{1,0:T(8,128)S(1)}) custom-call(s32[8]{0:T(128)S(1)} %copy-done.3, bf16[4096,128]{1,0:T(8,128)(2,1)S(1)} %bitcast.15, bf16[1024,128]{1,0:T(8,128)(2,1)} %bitcast.2.g_ref, bf16[4096,128]{1,0:T(8,128)(2,1)S(1)} %bitcast.19, f32[1,4096]{1,0:T(1,128)S(1)} %reshape.33.lse_ref, ...), custom_call_target="tpu_custom_call" | custom-call | flops 2013265920 | bytes 2097152 | tf_op jit(solution)/shard_map/pallas_call | solution.py:267
  24.8 4.6 %shard_map.97 = (bf16[1024,128]{1,0:T(8,128)(2,1)S(1)}, f32[512,256]{1,0:T(8,128)S(1)}, f32[128,256]{1,0:T(8,128)S(1)}, bf16[128,256]{1,0:T(8,128)(2,1)S(1)}, bf...) custom-call(s32[8]{0:T(128)S(1)} %copy-done.3, bf16[4096,128]{1,0:T(8,128)(2,1)S(1)} %bitcast.16, ...), custom_call_target="tpu_custom_call" | custom-call | flops 2013265920 | bytes 2097152 | tf_op jit(solution)/shard_map/pallas_call | solution.py:267
  29.4 0.1 collective-permute-start.7
  29.4 0.1 collective-permute-start.8
  29.5 1.8 %collective-permute-start.9 = (bf16[128,256]{1,0:T(8,128)(2,1)S(1)}, bf16[128,256]{1,0:T(8,128)(2,1)S(1)}, u32[]{:S(2)}, u32[]{:S(2)}) collective-permute-start(bf16[128,256]{1,0:T(8,128)(2,1)S(1)} %get-tuple-element.44), channel_id=1, source_target_pairs={{0,3},{1,2},{2,1},{3,0},{4,7},{5,6},{6,5},{7,4},{8,11},{9,10},{10,... | collective-permute-start | bytes 196616 | tf_op jit(solution)/shard_map/ppermute | solution.py:28
  31.3 1.7 %shard_map.98 = (bf16[1024,128]{1,0:T(8,128)(2,1)S(1)}, f32[512,256]{1,0:T(8,128)S(1)}) custom-call(s32[8]{0:T(128)S(1)} %copy-done.3, bf16[4096,128]{1,0:T(8,128)(2,1)S(1)} %bitcast.17, bf16[1024,128]{1,0:T(8,128)(2,1)S(1)} %bitcast.25, bf16[4096,128]{1,0:T(8,128)(2,1)S(1)} %bitcast.21, f32[1,4096]{1,0:T(1,128)S(1)} %reshape.33.lse_ref, ...), custom_call_target="tpu_custom_call" | custom-call | flops 671088640 | bytes 2097152 | tf_op jit(solution)/shard_map/pallas_call | solution.py:267
  33.0 1.4 %collective-permute-done.8.refs_3_ = bf16[128,256]{1,0:T(8,128)(2,1)S(1)} collective-permute-done((bf16[128,256]{1,0:T(8,128)(2,1)S(1)}, bf16[128,256]{1,0:T(8,128)(2,1)S(1)}, u32[]{:S(2)}, u32[]{:S(2)}) %collective-permute-start.8) | collective-permute-done | bytes 65568 | tf_op jit(solution)/shard_map/ppermute | solution.py:28
  34.4 0.5 %collective-permute-done.9.refs_4_ = bf16[128,256]{1,0:T(8,128)(2,1)S(1)} collective-permute-done((bf16[128,256]{1,0:T(8,128)(2,1)S(1)}, bf16[128,256]{1,0:T(8,128)(2,1)S(1)}, u32[]{:S(2)}, u32[]{:S(2)}) %collective-permute-start.9) | collective-permute-done | bytes 65568 | tf_op jit(solution)/shard_map/ppermute | solution.py:28
  34.9 1.7 %shard_map.99 = (bf16[1024,128]{1,0:T(8,128)(2,1)S(1)}, f32[128,256]{1,0:T(8,128)S(1)}, bf16[128,256]{1,0:T(8,128)(2,1)S(1)}, bf16[128,256]{1,0:T(8,128)(2,1)S(1...) custom-call(s32[8]{0:T(128)S(1)} %copy-done.3, bf16[4096,128]{1,0:T(8,128)(2,1)S(1)} %bitcast.18, ...), custom_call_target="tpu_custom_call" | custom-call | flops 671088640 | bytes 2097152 | tf_op jit(solution)/shard_map/pallas_call | solution.py:267
  36.6 0.3 collective-permute-start.10
  37.0 1.4 %collective-permute-start.11 = (bf16[128,256]{1,0:T(8,128)(2,1)S(1)}, bf16[128,256]{1,0:T(8,128)(2,1)S(1)}, u32[]{:S(2)}, u32[]{:S(2)}) collective-permute-start(bf16[128,256]{1,0:T(8,128)(2,1)S(1)} %get-tuple-element.48), channel_id=1, source_target_pairs={{0,2},{1,3},{2,0},{3,1},{4,6},{5,7},{6,4},{7,5},{8,10},{9,11},{10,... | collective-permute-start | bytes 196616 | tf_op jit(solution)/shard_map/ppermute | solution.py:28
  38.4 0.2 collective-permute-start.12
  38.6 1.0 %shard_map.100 = bf16[4096,128]{1,0:T(8,128)(2,1)} custom-call(bf16[1024,128]{1,0:T(8,128)(2,1)S(1)} %get-tuple-element.32.refs_0_, bf16[1024,128]{1,0:T(8,128)(2,1)S(1)} %get-tuple-element.35.refs_1_, bf16[1024,128]{1,0:T(8,128)(2,1)S(1)} %get-tuple-element.38.refs_2_, bf16[1024,128]{1,0:T(8,128)(2,1)S(1)} %get-tuple-element.45.refs_3_), custom_call_target="tpu_custom_call" | custom-call | tf_op jit(solution)/shard_map/pallas_call | solution.py:213
  39.6 1.7 %collective-permute-done.11.refs_2_ = bf16[128,256]{1,0:T(8,128)(2,1)S(1)} collective-permute-done((bf16[128,256]{1,0:T(8,128)(2,1)S(1)}, bf16[128,256]{1,0:T(8,128)(2,1)S(1)}, u32[]{:S(2)}, u32[]{:S(2)}) %collective-permute-start.11) | collective-permute-done | bytes 65568 | tf_op jit(solution)/shard_map/ppermute | solution.py:28
  41.3 1.2 %collective-permute-done.12.refs_3_ = bf16[128,256]{1,0:T(8,128)(2,1)S(1)} collective-permute-done((bf16[128,256]{1,0:T(8,128)(2,1)S(1)}, bf16[128,256]{1,0:T(8,128)(2,1)S(1)}, u32[]{:S(2)}, u32[]{:S(2)}) %collective-permute-start.12) | collective-permute-done | bytes 65568 | tf_op jit(solution)/shard_map/ppermute | solution.py:28
  42.5 0.7 %shard_map.101 = (bf16[256,128]{1,0:T(8,128)(2,1)}, bf16[256,128]{1,0:T(8,128)(2,1)}) custom-call(f32[128,256]{1,0:T(8,128)S(1)} %get-tuple-element.46.refs_0_, bf16[128,256]{1,0:T(8,128)(2,1)S(1)} %collective-permute-done.10.refs_1_, bf16[128,256]{1,0:T(8,128)(2,1)S(1)} %collective-permute-done.11.refs_2_, ...), custom_call_target="tpu_custom_call" | custom-call | tf_op jit(solution)/shard_map/pallas_call | solution.py:294
  (13 shorter events, 0.0 us)
Async XLA Ops:
  0.6 1.2 %copy-start.2 = (bf16[1,256,16,128]{3,2,1,0:T(8,128)(2,1)S(1)}, bf16[1,256,16,128]{3,2,1,0:T(8,128)(2,1)}, u32[]{:S(2)}) copy-start(bf16[1,256,16,128]{3,2,1,0:T(8,128)(2,1)} %param.11) | copy-start | bytes 3145732
  1.9 18.3 %copy-start = (bf16[1,256,16,128]{3,2,1,0:T(8,128)(2,1)S(1)}, bf16[1,256,16,128]{3,2,1,0:T(8,128)(2,1)}, u32[]{:S(2)}) copy-start(bf16[1,256,16,128]{3,2,1,0:T(8,128)(2,1)} %param.7) | copy-start | bytes 3145732
  1.9 18.3 %copy-start.1 = (bf16[1,256,16,128]{3,2,1,0:T(8,128)(2,1)S(1)}, bf16[1,256,16,128]{3,2,1,0:T(8,128)(2,1)}, u32[]{:S(2)}) copy-start(bf16[1,256,16,128]{3,2,1,0:T(8,128)(2,1)} %param.10) | copy-start | bytes 3145732
  2.6 17.6 %collective-permute-start = (bf16[64,16,128]{2,1,0:T(8,128)(2,1)}, bf16[64,16,128]{2,1,0:T(8,128)(2,1)}, u32[]{:S(2)}, u32[]{:S(2)}) collective-permute-start(bf16[64,16,128]{2,1,0:T(8,128)(2,1)} %get-tuple-element.28), channel_id=1, source_target_pairs={{0,28},{4,0},{8,4},{12,8},{16,12},{20,16},{24,20},{28,24},{1,29},{... | collective-permute-start | bytes 786440 | tf_op jit(solution)/shard_map/ppermute | solution.py:23
  9.5 5.8 %collective-permute-start.3 = (bf16[256,256]{1,0:T(8,128)(2,1)S(1)}, bf16[256,256]{1,0:T(8,128)(2,1)S(1)}, u32[]{:S(2)}, u32[]{:S(2)}) collective-permute-start(bf16[256,256]{1,0:T(8,128)(2,1)S(1)} %pad_maximum_fusion.refs_0_), channel_id=1, source_target_pairs={{0,3},{1,2},{2,1},{3,0},{4,7},{5,6},{6,5},{7,4},{8,11},{9,10},{10,... | collective-permute-start | bytes 393224 | tf_op jit(solution)/shard_map/ppermute | solution.py:28
  10.3 7.9 %collective-permute-start.2 = (bf16[256,256]{1,0:T(8,128)(2,1)S(1)}, bf16[256,256]{1,0:T(8,128)(2,1)S(1)}, u32[]{:S(2)}, u32[]{:S(2)}) collective-permute-start(bf16[256,256]{1,0:T(8,128)(2,1)S(1)} %pad_maximum_fusion.refs_0_), channel_id=1, source_target_pairs={{0,2},{1,3},{2,0},{3,1},{4,6},{5,7},{6,4},{7,5},{8,10},{9,11},{10,... | collective-permute-start | bytes 393224 | tf_op jit(solution)/shard_map/ppermute | solution.py:28
  11.2 7.5 %collective-permute-start.1 = (bf16[256,256]{1,0:T(8,128)(2,1)S(1)}, bf16[256,256]{1,0:T(8,128)(2,1)S(1)}, u32[]{:S(2)}, u32[]{:S(2)}) collective-permute-start(bf16[256,256]{1,0:T(8,128)(2,1)S(1)} %pad_maximum_fusion.refs_0_), channel_id=1, source_target_pairs={{0,1},{1,0},{2,3},{3,2},{4,5},{5,4},{6,7},{7,6},{8,9},{9,8},{10,11... | collective-permute-start | bytes 393224 | tf_op jit(solution)/shard_map/ppermute | solution.py:28
  11.5 13.3 %collective-permute-start.4 = (bf16[64,16,128]{2,1,0:T(8,128)(2,1)S(1)}, bf16[64,16,128]{2,1,0:T(8,128)(2,1)}, u32[]{:S(2)}, u32[]{:S(2)}) collective-permute-start(bf16[64,16,128]{2,1,0:T(8,128)(2,1)S(1)} %get-tuple-element.33), channel_id=1, source_target_pairs={{0,28},{4,0},{8,4},{12,8},{16,12},{20,16},{24,20},{28,24},{1,29},{... | collective-permute-start | bytes 786440 | tf_op jit(solution)/shard_map/ppermute | solution.py:23
  15.3 16.0 %collective-permute-start.5 = (bf16[64,16,128]{2,1,0:T(8,128)(2,1)S(1)}, bf16[64,16,128]{2,1,0:T(8,128)(2,1)S(1)}, u32[]{:S(2)}, u32[]{:S(2)}) collective-permute-start(bf16[64,16,128]{2,1,0:T(8,128)(2,1)S(1)} %get-tuple-element.36), channel_id=1, source_target_pairs={{0,28},{4,0},{8,4},{12,8},{16,12},{20,16},{24,20},{28,24},{1,29},{... | collective-permute-start | bytes 786440 | tf_op jit(solution)/shard_map/ppermute | solution.py:23
  18.2 14.8 %collective-permute-start.6 = (bf16[64,16,128]{2,1,0:T(8,128)(2,1)S(1)}, bf16[64,16,128]{2,1,0:T(8,128)(2,1)S(1)}, u32[]{:S(2)}, u32[]{:S(2)}) collective-permute-start(bf16[64,16,128]{2,1,0:T(8,128)(2,1)S(1)} %get-tuple-element.39), channel_id=1, source_target_pairs={{0,28},{4,0},{8,4},{12,8},{16,12},{20,16},{24,20},{28,24},{1,29},{... | collective-permute-start | bytes 786440 | tf_op jit(solution)/shard_map/ppermute | solution.py:23
  18.7 0.7 %copy-start.3 = (s32[8]{0:T(128)S(1)}, s32[8]{0:T(128)}, u32[]{:S(2)}) copy-start(s32[8]{0:T(128)} %starts_ref.9) | copy-start | bytes 100
  29.4 3.7 %collective-permute-start.7 = (bf16[128,256]{1,0:T(8,128)(2,1)S(1)}, bf16[128,256]{1,0:T(8,128)(2,1)S(1)}, u32[]{:S(2)}, u32[]{:S(2)}) collective-permute-start(bf16[128,256]{1,0:T(8,128)(2,1)S(1)} %get-tuple-element.42), channel_id=1, source_target_pairs={{0,1},{1,0},{2,3},{3,2},{4,5},{5,4},{6,7},{7,6},{8,9},{9,8},{10,11... | collective-permute-start | bytes 196616 | tf_op jit(solution)/shard_map/ppermute | solution.py:28
  29.4 5.0 %collective-permute-start.8 = (bf16[128,256]{1,0:T(8,128)(2,1)S(1)}, bf16[128,256]{1,0:T(8,128)(2,1)S(1)}, u32[]{:S(2)}, u32[]{:S(2)}) collective-permute-start(bf16[128,256]{1,0:T(8,128)(2,1)S(1)} %get-tuple-element.43), channel_id=1, source_target_pairs={{0,2},{1,3},{2,0},{3,1},{4,6},{5,7},{6,4},{7,5},{8,10},{9,11},{10,... | collective-permute-start | bytes 196616 | tf_op jit(solution)/shard_map/ppermute | solution.py:28
  29.5 5.4 %collective-permute-start.9 = (bf16[128,256]{1,0:T(8,128)(2,1)S(1)}, bf16[128,256]{1,0:T(8,128)(2,1)S(1)}, u32[]{:S(2)}, u32[]{:S(2)}) collective-permute-start(bf16[128,256]{1,0:T(8,128)(2,1)S(1)} %get-tuple-element.44), channel_id=1, source_target_pairs={{0,3},{1,2},{2,1},{3,0},{4,7},{5,6},{6,5},{7,4},{8,11},{9,10},{10,... | collective-permute-start | bytes 196616 | tf_op jit(solution)/shard_map/ppermute | solution.py:28
  36.6 2.9 %collective-permute-start.10 = (bf16[128,256]{1,0:T(8,128)(2,1)S(1)}, bf16[128,256]{1,0:T(8,128)(2,1)S(1)}, u32[]{:S(2)}, u32[]{:S(2)}) collective-permute-start(bf16[128,256]{1,0:T(8,128)(2,1)S(1)} %get-tuple-element.47), channel_id=1, source_target_pairs={{0,1},{1,0},{2,3},{3,2},{4,5},{5,4},{6,7},{7,6},{8,9},{9,8},{10,11... | collective-permute-start | bytes 196616 | tf_op jit(solution)/shard_map/ppermute | solution.py:28
  37.0 4.3 %collective-permute-start.11 = (bf16[128,256]{1,0:T(8,128)(2,1)S(1)}, bf16[128,256]{1,0:T(8,128)(2,1)S(1)}, u32[]{:S(2)}, u32[]{:S(2)}) collective-permute-start(bf16[128,256]{1,0:T(8,128)(2,1)S(1)} %get-tuple-element.48), channel_id=1, source_target_pairs={{0,2},{1,3},{2,0},{3,1},{4,6},{5,7},{6,4},{7,5},{8,10},{9,11},{10,... | collective-permute-start | bytes 196616 | tf_op jit(solution)/shard_map/ppermute | solution.py:28
  38.4 4.1 %collective-permute-start.12 = (bf16[128,256]{1,0:T(8,128)(2,1)S(1)}, bf16[128,256]{1,0:T(8,128)(2,1)S(1)}, u32[]{:S(2)}, u32[]{:S(2)}) collective-permute-start(bf16[128,256]{1,0:T(8,128)(2,1)S(1)} %get-tuple-element.49), channel_id=1, source_target_pairs={{0,3},{1,2},{2,1},{3,0},{4,7},{5,6},{6,5},{7,4},{8,11},{9,10},{10,... | collective-permute-start | bytes 196616 | tf_op jit(solution)/shard_map/ppermute | solution.py:28

commit v3 on v2

v3 whole, which is shorter than its diff:
```python
import functools
import math

import jax
import jax.numpy as jnp
from jax import lax
from jax.experimental import pallas as pl
from jax.experimental.pallas import tpu as pltpu
from jax.sharding import PartitionSpec as P

KEY_BLOCK = 256
CHUNK_TOKENS = 64
VMEM_LIMIT = 40 * 1024 * 1024
CUT_LIMIT = 60 * 1024 * 1024

WHOLE = pl.BlockSpec(memory_space=pltpu.VMEM)
SCALARS = pl.BlockSpec(memory_space=pltpu.SMEM)
ANYWHERE = pl.BlockSpec(memory_space=pl.ANY)
NT = (((1,), (1,)), ((), ()))


def from_behind(shard, axis, by):
    length = lax.axis_size(axis)
    return lax.ppermute(shard, axis, [(i, (i + by) % length) for i in range(length)])


def with_partner(shard, axis, step):
    length = lax.axis_size(axis)
    return lax.ppermute(shard, axis, [(i, i ^ step) for i in range(length)])


def params(limit=VMEM_LIMIT):
    return pltpu.CompilerParams(vmem_limit_bytes=limit)


def cut_kernel(cuts, starts_in_ref, source_ref, keys_ref, values_ref, *refs):
    starts_ref, pair_ref, *out_refs, sems = refs
    head_size = keys_ref.shape[1]
    moves = [(keys_ref, pair_ref.at[:, pl.ds(0, head_size)])]
    moves.append((values_ref, pair_ref.at[:, pl.ds(head_size, head_size)]))
    for (first, size), out_ref in zip(cuts, out_refs):
        moves.append((source_ref.at[pl.ds(first, size)], out_ref))
    copies = [pltpu.make_async_copy(*move, sems.at[i]) for i, move in enumerate(moves)]
    for copy in copies:
        copy.start()
    for span in range(starts_ref.shape[0]):
        starts_ref[span] = starts_in_ref[span]
    for copy in copies:
        copy.wait()


def cut(span_start, source, keys, values, cuts):
    row_count, head_size = keys.shape
    return pl.pallas_call(
        functools.partial(cut_kernel, cuts),
        out_shape=[
            jax.ShapeDtypeStruct(span_start.shape, span_start.dtype),
            jax.ShapeDtypeStruct((row_count, 2 * head_size), keys.dtype),
        ]
        + [jax.ShapeDtypeStruct((size, *source.shape[1:]), source.dtype) for _, size in cuts],
        in_specs=[SCALARS] + [ANYWHERE] * 3,
        out_specs=[SCALARS] + [ANYWHERE] * (len(cuts) + 1),
        scratch_shapes=[pltpu.SemaphoreType.DMA((len(cuts) + 2,))],
        compiler_params=params(CUT_LIMIT),
        cost_estimate=pl.CostEstimate(
            flops=0, bytes_accessed=2 * source.size * source.dtype.itemsize, transcendentals=0
        ),
    )(span_start, source, keys, values)


def sort_keys_kernel(codes, span_rows, head_size, starts_ref, *refs):
    count = len(codes)
    blocks = refs[:count]
    keys_ref, values_ref, keys_t_ref = refs[count:]
    me = lax.axis_index("ctx")
    values_ref[:, head_size:] = jnp.full(
        (values_ref.shape[0], values_ref.shape[1] - head_size), -1.0, values_ref.dtype
    )
    for block, code in zip(blocks, codes):
        owner = lax.bitwise_xor(me, code)
        for half in range(2):
            start = pl.multiple_of(starts_ref[2 * owner + half], span_rows)
            rows = pl.ds(start, span_rows)
            part = block[half * span_rows : (half + 1) * span_rows, :]
            keys_ref[rows, :] = part[:, :head_size]
            values_ref[rows, :head_size] = part[:, head_size:]
            keys_t_ref[:, rows] = part[:, :head_size].astype(jnp.float32).T.astype(jnp.bfloat16)


def sort_keys(span_start, blocks, codes, span_rows, head_size):
    count = len(blocks)
    total = count * 2 * span_rows
    return pl.pallas_call(
        functools.partial(sort_keys_kernel, codes, span_rows, head_size),
        out_shape=(
            jax.ShapeDtypeStruct((total, head_size), jnp.bfloat16),
            jax.ShapeDtypeStruct((total, 2 * head_size), jnp.bfloat16),
            jax.ShapeDtypeStruct((head_size, total), jnp.bfloat16),
        ),
        in_specs=[SCALARS] + [WHOLE] * count,
        out_specs=(WHOLE,) * 3,
        compiler_params=params(),
    )(span_start, *blocks)


def chunk_grads(
    chunk, heads, span_rows, starts_ref, q_ref, g_ref, o_ref, lse_ref, keys_ref, values_ref,
    keys_t_ref, total_ref, dq_ref,
):
    half, first, tokens = chunk
    head_size = q_ref.shape[1]
    scale = head_size**-0.5
    to_log2 = math.log2(math.e)
    me = lax.axis_index("ctx")
    start = starts_ref[2 * me + half]
    row_count = tokens * heads
    row_first = (half * span_rows + first) * heads
    rows = slice(row_first, row_first + row_count)
    full_blocks = start // KEY_BLOCK

    q = q_ref[rows, :]
    g = g_ref[...]
    products = (g.astype(jnp.float32) * o_ref[rows, :].astype(jnp.float32)).astype(jnp.bfloat16)
    g_wide = jnp.concatenate([g, products], axis=1)
    lse2 = lse_ref[0:1, rows] * to_log2
    dq_ref[...] = jnp.zeros_like(dq_ref)

    def block(index, masked):
        base = pl.multiple_of(index * KEY_BLOCK, KEY_BLOCK)
        at = pl.ds(base, KEY_BLOCK)
        scores = lax.dot_general(keys_ref[at, :], q, NT, preferred_element_type=jnp.float32)
        probs = jnp.exp2(scores * (scale * to_log2) - lse2)
        if masked:
            query_row = lax.broadcasted_iota(jnp.int32, (1, row_count), 1)
            query_pos = start + first + query_row // heads
            key_pos = base + lax.broadcasted_iota(jnp.int32, (KEY_BLOCK, 1), 0)
            probs = jnp.where(key_pos <= query_pos, probs, 0.0)
        centred = lax.dot_general(values_ref[at, :], g_wide, NT, preferred_element_type=jnp.float32)
        grad_scores = (probs * centred).astype(jnp.bfloat16)
        probs_low = probs.astype(jnp.bfloat16)
        total_ref[at, :head_size] += jnp.dot(grad_scores, q, preferred_element_type=jnp.float32)
        total_ref[at, head_size:] += jnp.dot(probs_low, g, preferred_element_type=jnp.float32)
        dq_ref[...] += jnp.dot(keys_t_ref[:, at], grad_scores, preferred_element_type=jnp.float32)

    def dense(index, carry):
        block(index, False)
        return carry

    lax.fori_loop(0, full_blocks, dense, 0)
    block(full_blocks, True)


def hand_out(half, count, span_rows, starts_ref, total_ref, own_ref, send_refs):
    head_size = total_ref.shape[1] // 2
    scale = head_size**-0.5
    me = lax.axis_index("ctx")
    for step in range(count):
        owner = lax.bitwise_xor(me, step)
        start = pl.multiple_of(starts_ref[2 * owner + half], span_rows)
        rows = pl.ds(start, span_rows)
        target = own_ref if step == 0 else send_refs[step - 1]
        target[:, :head_size] = (total_ref[rows, :head_size] * scale).astype(target.dtype)
        target[:, head_size:] = total_ref[rows, head_size:].astype(target.dtype)


def add_terms(term_refs):
    total = term_refs[0][...]
    for term_ref in term_refs[1:]:
        total = total + term_ref[...].astype(jnp.float32)
    return total


def chunk_kernel(
    chunk, heads, span_rows, count, is_first, hands_out, n_after, starts_ref, q_ref, g_ref, o_ref,
    lse_ref, keys_ref, values_ref, keys_t_ref, *refs,
):
    refs = list(refs[n_after:])
    total_in = None if is_first else refs.pop(0)
    dq_ref, total_ref, *handed = refs
    if is_first:
        total_ref[...] = jnp.zeros_like(total_ref)
    else:
        total_ref[...] = total_in[: total_ref.shape[0], :]
    chunk_grads(
        chunk, heads, span_rows, starts_ref, q_ref, g_ref, o_ref, lse_ref, keys_ref, values_ref,
        keys_t_ref, total_ref, dq_ref,
    )
    if hands_out:
        hand_out(chunk[0], count, span_rows, starts_ref, total_ref, handed[0], handed[1:])


def add_kernel(count, span_rows, head_size, *refs):
    term_refs, upper_ref, (key_ref, value_ref) = refs[:count], refs[count], refs[count + 1 :]
    lower = add_terms(term_refs).astype(jnp.bfloat16)
    for out_ref, columns in ((key_ref, slice(0, head_size)), (value_ref, slice(head_size, None))):
        out_ref[:span_rows, :] = lower[:, columns]
        out_ref[span_rows:, :] = upper_ref[:, columns]


def finish_kernel(count, places, *refs):
    term_refs, refs = refs[:count], refs[count:]
    part_refs, (upper_ref, out_ref, held, sems) = refs[: len(places)], refs[len(places) :]
    scale = out_ref.shape[1] ** -0.5
    copies = []
    for i, (first, part_ref) in enumerate(zip(places, part_refs)):
        rows = pl.ds(first, part_ref.shape[1])
        held[rows, :] = (part_ref[...] * scale).T.astype(jnp.bfloat16)
        copies.append(pltpu.make_async_copy(held.at[rows], out_ref.at[rows], sems.at[i]))
        copies[-1].start()
    upper_ref[...] = add_terms(term_refs).astype(jnp.bfloat16)
    for copy in copies:
        copy.wait()


def finish(terms, parts, places, shape):
    return pl.pallas_call(
        functools.partial(finish_kernel, len(terms), places),
        out_shape=(
            jax.ShapeDtypeStruct(terms[0].shape, jnp.bfloat16),
            jax.ShapeDtypeStruct(shape, jnp.bfloat16),
        ),
        in_specs=[WHOLE] * (len(terms) + len(parts)),
        out_specs=(WHOLE, ANYWHERE),
        scratch_shapes=[
            pltpu.VMEM(shape, jnp.bfloat16),
            pltpu.SemaphoreType.DMA((len(parts),)),
        ],
        compiler_params=params(),
    )(*terms, *parts)


def body(queries, keys, values, outputs, grad_held, lse, span_start):
    count = lax.axis_size("ctx")
    row_count, heads, head_size = queries.shape[1:]
    span_rows = row_count // 2
    total = count * row_count
    chunks = [
        (half, first, CHUNK_TOKENS) for half in (1, 0) for first in range(0, span_rows, CHUNK_TOKENS)
    ]
    per_half = len(chunks) // 2

    starts, pair, *pieces = cut(
        span_start, grad_held[0], keys[0], values[0],
        [(half * span_rows + first, size) for half, first, size in chunks],
    )
    grads = [from_behind(piece, "section", -1) for piece in pieces]

    blocks, codes = [pair], [0]
    step = count // 2
    while step:
        blocks = blocks + [with_partner(block, "ctx", step) for block in blocks]
        codes = codes + [code ^ step for code in codes]
        step //= 2
    sorted_keys = sort_keys(starts, blocks, codes, span_rows, head_size)

    q_flat = queries.reshape(row_count * heads, head_size)
    o_flat = outputs.reshape(row_count * heads, head_size)
    lse_flat = lse[0].T.reshape(1, row_count * heads)

    span_wide = (span_rows, 2 * head_size)
    running, received, dq_parts = [], [], []
    for number, chunk in enumerate(chunks):
        half, _, tokens = chunk
        rows = tokens * heads
        is_first = number == 0
        hands_out = number % per_half == per_half - 1
        after = received if number == len(chunks) - 1 else []
        if after:
            upper_terms = received
        operands = [
            q_flat, grads[number].reshape(rows, head_size), o_flat, lse_flat, *sorted_keys, *after,
            *running,
        ]
        out_shape = [
            jax.ShapeDtypeStruct((head_size, rows), jnp.float32),
            jax.ShapeDtypeStruct((total if half else total // 2, 2 * head_size), jnp.float32),
        ]
        if hands_out:
            out_shape.append(jax.ShapeDtypeStruct(span_wide, jnp.float32))
            out_shape += [jax.ShapeDtypeStruct(span_wide, jnp.bfloat16)] * (count - 1)
        pairs = rows * (3 * total // 4 if half == 1 else total // 4)
        dq, running_total, *handed = pl.pallas_call(
            functools.partial(
                chunk_kernel, chunk, heads, span_rows, count, is_first, hands_out, len(after)
            ),
            out_shape=out_shape,
            in_specs=[SCALARS] + [WHOLE] * len(operands),
            out_specs=[WHOLE] * len(out_shape),
            compiler_params=params(),
            cost_estimate=pl.CostEstimate(
                flops=20 * pairs * head_size, bytes_accessed=2 * 2**20, transcendentals=pairs
            ),
        )(starts, *operands)
        dq_parts.append(dq)
        running = [running_total]
        if hands_out:
            received = [handed[0]] + [
                with_partner(send, "ctx", step) for step, send in enumerate(handed[1:], start=1)
            ]

    places = [(half * span_rows + first) * heads for half, first, _ in chunks]
    upper_sum, dq = finish(upper_terms, dq_parts, places, q_flat.shape)
    key_out, value_out = pl.pallas_call(
        functools.partial(add_kernel, count, span_rows, head_size),
        out_shape=(jax.ShapeDtypeStruct((row_count, head_size), jnp.bfloat16),) * 2,
        in_specs=[WHOLE] * (count + 1),
        out_specs=(WHOLE,) * 2,
        compiler_params=params(),
    )(*received, upper_sum)
    return (dq.reshape(queries.shape), key_out[None], value_out[None])


def solution(mesh):
    placed = (
        P("section", "ctx", None, None),
        P("section", "ctx", None),
        P("section", "ctx", None),
        P("section", "ctx", None, None),
        P("section", "ctx", None, None),
        P("section", None, "ctx"),
        P(),
    )
    return jax.shard_map(
        body,
        mesh=mesh,
        in_specs=placed,
        out_specs=(
            P("section", "ctx", None, None),
            P("section", "ctx", None),
            P("section", "ctx", None),
        ),
        check_vma=False,
    )
```

time: 43.5 us -> 78.1 us (1.80)
  Pallas kernels: 15.7 us -> 52.8 us
  waiting for transfers between devices: 9.53 us -> 5.25 us
  starting transfers between devices: 13.4 us -> 17.2 us
  local copies, waits for them, and re-layouts: 2.81 us -> 1.45 us
  other arithmetic: 0.89 us -> 0 us
    pallas_call x1, Pallas kernels: 0.74 us -> 38.2 us  [cut(): pl.pallas_call(functools.partial(cut_kernel, cuts), out_shape=[jax.ShapeD...]
    ppermute x9, waiting for transfers between devices: 9.52 us -> 2.66 us  [with_partner(): return lax.ppermute(shard, axis, [(i, i ^ step) for i in range(length)])]
    ppermute x4, waiting for transfers between devices: 0.01 us -> 2.59 us  [from_behind(): lax.ppermute(shard, axis, [(i, (i + by) % length) for i in range(length)])]
    ppermute x4, starting transfers between devices: 7.65 us -> 9.91 us  [from_behind(): lax.ppermute(shard, axis, [(i, (i + by) % length) for i in range(length)])]
    ppermute x9, starting transfers between devices: 5.78 us -> 7.33 us  [with_partner(): return lax.ppermute(shard, axis, [(i, i ^ step) for i in range(length)])]
    concatenate x1 -> x0, other arithmetic: 0.89 us -> none  [body(): pair = jnp.concatenate([keys[0], values[0]], axis=1)]
    unnamed x8 -> x10, local copies, waits for them, and re-layouts: 1.88 us -> 1.24 us
  transfers between devices with their start and end apart: 13 -> 13, of which waited for: 6 -> 3; matrix products, arithmetic and copies ran while one was open for 4% -> 0% of each run, Pallas kernels for 29% -> 15%
where the time goes in v3:
time: 78.1 us; the launch traced here: 77.6 us
  Pallas kernels  52.8 us (68%)
  starting transfers between devices  17.2 us (22%)
  waiting for transfers between devices  5.25 us (7%)
  local copies, waits for them, and re-layouts  1.45 us (2%)
  between operations  0.79 us (1%)
    pallas_call x1, Pallas kernels, cut(): pl.pallas_call(functools.partial(cut_kernel, cuts), out_shape=[jax.ShapeD...  38.2 us
    pallas_call x4, Pallas kernels, body(): pl.pallas_call(functools.partial(chunk_kernel, chunk, heads, span_rows, c...  12 us
    ppermute x4, starting transfers between devices, from_behind(): lax.ppermute(shard, axis, [(i, (i + by) % length) for i in range(length)])  9.91 us
    ppermute x9, starting transfers between devices, with_partner(): return lax.ppermute(shard, axis, [(i, i ^ step) for i in range(length)])  7.33 us
    ppermute x9, waiting for transfers between devices, with_partner(): return lax.ppermute(shard, axis, [(i, i ^ step) for i in range(length)])  2.66 us
    ppermute x4, waiting for transfers between devices, from_behind(): lax.ppermute(shard, axis, [(i, (i + by) % length) for i in range(length)])  2.59 us
  transfers between devices with their start and end apart: 13, of which 3 were waited for; matrix products, arithmetic and copies ran while one was open for 0% of the time, Pallas kernels for 15%

profile of v3, /device:TPU:0, one launch (start us, length us, event | category | flops | bytes accessed | tf_op | source)
XLA Modules:
  0.0 77.6 jit_solution(11703287089916781681)
XLA Ops:
  0.7 38.2 %shard_map.94 = (s32[8]{0:T(128)}, bf16[256,256]{1,0:T(8,128)(2,1)}, bf16[64,16,128]{2,1,0:T(8,128)(2,1)}, bf16[64,16,128]{2,1,0:T(8,128)(2,1)}, bf16[64,16,128]...) custom-call(s32[8]{0:T(128)} %starts_in_ref.1, bf16[256,16,128]{2,1,0:T(8,128)(2,1)} %bitcast.27, bf16[256,128]{1,0:T(8,128)(2,1)} %bitcast.28, ...), custom_call_target="tpu_custom_call" | custom-call | bytes 2097152 | tf_op jit(solution)/shard_map/pallas_call | solution.py:54
  38.9 3.0 %collective-permute-start.1 = (bf16[256,256]{1,0:T(8,128)(2,1)}, bf16[256,256]{1,0:T(8,128)(2,1)S(1)}, u32[]{:S(2)}, u32[]{:S(2)}) collective-permute-start(bf16[256,256]{1,0:T(8,128)(2,1)} %get-tuple-element.33.refs_0_), channel_id=1, source_target_pairs={{0,2},{1,3},{2,0},{3,1},{4,6},{5,7},{6,4},{7,5},{8,10},{9,11},{10,... | collective-permute-start | bytes 393224 | tf_op jit(solution)/shard_map/ppermute | solution.py:29
  41.9 4.5 %collective-permute-start.4 = (bf16[64,16,128]{2,1,0:T(8,128)(2,1)}, bf16[64,16,128]{2,1,0:T(8,128)(2,1)S(1)}, u32[]{:S(2)}, u32[]{:S(2)}) collective-permute-start(bf16[64,16,128]{2,1,0:T(8,128)(2,1)} %get-tuple-element.37), channel_id=1, source_target_pairs={{0,28},{4,0},{8,4},{12,8},{16,12},{20,16},{24,20},{28,24},{1,29},{... | collective-permute-start | bytes 786440 | tf_op jit(solution)/shard_map/ppermute | solution.py:24
  46.4 0.0 collective-permute-start.2
  46.4 0.0 collective-permute-done.1.refs_1_
  46.4 0.5 collective-permute-start.3
  46.9 3.4 %collective-permute-start = (bf16[64,16,128]{2,1,0:T(8,128)(2,1)}, bf16[64,16,128]{2,1,0:T(8,128)(2,1)S(1)}, u32[]{:S(2)}, u32[]{:S(2)}) collective-permute-start(bf16[64,16,128]{2,1,0:T(8,128)(2,1)} %get-tuple-element.32), channel_id=1, source_target_pairs={{0,28},{4,0},{8,4},{12,8},{16,12},{20,16},{24,20},{28,24},{1,29},{... | collective-permute-start | bytes 786440 | tf_op jit(solution)/shard_map/ppermute | solution.py:24
  50.4 0.5 collective-permute-start.8
  50.9 0.1 copy.11
  51.0 0.1 reshape.33.lse_ref
  51.1 0.0 collective-permute-done.2.refs_2_
  51.1 0.0 copy-start.3
  51.1 1.4 %collective-permute-start.9 = (bf16[64,16,128]{2,1,0:T(8,128)(2,1)}, bf16[64,16,128]{2,1,0:T(8,128)(2,1)S(1)}, u32[]{:S(2)}, u32[]{:S(2)}) collective-permute-start(bf16[64,16,128]{2,1,0:T(8,128)(2,1)} %get-tuple-element.48), channel_id=1, source_target_pairs={{0,28},{4,0},{8,4},{12,8},{16,12},{20,16},{24,20},{28,24},{1,29},{... | collective-permute-start | bytes 786440 | tf_op jit(solution)/shard_map/ppermute | solution.py:24
  52.6 0.8 %shard_map.95 = (bf16[1024,128]{1,0:T(8,128)(2,1)S(1)}, bf16[1024,256]{1,0:T(8,128)(2,1)S(1)}, bf16[128,1024]{1,0:T(8,128)(2,1)S(1)}) custom-call(s32[8]{0:T(128)S(1)} %copy-done.3, bf16[256,256]{1,0:T(8,128)(2,1)S(1)} %copy-done.2, bf16[256,256]{1,0:T(8,128)(2,1)S(1)} %collective-permute-done.1.refs_1_, ...), custom_call_target="tpu_custom_call" | custom-call | tf_op jit(solution)/shard_map/pallas_call | solution.py:93
  53.4 0.0 collective-permute-done.4
  53.4 0.0 copy-start.1
  53.4 1.2 %copy-done.1 = bf16[1,256,16,128]{3,2,1,0:T(8,128)(2,1)S(1)} copy-done((bf16[1,256,16,128]{3,2,1,0:T(8,128)(2,1)S(1)}, bf16[1,256,16,128]{3,2,1,0:T(8,128)(2,1)}, u32[]{:S(2)}) %copy-start.1) | copy-done | bytes 1048600
  54.6 4.0 %shard_map.96 = (f32[128,1024]{1,0:T(8,128)S(1)}, f32[1024,256]{1,0:T(8,128)S(1)}) custom-call(s32[8]{0:T(128)S(1)} %copy-done.3, bf16[4096,128]{1,0:T(8,128)(2,1)S(1)} %bitcast.15, bf16[1024,128]{1,0:T(8,128)(2,1)S(1)} %bitcast.25, bf16[4096,128]{1,0:T(8,128)(2,1)S(1)} %bitcast.19, f32[1,4096]{1,0:T(1,128)S(1)} %reshape.33.lse_ref, ...), custom_call_target="tpu_custom_call" | custom-call | flops 2013265920 | bytes 2097152 | tf_op jit(solution)/shard_map/pallas_call | solution.py:282
  58.7 0.0 collective-permute-done
  58.7 4.1 %shard_map.97 = (f32[128,1024]{1,0:T(8,128)S(1)}, f32[1024,256]{1,0:T(8,128)S(1)}, f32[128,256]{1,0:T(8,128)S(1)}, bf16[128,256]{1,0:T(8,128)(2,1)S(1)}, bf16[12...) custom-call(s32[8]{0:T(128)S(1)} %copy-done.3, bf16[4096,128]{1,0:T(8,128)(2,1)S(1)} %bitcast.16, ...), custom_call_target="tpu_custom_call" | custom-call | flops 2013265920 | bytes 2097152 | tf_op jit(solution)/shard_map/pallas_call | solution.py:282
  62.7 0.1 collective-permute-start.5
  62.8 0.1 collective-permute-start.6
  62.9 1.8 %collective-permute-start.7 = (bf16[128,256]{1,0:T(8,128)(2,1)S(1)}, bf16[128,256]{1,0:T(8,128)(2,1)S(1)}, u32[]{:S(2)}, u32[]{:S(2)}) collective-permute-start(bf16[128,256]{1,0:T(8,128)(2,1)S(1)} %get-tuple-element.42), channel_id=1, source_target_pairs={{0,3},{1,2},{2,1},{3,0},{4,7},{5,6},{6,5},{7,4},{8,11},{9,10},{10,... | collective-permute-start | bytes 196616 | tf_op jit(solution)/shard_map/ppermute | solution.py:29
  64.7 1.6 %shard_map.98 = (f32[128,1024]{1,0:T(8,128)S(1)}, f32[512,256]{1,0:T(8,128)S(1)}) custom-call(s32[8]{0:T(128)S(1)} %copy-done.3, bf16[4096,128]{1,0:T(8,128)(2,1)S(1)} %bitcast.17, bf16[1024,128]{1,0:T(8,128)(2,1)S(1)} %bitcast.24, bf16[4096,128]{1,0:T(8,128)(2,1)S(1)} %bitcast.21, f32[1,4096]{1,0:T(1,128)S(1)} %reshape.33.lse_ref, ...), custom_call_target="tpu_custom_call" | custom-call | flops 671088640 | bytes 2097152 | tf_op jit(solution)/shard_map/pallas_call | solution.py:282
  66.3 2.6 %collective-permute-done.9 = bf16[64,16,128]{2,1,0:T(8,128)(2,1)S(1)} collective-permute-done((bf16[64,16,128]{2,1,0:T(8,128)(2,1)}, bf16[64,16,128]{2,1,0:T(8,128)(2,1)S(1)}, u32[]{:S(2)}, u32[]{:S(2)}) %collective-permute-start.9) | collective-permute-done | bytes 262176 | tf_op jit(solution)/shard_map/ppermute | solution.py:24
  68.9 2.3 %shard_map.99 = (f32[128,1024]{1,0:T(8,128)S(1)}, f32[512,256]{1,0:T(8,128)}, f32[128,256]{1,0:T(8,128)S(1)}, bf16[128,256]{1,0:T(8,128)(2,1)S(1)}, bf16[128,256...) custom-call(s32[8]{0:T(128)S(1)} %copy-done.3, bf16[4096,128]{1,0:T(8,128)(2,1)S(1)} %bitcast.18, ...), custom_call_target="tpu_custom_call" | custom-call | flops 671088640 | bytes 2097152 | tf_op jit(solution)/shard_map/pallas_call | solution.py:282
  71.2 1.6 %collective-permute-start.11 = (bf16[128,256]{1,0:T(8,128)(2,1)S(1)}, bf16[128,256]{1,0:T(8,128)(2,1)S(1)}, u32[]{:S(2)}, u32[]{:S(2)}) collective-permute-start(bf16[128,256]{1,0:T(8,128)(2,1)S(1)} %get-tuple-element.54), channel_id=1, source_target_pairs={{0,2},{1,3},{2,0},{3,1},{4,6},{5,7},{6,4},{7,5},{8,10},{9,11},{10,... | collective-permute-start | bytes 196616 | tf_op jit(solution)/shard_map/ppermute | solution.py:29
  72.8 0.3 collective-permute-start.12
  73.1 1.1 %shard_map.100 = (bf16[128,256]{1,0:T(8,128)(2,1)S(1)}, bf16[4096,128]{1,0:T(8,128)(2,1)}) custom-call(f32[128,256]{1,0:T(8,128)S(1)} %get-tuple-element.39.refs_0_, bf16[128,256]{1,0:T(8,128)(2,1)S(1)} %collective-permute-done.5.refs_1_, bf16[128,256]{1,0:T(8,128)(2,1)S(1)} %collective-permute-done.6.refs_2_, ...), custom_call_target="tpu_custom_call" | custom-call | tf_op jit(solution)/shard_map/pallas_call | solution.py:216
  74.2 1.5 %collective-permute-done.11.refs_2_ = bf16[128,256]{1,0:T(8,128)(2,1)S(1)} collective-permute-done((bf16[128,256]{1,0:T(8,128)(2,1)S(1)}, bf16[128,256]{1,0:T(8,128)(2,1)S(1)}, u32[]{:S(2)}, u32[]{:S(2)}) %collective-permute-start.11) | collective-permute-done | bytes 65568 | tf_op jit(solution)/shard_map/ppermute | solution.py:29
  75.7 1.2 %collective-permute-done.12.refs_3_ = bf16[128,256]{1,0:T(8,128)(2,1)S(1)} collective-permute-done((bf16[128,256]{1,0:T(8,128)(2,1)S(1)}, bf16[128,256]{1,0:T(8,128)(2,1)S(1)}, u32[]{:S(2)}, u32[]{:S(2)}) %collective-permute-start.12) | collective-permute-done | bytes 65568 | tf_op jit(solution)/shard_map/ppermute | solution.py:29
  76.9 0.7 shard_map.101
  (14 shorter events, 0.0 us)
Async XLA Ops:
  0.6 52.7 %copy-start = (bf16[1,256,16,128]{3,2,1,0:T(8,128)(2,1)S(1)}, bf16[1,256,16,128]{3,2,1,0:T(8,128)(2,1)}, u32[]{:S(2)}) copy-start(bf16[1,256,16,128]{3,2,1,0:T(8,128)(2,1)} %param.7) | copy-start | bytes 3145732
  0.6 50.2 %copy-start.4 = (f32[1,16,256]{2,1,0:T(8,128)S(1)}, f32[1,16,256]{2,1,0:T(8,128)}, u32[]{:S(2)}) copy-start(f32[1,16,256]{2,1,0:T(8,128)} %param.12) | copy-start | bytes 49156
  38.9 7.6 %collective-permute-start.1 = (bf16[256,256]{1,0:T(8,128)(2,1)}, bf16[256,256]{1,0:T(8,128)(2,1)S(1)}, u32[]{:S(2)}, u32[]{:S(2)}) collective-permute-start(bf16[256,256]{1,0:T(8,128)(2,1)} %get-tuple-element.33.refs_0_), channel_id=1, source_target_pairs={{0,2},{1,3},{2,0},{3,1},{4,6},{5,7},{6,4},{7,5},{8,10},{9,11},{10,... | collective-permute-start | bytes 393224 | tf_op jit(solution)/shard_map/ppermute | solution.py:29
  41.9 11.5 %collective-permute-start.4 = (bf16[64,16,128]{2,1,0:T(8,128)(2,1)}, bf16[64,16,128]{2,1,0:T(8,128)(2,1)S(1)}, u32[]{:S(2)}, u32[]{:S(2)}) collective-permute-start(bf16[64,16,128]{2,1,0:T(8,128)(2,1)} %get-tuple-element.37), channel_id=1, source_target_pairs={{0,28},{4,0},{8,4},{12,8},{16,12},{20,16},{24,20},{28,24},{1,29},{... | collective-permute-start | bytes 786440 | tf_op jit(solution)/shard_map/ppermute | solution.py:24
  46.4 4.7 %collective-permute-start.2 = (bf16[256,256]{1,0:T(8,128)(2,1)}, bf16[256,256]{1,0:T(8,128)(2,1)S(1)}, u32[]{:S(2)}, u32[]{:S(2)}) collective-permute-start(bf16[256,256]{1,0:T(8,128)(2,1)} %get-tuple-element.33.refs_0_), channel_id=1, source_target_pairs={{0,1},{1,0},{2,3},{3,2},{4,5},{5,4},{6,7},{7,6},{8,9},{9,8},{10,11... | collective-permute-start | bytes 393224 | tf_op jit(solution)/shard_map/ppermute | solution.py:29
  46.4 6.1 %collective-permute-start.3 = (bf16[256,256]{1,0:T(8,128)(2,1)S(1)}, bf16[256,256]{1,0:T(8,128)(2,1)S(1)}, u32[]{:S(2)}, u32[]{:S(2)}) collective-permute-start(bf16[256,256]{1,0:T(8,128)(2,1)S(1)} %collective-permute-done.1.refs_1_), channel_id=1, source_target_pairs={{0,1},{1,0},{2,3},{3,2},{4,5},{5,4},{6,7},{7,6},{8,9},{9,8},{10,11... | collective-permute-start | bytes 393224 | tf_op jit(solution)/shard_map/ppermute | solution.py:29
  46.9 11.7 %collective-permute-start = (bf16[64,16,128]{2,1,0:T(8,128)(2,1)}, bf16[64,16,128]{2,1,0:T(8,128)(2,1)S(1)}, u32[]{:S(2)}, u32[]{:S(2)}) collective-permute-start(bf16[64,16,128]{2,1,0:T(8,128)(2,1)} %get-tuple-element.32), channel_id=1, source_target_pairs={{0,28},{4,0},{8,4},{12,8},{16,12},{20,16},{24,20},{28,24},{1,29},{... | collective-permute-start | bytes 786440 | tf_op jit(solution)/shard_map/ppermute | solution.py:24
  50.4 14.3 %collective-permute-start.8 = (bf16[64,16,128]{2,1,0:T(8,128)(2,1)}, bf16[64,16,128]{2,1,0:T(8,128)(2,1)S(1)}, u32[]{:S(2)}, u32[]{:S(2)}) collective-permute-start(bf16[64,16,128]{2,1,0:T(8,128)(2,1)} %get-tuple-element.45), channel_id=1, source_target_pairs={{0,28},{4,0},{8,4},{12,8},{16,12},{20,16},{24,20},{28,24},{1,29},{... | collective-permute-start | bytes 786440 | tf_op jit(solution)/shard_map/ppermute | solution.py:24
  50.9 1.7 %copy-start.2 = (bf16[256,256]{1,0:T(8,128)(2,1)S(1)}, bf16[256,256]{1,0:T(8,128)(2,1)}, u32[]{:S(2)}) copy-start(bf16[256,256]{1,0:T(8,128)(2,1)} %get-tuple-element.33.refs_0_) | copy-start | bytes 393220
  51.1 1.4 %copy-start.3 = (s32[8]{0:T(128)S(1)}, s32[8]{0:T(128)}, u32[]{:S(2)}) copy-start(s32[8]{0:T(128)} %get-tuple-element.31.starts_ref) | copy-start | bytes 100
  51.1 17.7 %collective-permute-start.9 = (bf16[64,16,128]{2,1,0:T(8,128)(2,1)}, bf16[64,16,128]{2,1,0:T(8,128)(2,1)S(1)}, u32[]{:S(2)}, u32[]{:S(2)}) collective-permute-start(bf16[64,16,128]{2,1,0:T(8,128)(2,1)} %get-tuple-element.48), channel_id=1, source_target_pairs={{0,28},{4,0},{8,4},{12,8},{16,12},{20,16},{24,20},{28,24},{1,29},{... | collective-permute-start | bytes 786440 | tf_op jit(solution)/shard_map/ppermute | solution.py:24
  53.4 1.2 %copy-start.1 = (bf16[1,256,16,128]{3,2,1,0:T(8,128)(2,1)S(1)}, bf16[1,256,16,128]{3,2,1,0:T(8,128)(2,1)}, u32[]{:S(2)}) copy-start(bf16[1,256,16,128]{3,2,1,0:T(8,128)(2,1)} %param.10) | copy-start | bytes 3145732
  62.7 6.1 %collective-permute-start.5 = (bf16[128,256]{1,0:T(8,128)(2,1)S(1)}, bf16[128,256]{1,0:T(8,128)(2,1)S(1)}, u32[]{:S(2)}, u32[]{:S(2)}) collective-permute-start(bf16[128,256]{1,0:T(8,128)(2,1)S(1)} %get-tuple-element.40), channel_id=1, source_target_pairs={{0,1},{1,0},{2,3},{3,2},{4,5},{5,4},{6,7},{7,6},{8,9},{9,8},{10,11... | collective-permute-start | bytes 196616 | tf_op jit(solution)/shard_map/ppermute | solution.py:29
  62.8 6.1 %collective-permute-start.6 = (bf16[128,256]{1,0:T(8,128)(2,1)S(1)}, bf16[128,256]{1,0:T(8,128)(2,1)S(1)}, u32[]{:S(2)}, u32[]{:S(2)}) collective-permute-start(bf16[128,256]{1,0:T(8,128)(2,1)S(1)} %get-tuple-element.41), channel_id=1, source_target_pairs={{0,2},{1,3},{2,0},{3,1},{4,6},{5,7},{6,4},{7,5},{8,10},{9,11},{10,... | collective-permute-start | bytes 196616 | tf_op jit(solution)/shard_map/ppermute | solution.py:29
  62.9 6.0 %collective-permute-start.7 = (bf16[128,256]{1,0:T(8,128)(2,1)S(1)}, bf16[128,256]{1,0:T(8,128)(2,1)S(1)}, u32[]{:S(2)}, u32[]{:S(2)}) collective-permute-start(bf16[128,256]{1,0:T(8,128)(2,1)S(1)} %get-tuple-element.42), channel_id=1, source_target_pairs={{0,3},{1,2},{2,1},{3,0},{4,7},{5,6},{6,5},{7,4},{8,11},{9,10},{10,... | collective-permute-start | bytes 196616 | tf_op jit(solution)/shard_map/ppermute | solution.py:29
  71.2 3.0 %collective-permute-start.10 = (bf16[128,256]{1,0:T(8,128)(2,1)S(1)}, bf16[128,256]{1,0:T(8,128)(2,1)S(1)}, u32[]{:S(2)}, u32[]{:S(2)}) collective-permute-start(bf16[128,256]{1,0:T(8,128)(2,1)S(1)} %get-tuple-element.53), channel_id=1, source_target_pairs={{0,1},{1,0},{2,3},{3,2},{4,5},{5,4},{6,7},{7,6},{8,9},{9,8},{10,11... | collective-permute-start | bytes 196616 | tf_op jit(solution)/shard_map/ppermute | solution.py:29
  71.2 4.5 %collective-permute-start.11 = (bf16[128,256]{1,0:T(8,128)(2,1)S(1)}, bf16[128,256]{1,0:T(8,128)(2,1)S(1)}, u32[]{:S(2)}, u32[]{:S(2)}) collective-permute-start(bf16[128,256]{1,0:T(8,128)(2,1)S(1)} %get-tuple-element.54), channel_id=1, source_target_pairs={{0,2},{1,3},{2,0},{3,1},{4,6},{5,7},{6,4},{7,5},{8,10},{9,11},{10,... | collective-permute-start | bytes 196616 | tf_op jit(solution)/shard_map/ppermute | solution.py:29
  72.8 4.1 %collective-permute-start.12 = (bf16[128,256]{1,0:T(8,128)(2,1)S(1)}, bf16[128,256]{1,0:T(8,128)(2,1)S(1)}, u32[]{:S(2)}, u32[]{:S(2)}) collective-permute-start(bf16[128,256]{1,0:T(8,128)(2,1)S(1)} %get-tuple-element.55), channel_id=1, source_target_pairs={{0,3},{1,2},{2,1},{3,0},{4,7},{5,6},{6,5},{7,4},{8,11},{9,10},{10,... | collective-permute-start | bytes 196616 | tf_op jit(solution)/shard_map/ppermute | solution.py:29

commit v4 on v3

--- a/solution.py
+++ b/solution.py
@@ -11,7 +11,6 @@
 KEY_BLOCK = 256
 CHUNK_TOKENS = 64
 VMEM_LIMIT = 40 * 1024 * 1024
-CUT_LIMIT = 60 * 1024 * 1024
 
 WHOLE = pl.BlockSpec(memory_space=pltpu.VMEM)
 SCALARS = pl.BlockSpec(memory_space=pltpu.SMEM)
@@ -31,41 +30,6 @@
 
 def params(limit=VMEM_LIMIT):
     return pltpu.CompilerParams(vmem_limit_bytes=limit)
-
-
-def cut_kernel(cuts, starts_in_ref, source_ref, keys_ref, values_ref, *refs):
-    starts_ref, pair_ref, *out_refs, sems = refs
-    head_size = keys_ref.shape[1]
-    moves = [(keys_ref, pair_ref.at[:, pl.ds(0, head_size)])]
-    moves.append((values_ref, pair_ref.at[:, pl.ds(head_size, head_size)]))
-    for (first, size), out_ref in zip(cuts, out_refs):
-        moves.append((source_ref.at[pl.ds(first, size)], out_ref))
-    copies = [pltpu.make_async_copy(*move, sems.at[i]) for i, move in enumerate(moves)]
-    for copy in copies:
-        copy.start()
-    for span in range(starts_ref.shape[0]):
-        starts_ref[span] = starts_in_ref[span]
-    for copy in copies:
-        copy.wait()
-
-
-def cut(span_start, source, keys, values, cuts):
-    row_count, head_size = keys.shape
-    return pl.pallas_call(
-        functools.partial(cut_kernel, cuts),
-        out_shape=[
-            jax.ShapeDtypeStruct(span_start.shape, span_start.dtype),
-            jax.ShapeDtypeStruct((row_count, 2 * head_size), keys.dtype),
-        ]
-        + [jax.ShapeDtypeStruct((size, *source.shape[1:]), source.dtype) for _, size in cuts],
-        in_specs=[SCALARS] + [ANYWHERE] * 3,
-        out_specs=[SCALARS] + [ANYWHERE] * (len(cuts) + 1),
-        scratch_shapes=[pltpu.SemaphoreType.DMA((len(cuts) + 2,))],
-        compiler_params=params(CUT_LIMIT),
-        cost_estimate=pl.CostEstimate(
-            flops=0, bytes_accessed=2 * source.size * source.dtype.itemsize, transcendentals=0
-        ),
-    )(span_start, source, keys, values)
 
 
 def sort_keys_kernel(codes, span_rows, head_size, starts_ref, *refs):
@@ -81,10 +45,11 @@
         for half in range(2):
             start = pl.multiple_of(starts_ref[2 * owner + half], span_rows)
             rows = pl.ds(start, span_rows)
-            part = block[half * span_rows : (half + 1) * span_rows, :]
-            keys_ref[rows, :] = part[:, :head_size]
-            values_ref[rows, :head_size] = part[:, head_size:]
-            keys_t_ref[:, rows] = part[:, :head_size].astype(jnp.float32).T.astype(jnp.bfloat16)
+            part = slice(half * span_rows, (half + 1) * span_rows)
+            keys = block[0, part, :]
+            keys_ref[rows, :] = keys
+            values_ref[rows, :head_size] = block[1, part, :]
+            keys_t_ref[:, rows] = keys.astype(jnp.float32).T.astype(jnp.bfloat16)
 
 
 def sort_keys(span_start, blocks, codes, span_rows, head_size):
@@ -171,12 +136,13 @@
 
 
 def chunk_kernel(
-    chunk, heads, span_rows, count, is_first, hands_out, n_after, starts_ref, q_ref, g_ref, o_ref,
+    chunk, heads, span_rows, count, is_first, is_last, hands_out, n_after, starts_ref, q_ref, g_ref, o_ref,
     lse_ref, keys_ref, values_ref, keys_t_ref, *refs,
 ):
     refs = list(refs[n_after:])
     total_in = None if is_first else refs.pop(0)
-    dq_ref, total_ref, *handed = refs
+    total_ref = refs.pop() if is_last else refs.pop(1)
+    dq_ref, *handed = refs
     if is_first:
         total_ref[...] = jnp.zeros_like(total_ref)
     else:
@@ -239,19 +205,20 @@
     ]
     per_half = len(chunks) // 2
 
-    starts, pair, *pieces = cut(
-        span_start, grad_held[0], keys[0], values[0],
-        [(half * span_rows + first, size) for half, first, size in chunks],
-    )
+    cuts = [half * span_rows + first for half, first, _ in chunks]
+    pieces = [grad_held[0, cuts[0] : cuts[0] + CHUNK_TOKENS]]
+    pieces[0], rest = lax.optimization_barrier((pieces[0], grad_held[0]))
+    pieces += [rest[at : at + CHUNK_TOKENS] for at in cuts[1:]]
     grads = [from_behind(piece, "section", -1) for piece in pieces]
 
+    pair = jnp.concatenate([keys, values], axis=0)
     blocks, codes = [pair], [0]
     step = count // 2
     while step:
         blocks = blocks + [with_partner(block, "ctx", step) for block in blocks]
         codes = codes + [code ^ step for code in codes]
         step //= 2
-    sorted_keys = sort_keys(starts, blocks, codes, span_rows, head_size)
+    sorted_keys = sort_keys(span_start, blocks, codes, span_rows, head_size)
 
     q_flat = queries.reshape(row_count * heads, head_size)
     o_flat = outputs.reshape(row_count * heads, head_size)
@@ -262,37 +229,39 @@
     for number, chunk in enumerate(chunks):
         half, _, tokens = chunk
         rows = tokens * heads
-        is_first = number == 0
+        is_first, is_last = number == 0, number == len(chunks) - 1
         hands_out = number % per_half == per_half - 1
-        after = received if number == len(chunks) - 1 else []
+        after = received if is_last else []
         if after:
             upper_terms = received
         operands = [
             q_flat, grads[number].reshape(rows, head_size), o_flat, lse_flat, *sorted_keys, *after,
             *running,
         ]
-        out_shape = [
-            jax.ShapeDtypeStruct((head_size, rows), jnp.float32),
-            jax.ShapeDtypeStruct((total if half else total // 2, 2 * head_size), jnp.float32),
-        ]
+        total_shape = (total if half else total // 2, 2 * head_size)
+        out_shape = [jax.ShapeDtypeStruct((head_size, rows), jnp.float32)]
+        if not is_last:
+            out_shape.append(jax.ShapeDtypeStruct(total_shape, jnp.float32))
         if hands_out:
             out_shape.append(jax.ShapeDtypeStruct(span_wide, jnp.float32))
             out_shape += [jax.ShapeDtypeStruct(span_wide, jnp.bfloat16)] * (count - 1)
         pairs = rows * (3 * total // 4 if half == 1 else total // 4)
-        dq, running_total, *handed = pl.pallas_call(
+        dq, *handed = pl.pallas_call(
             functools.partial(
-                chunk_kernel, chunk, heads, span_rows, count, is_first, hands_out, len(after)
+                chunk_kernel, chunk, heads, span_rows, count, is_first, is_last, hands_out,
+                len(after),
             ),
             out_shape=out_shape,
             in_specs=[SCALARS] + [WHOLE] * len(operands),
             out_specs=[WHOLE] * len(out_shape),
+            scratch_shapes=[pltpu.VMEM(total_shape, jnp.float32)] if is_last else [],
             compiler_params=params(),
             cost_estimate=pl.CostEstimate(
                 flops=20 * pairs * head_size, bytes_accessed=2 * 2**20, transcendentals=pairs
             ),
-        )(starts, *operands)
+        )(span_start, *operands)
         dq_parts.append(dq)
-        running = [running_total]
+        running = [] if is_last else [handed.pop(0)]
         if hands_out:
             received = [handed[0]] + [
                 with_partner(send, "ctx", step) for step, send in enumerate(handed[1:], start=1)

time: 78.1 us -> 45.2 us (0.58)
  Pallas kernels: 52.8 us -> 13.8 us
  local copies, waits for them, and re-layouts: 1.45 us -> 6.37 us
  waiting for transfers between devices: 5.25 us -> 6.52 us
    pallas_call x1 -> x0, Pallas kernels: 38.2 us -> none  [cut(): pl.pallas_call(functools.partial(cut_kernel, cuts), out_shape=[jax.ShapeD...]
    slice x0 -> x1, local copies, waits for them, and re-layouts: none -> 2.01 us  [body(): pieces += [rest[at:at + CHUNK_TOKENS] for at in cuts[1:]]]
    squeeze x0 -> x1, local copies, waits for them, and re-layouts: none -> 1.68 us  [body(): pieces = [grad_held[0, cuts[0]:cuts[0] + CHUNK_TOKENS]]]
    ppermute x4, waiting for transfers between devices: 2.59 us -> 4.06 us  [from_behind(): lax.ppermute(shard, axis, [(i, (i + by) % length) for i in range(length)])]
    ppermute x9, starting transfers between devices: 7.33 us -> 8.35 us  [with_partner(): return lax.ppermute(shard, axis, [(i, i ^ step) for i in range(length)])]
    reshape x1, local copies, waits for them, and re-layouts: 0.11 us -> 1.01 us  [body(): lse_flat = lse[0].T.reshape(1, row_count * heads)]
    pallas_call x4, Pallas kernels: 12 us -> 11.2 us  [body(): pl.pallas_call(functools.partial(chunk_kernel, chunk, heads, span_rows, c...]
    ppermute x4, starting transfers between devices: 9.91 us -> 9.12 us  [from_behind(): lax.ppermute(shard, axis, [(i, (i + by) % length) for i in range(length)])]
  transfers between devices with their start and end apart: 13 -> 13, of which waited for: 3 -> 3; matrix products, arithmetic and copies ran while one was open for 0% -> 12% of each run, Pallas kernels for 15% -> 24%
where the time goes in v4:
time: 45.2 us; the launch traced here: 45 us
  starting transfers between devices  17.5 us (39%)
  Pallas kernels  13.8 us (31%)
  waiting for transfers between devices  6.52 us (14%)
  local copies, waits for them, and re-layouts  6.37 us (14%)
  between operations  0.81 us (2%)
    pallas_call x4, Pallas kernels, body(): pl.pallas_call(functools.partial(chunk_kernel, chunk, heads, span_rows, c...  11.2 us
    ppermute x4, starting transfers between devices, from_behind(): lax.ppermute(shard, axis, [(i, (i + by) % length) for i in range(length)])  9.12 us
    ppermute x9, starting transfers between devices, with_partner(): return lax.ppermute(shard, axis, [(i, i ^ step) for i in range(length)])  8.35 us
    ppermute x4, waiting for transfers between devices, from_behind(): lax.ppermute(shard, axis, [(i, (i + by) % length) for i in range(length)])  4.06 us
    ppermute x9, waiting for transfers between devices, with_partner(): return lax.ppermute(shard, axis, [(i, i ^ step) for i in range(length)])  2.46 us
    slice x1, local copies, waits for them, and re-layouts, body(): pieces += [rest[at:at + CHUNK_TOKENS] for at in cuts[1:]]  2.01 us
    squeeze x1, local copies, waits for them, and re-layouts, body(): pieces = [grad_held[0, cuts[0]:cuts[0] + CHUNK_TOKENS]]  1.68 us
    pallas_call x1, Pallas kernels, finish(): pl.pallas_call(functools.partial(finish_kernel, len(terms), places), out_...  1.13 us
  transfers between devices with their start and end apart: 13, of which 3 were waited for; matrix products, arithmetic and copies ran while one was open for 12% of the time, Pallas kernels for 24%

profile of v4, /device:TPU:0, one launch (start us, length us, event | category | flops | bytes accessed | tf_op | source)
XLA Modules:
  0.0 45.0 jit_solution(5418661390815263792)
XLA Ops:
  0.6 0.9 %constant_dynamic-update-slice_fusion.1 = bf16[2,256,128]{2,1,0:T(8,128)(2,1)S(1)} fusion(bf16[1,256,128]{2,1,0:T(8,128)(2,1)} %param.8), kind=kLoop, calls=%fused_computation.2 | loop fusion | bytes 131072
  1.5 0.5 %collective-permute-start.2 = (bf16[2,256,128]{2,1,0:T(8,128)(2,1)S(1)}, bf16[2,256,128]{2,1,0:T(8,128)(2,1)S(1)}, u32[]{:S(2)}, u32[]{:S(2)}) collective-permute-start(bf16[2,256,128]{2,1,0:T(8,128)(2,1)S(1)} %constant_dynamic-update-slice_fusion.refs_0_), channel_id=1, source_target_pairs={{0,1},{1,0},{2,3},{3,2},{4,5},{5,4},{6,7},{7,6},{8,9},{9,8},{10,11... | collective-permute-start | bytes 393224 | tf_op jit(solution)/shard_map/ppermute | solution.py:28
  2.1 2.6 %collective-permute-start.1 = (bf16[2,256,128]{2,1,0:T(8,128)(2,1)S(1)}, bf16[2,256,128]{2,1,0:T(8,128)(2,1)S(1)}, u32[]{:S(2)}, u32[]{:S(2)}) collective-permute-start(bf16[2,256,128]{2,1,0:T(8,128)(2,1)S(1)} %constant_dynamic-update-slice_fusion.refs_0_), channel_id=1, source_target_pairs={{0,2},{1,3},{2,0},{3,1},{4,6},{5,7},{6,4},{7,5},{8,10},{9,11},{10,... | collective-permute-start | bytes 393224 | tf_op jit(solution)/shard_map/ppermute | solution.py:28
  4.6 1.7 %slice_bitcast_fusion = bf16[64,16,128]{2,1,0:T(8,128)(2,1)} fusion(bf16[1,256,16,128]{3,2,1,0:T(8,128)(2,1)} %param.11), kind=kLoop, calls=%fused_computation | loop fusion | bytes 524288 | tf_op jit(solution)/shard_map/squeeze | solution.py:209
  6.3 4.5 %collective-permute-start.4 = (bf16[64,16,128]{2,1,0:T(8,128)(2,1)}, bf16[64,16,128]{2,1,0:T(8,128)(2,1)S(1)}, u32[]{:S(2)}, u32[]{:S(2)}) collective-permute-start(bf16[64,16,128]{2,1,0:T(8,128)(2,1)} %slice_bitcast_fusion), channel_id=1, source_target_pairs={{0,28},{4,0},{8,4},{12,8},{16,12},{20,16},{24,20},{28,24},{1,29},{... | collective-permute-start | bytes 786440 | tf_op jit(solution)/shard_map/ppermute | solution.py:23
  10.9 0.0 collective-permute-done.1.refs_1_
  10.9 2.0 %fusion = (bf16[64,16,128]{2,1,0:T(8,128)(2,1)}, bf16[64,16,128]{2,1,0:T(8,128)(2,1)}, bf16[64,16,128]{2,1,0:T(8,128)(2,1)}) fusion(bf16[256,16,128]{2,1,0:T(8,128)(2,1)} %bitcast.27), kind=kLoop, calls=%fused_computation.3 | loop fusion | bytes 1572864 | tf_op jit(solution)/shard_map/slice | solution.py:211
  12.9 2.6 %collective-permute-start = (bf16[64,16,128]{2,1,0:T(8,128)(2,1)}, bf16[64,16,128]{2,1,0:T(8,128)(2,1)S(1)}, u32[]{:S(2)}, u32[]{:S(2)}) collective-permute-start(bf16[64,16,128]{2,1,0:T(8,128)(2,1)} %get-tuple-element.53), channel_id=1, source_target_pairs={{0,28},{4,0},{8,4},{12,8},{16,12},{20,16},{24,20},{28,24},{1,29},{... | collective-permute-start | bytes 786440 | tf_op jit(solution)/shard_map/ppermute | solution.py:23
  15.5 0.5 %collective-permute-start.9 = (bf16[64,16,128]{2,1,0:T(8,128)(2,1)}, bf16[64,16,128]{2,1,0:T(8,128)(2,1)S(1)}, u32[]{:S(2)}, u32[]{:S(2)}) collective-permute-start(bf16[64,16,128]{2,1,0:T(8,128)(2,1)} %get-tuple-element.51), channel_id=1, source_target_pairs={{0,28},{4,0},{8,4},{12,8},{16,12},{20,16},{24,20},{28,24},{1,29},{... | collective-permute-start | bytes 786440 | tf_op jit(solution)/shard_map/ppermute | solution.py:23
  16.1 0.8 %copy.11 = f32[256,16]{1,0:T(8,128)} copy(f32[256,16]{0,1:T(8,128)S(1)} %bitcast.28) | data formatting | bytes 32768 | tf_op jit(solution)/shard_map/transpose | solution.py:225
  16.8 1.0 %reshape.33.lse_ref = f32[1,4096]{1,0:T(1,128)S(1)} reshape(f32[256,16]{1,0:T(8,128)} %copy.11) | data formatting | bytes 32768 | tf_op jit(solution)/shard_map/reshape | solution.py:225
  17.8 0.0 collective-permute-done.2.refs_2_
  17.8 1.4 %collective-permute-start.8 = (bf16[64,16,128]{2,1,0:T(8,128)(2,1)}, bf16[64,16,128]{2,1,0:T(8,128)(2,1)S(1)}, u32[]{:S(2)}, u32[]{:S(2)}) collective-permute-start(bf16[64,16,128]{2,1,0:T(8,128)(2,1)} %get-tuple-element.52), channel_id=1, source_target_pairs={{0,28},{4,0},{8,4},{12,8},{16,12},{20,16},{24,20},{28,24},{1,29},{... | collective-permute-start | bytes 786440 | tf_op jit(solution)/shard_map/ppermute | solution.py:23
  19.3 0.0 collective-permute-done.3.refs_3_
  19.3 0.8 %shard_map.94 = (bf16[1024,128]{1,0:T(8,128)(2,1)S(1)}, bf16[1024,256]{1,0:T(8,128)(2,1)S(1)}, bf16[128,1024]{1,0:T(8,128)(2,1)S(1)}) custom-call(s32[8]{0:T(128)S(1)} %copy-done.2, bf16[2,256,128]{2,1,0:T(8,128)(2,1)S(1)} %constant_dynamic-update-slice_fusion.refs_0_, bf16[2,256,128]{2,1,0:T(8,128)(2,1)S(1)} %collective-permute-done.1.refs_1_, ...), custom_call_target="tpu_custom_call" | custom-call | tf_op jit(solution)/shard_map/pallas_call | solution.py:58
  20.1 0.0 collective-permute-done.4
  20.1 3.2 %shard_map.95 = (f32[128,1024]{1,0:T(8,128)S(1)}, f32[1024,256]{1,0:T(8,128)S(1)}) custom-call(s32[8]{0:T(128)S(1)} %copy-done.2, bf16[4096,128]{1,0:T(8,128)(2,1)S(1)} %bitcast.15, bf16[1024,128]{1,0:T(8,128)(2,1)S(1)} %bitcast.25, bf16[4096,128]{1,0:T(8,128)(2,1)S(1)} %bitcast.19, f32[1,4096]{1,0:T(1,128)S(1)} %reshape.33.lse_ref, ...), custom_call_target="tpu_custom_call" | custom-call | flops 2013265920 | bytes 2097152 | tf_op jit(solution)/shard_map/pallas_call | solution.py:249
  23.3 3.2 %shard_map.96 = (f32[128,1024]{1,0:T(8,128)S(1)}, f32[1024,256]{1,0:T(8,128)S(1)}, f32[128,256]{1,0:T(8,128)S(1)}, bf16[128,256]{1,0:T(8,128)(2,1)S(1)}, bf16[12...) custom-call(s32[8]{0:T(128)S(1)} %copy-done.2, bf16[4096,128]{1,0:T(8,128)(2,1)S(1)} %bitcast.16, ...), custom_call_target="tpu_custom_call" | custom-call | flops 2013265920 | bytes 2097152 | tf_op jit(solution)/shard_map/pallas_call | solution.py:249
  26.6 0.1 collective-permute-start.5
  26.6 3.2 %collective-permute-start.6 = (bf16[128,256]{1,0:T(8,128)(2,1)S(1)}, bf16[128,256]{1,0:T(8,128)(2,1)S(1)}, u32[]{:S(2)}, u32[]{:S(2)}) collective-permute-start(bf16[128,256]{1,0:T(8,128)(2,1)S(1)} %get-tuple-element.35), channel_id=1, source_target_pairs={{0,2},{1,3},{2,0},{3,1},{4,6},{5,7},{6,4},{7,5},{8,10},{9,11},{10,... | collective-permute-start | bytes 196616 | tf_op jit(solution)/shard_map/ppermute | solution.py:28
  29.8 0.1 collective-permute-start.7
  29.9 4.1 %collective-permute-done.8 = bf16[64,16,128]{2,1,0:T(8,128)(2,1)S(1)} collective-permute-done((bf16[64,16,128]{2,1,0:T(8,128)(2,1)}, bf16[64,16,128]{2,1,0:T(8,128)(2,1)S(1)}, u32[]{:S(2)}, u32[]{:S(2)}) %collective-permute-start.8) | collective-permute-done | bytes 262176 | tf_op jit(solution)/shard_map/ppermute | solution.py:23
  33.9 2.4 %shard_map.97 = (f32[128,1024]{1,0:T(8,128)S(1)}, f32[512,256]{1,0:T(8,128)S(1)}) custom-call(s32[8]{0:T(128)S(1)} %copy-done.2, bf16[4096,128]{1,0:T(8,128)(2,1)S(1)} %bitcast.17, bf16[1024,128]{1,0:T(8,128)(2,1)S(1)} %bitcast.24, bf16[4096,128]{1,0:T(8,128)(2,1)S(1)} %bitcast.21, f32[1,4096]{1,0:T(1,128)S(1)} %reshape.33.lse_ref, ...), custom_call_target="tpu_custom_call" | custom-call | flops 671088640 | bytes 2097152 | tf_op jit(solution)/shard_map/pallas_call | solution.py:249
  36.3 0.0 collective-permute-done.9
  36.4 2.4 %shard_map.98 = (f32[128,1024]{1,0:T(8,128)S(1)}, f32[128,256]{1,0:T(8,128)S(1)}, bf16[128,256]{1,0:T(8,128)(2,1)S(1)}, bf16[128,256]{1,0:T(8,128)(2,1)S(1)}, bf16[128,256]{1,0:T(8,128)(2,1)S(1)}) custom-call(s32[8]{0:T(128)S(1)} %copy-done.2, bf16[4096,128]{1,0:T(8,128)(2,1)S(1)} %bitcast.18, bf16[1024,128]{1,0:T(8,128)(2,1)S(1)} %bitcast.23, ...), custom_call_target="tpu_custom_call" | custom-call | flops 671088640 | bytes 2097152 | tf_op jit(solution)/shard_map/pallas_call | solution.py:249
  38.8 0.1 collective-permute-start.10
  38.8 0.1 collective-permute-start.11
  38.9 1.8 %collective-permute-start.12 = (bf16[128,256]{1,0:T(8,128)(2,1)S(1)}, bf16[128,256]{1,0:T(8,128)(2,1)S(1)}, u32[]{:S(2)}, u32[]{:S(2)}) collective-permute-start(bf16[128,256]{1,0:T(8,128)(2,1)S(1)} %get-tuple-element.47), channel_id=1, source_target_pairs={{0,3},{1,2},{2,1},{3,0},{4,7},{5,6},{6,5},{7,4},{8,11},{9,10},{10,... | collective-permute-start | bytes 196616 | tf_op jit(solution)/shard_map/ppermute | solution.py:28
  40.7 1.1 %shard_map.99 = (bf16[128,256]{1,0:T(8,128)(2,1)S(1)}, bf16[4096,128]{1,0:T(8,128)(2,1)}) custom-call(f32[128,256]{1,0:T(8,128)S(1)} %get-tuple-element.33.refs_0_, bf16[128,256]{1,0:T(8,128)(2,1)S(1)} %collective-permute-done.5.refs_1_, bf16[128,256]{1,0:T(8,128)(2,1)S(1)} %collective-permute-done.6.refs_2_, ...), custom_call_target="tpu_custom_call" | custom-call | tf_op jit(solution)/shard_map/pallas_call | solution.py:182
  41.9 1.9 %collective-permute-done.11.refs_2_ = bf16[128,256]{1,0:T(8,128)(2,1)S(1)} collective-permute-done((bf16[128,256]{1,0:T(8,128)(2,1)S(1)}, bf16[128,256]{1,0:T(8,128)(2,1)S(1)}, u32[]{:S(2)}, u32[]{:S(2)}) %collective-permute-start.11) | collective-permute-done | bytes 65568 | tf_op jit(solution)/shard_map/ppermute | solution.py:28
  43.8 0.5 %collective-permute-done.12.refs_3_ = bf16[128,256]{1,0:T(8,128)(2,1)S(1)} collective-permute-done((bf16[128,256]{1,0:T(8,128)(2,1)S(1)}, bf16[128,256]{1,0:T(8,128)(2,1)S(1)}, u32[]{:S(2)}, u32[]{:S(2)}) %collective-permute-start.12) | collective-permute-done | bytes 65568 | tf_op jit(solution)/shard_map/ppermute | solution.py:28
  44.3 0.7 %shard_map.100 = (bf16[256,128]{1,0:T(8,128)(2,1)}, bf16[256,128]{1,0:T(8,128)(2,1)}) custom-call(f32[128,256]{1,0:T(8,128)S(1)} %get-tuple-element.44.refs_0_, bf16[128,256]{1,0:T(8,128)(2,1)S(1)} %collective-permute-done.10.refs_1_, bf16[128,256]{1,0:T(8,128)(2,1)S(1)} %collective-permute-done.11.refs_2_, ...), custom_call_target="tpu_custom_call" | custom-call | tf_op jit(solution)/shard_map/pallas_call | solution.py:272
  (17 shorter events, 0.0 us)
Async XLA Ops:
  0.6 0.9 %copy-start.3 = (bf16[1,256,128]{2,1,0:T(8,128)(2,1)S(1)}, bf16[1,256,128]{2,1,0:T(8,128)(2,1)}, u32[]{:S(2)}) copy-start(bf16[1,256,128]{2,1,0:T(8,128)(2,1)} %param.9) | copy-start | bytes 196612
  1.5 16.3 %collective-permute-start.2 = (bf16[2,256,128]{2,1,0:T(8,128)(2,1)S(1)}, bf16[2,256,128]{2,1,0:T(8,128)(2,1)S(1)}, u32[]{:S(2)}, u32[]{:S(2)}) collective-permute-start(bf16[2,256,128]{2,1,0:T(8,128)(2,1)S(1)} %constant_dynamic-update-slice_fusion.refs_0_), channel_id=1, source_target_pairs={{0,1},{1,0},{2,3},{3,2},{4,5},{5,4},{6,7},{7,6},{8,9},{9,8},{10,11... | collective-permute-start | bytes 393224 | tf_op jit(solution)/shard_map/ppermute | solution.py:28
  2.1 8.8 %collective-permute-start.1 = (bf16[2,256,128]{2,1,0:T(8,128)(2,1)S(1)}, bf16[2,256,128]{2,1,0:T(8,128)(2,1)S(1)}, u32[]{:S(2)}, u32[]{:S(2)}) collective-permute-start(bf16[2,256,128]{2,1,0:T(8,128)(2,1)S(1)} %constant_dynamic-update-slice_fusion.refs_0_), channel_id=1, source_target_pairs={{0,2},{1,3},{2,0},{3,1},{4,6},{5,7},{6,4},{7,5},{8,10},{9,11},{10,... | collective-permute-start | bytes 393224 | tf_op jit(solution)/shard_map/ppermute | solution.py:28
  4.6 11.4 %copy-start.4 = (f32[1,16,256]{2,1,0:T(8,128)S(1)}, f32[1,16,256]{2,1,0:T(8,128)}, u32[]{:S(2)}) copy-start(f32[1,16,256]{2,1,0:T(8,128)} %param.12) | copy-start | bytes 49156
  4.6 14.6 %copy-start.2 = (s32[8]{0:T(128)S(1)}, s32[8]{0:T(128)}, u32[]{:S(2)}) copy-start(s32[8]{0:T(128)} %starts_ref.9) | copy-start | bytes 100
  6.3 13.8 %copy-start = (bf16[1,256,16,128]{3,2,1,0:T(8,128)(2,1)S(1)}, bf16[1,256,16,128]{3,2,1,0:T(8,128)(2,1)}, u32[]{:S(2)}) copy-start(bf16[1,256,16,128]{3,2,1,0:T(8,128)(2,1)} %param.7) | copy-start | bytes 3145732
  6.3 13.8 %copy-start.1 = (bf16[1,256,16,128]{3,2,1,0:T(8,128)(2,1)S(1)}, bf16[1,256,16,128]{3,2,1,0:T(8,128)(2,1)}, u32[]{:S(2)}) copy-start(bf16[1,256,16,128]{3,2,1,0:T(8,128)(2,1)} %param.10) | copy-start | bytes 3145732
  6.3 13.7 %collective-permute-start.4 = (bf16[64,16,128]{2,1,0:T(8,128)(2,1)}, bf16[64,16,128]{2,1,0:T(8,128)(2,1)S(1)}, u32[]{:S(2)}, u32[]{:S(2)}) collective-permute-start(bf16[64,16,128]{2,1,0:T(8,128)(2,1)} %slice_bitcast_fusion), channel_id=1, source_target_pairs={{0,28},{4,0},{8,4},{12,8},{16,12},{20,16},{24,20},{28,24},{1,29},{... | collective-permute-start | bytes 786440 | tf_op jit(solution)/shard_map/ppermute | solution.py:23
  10.9 8.4 %collective-permute-start.3 = (bf16[2,256,128]{2,1,0:T(8,128)(2,1)S(1)}, bf16[2,256,128]{2,1,0:T(8,128)(2,1)S(1)}, u32[]{:S(2)}, u32[]{:S(2)}) collective-permute-start(bf16[2,256,128]{2,1,0:T(8,128)(2,1)S(1)} %collective-permute-done.1.refs_1_), channel_id=1, source_target_pairs={{0,1},{1,0},{2,3},{3,2},{4,5},{5,4},{6,7},{7,6},{8,9},{9,8},{10,11... | collective-permute-start | bytes 393224 | tf_op jit(solution)/shard_map/ppermute | solution.py:28
  12.9 10.4 %collective-permute-start = (bf16[64,16,128]{2,1,0:T(8,128)(2,1)}, bf16[64,16,128]{2,1,0:T(8,128)(2,1)S(1)}, u32[]{:S(2)}, u32[]{:S(2)}) collective-permute-start(bf16[64,16,128]{2,1,0:T(8,128)(2,1)} %get-tuple-element.53), channel_id=1, source_target_pairs={{0,28},{4,0},{8,4},{12,8},{16,12},{20,16},{24,20},{28,24},{1,29},{... | collective-permute-start | bytes 786440 | tf_op jit(solution)/shard_map/ppermute | solution.py:23
  15.5 20.8 %collective-permute-start.9 = (bf16[64,16,128]{2,1,0:T(8,128)(2,1)}, bf16[64,16,128]{2,1,0:T(8,128)(2,1)S(1)}, u32[]{:S(2)}, u32[]{:S(2)}) collective-permute-start(bf16[64,16,128]{2,1,0:T(8,128)(2,1)} %get-tuple-element.51), channel_id=1, source_target_pairs={{0,28},{4,0},{8,4},{12,8},{16,12},{20,16},{24,20},{28,24},{1,29},{... | collective-permute-start | bytes 786440 | tf_op jit(solution)/shard_map/ppermute | solution.py:23
  17.8 16.1 %collective-permute-start.8 = (bf16[64,16,128]{2,1,0:T(8,128)(2,1)}, bf16[64,16,128]{2,1,0:T(8,128)(2,1)S(1)}, u32[]{:S(2)}, u32[]{:S(2)}) collective-permute-start(bf16[64,16,128]{2,1,0:T(8,128)(2,1)} %get-tuple-element.52), channel_id=1, source_target_pairs={{0,28},{4,0},{8,4},{12,8},{16,12},{20,16},{24,20},{28,24},{1,29},{... | collective-permute-start | bytes 786440 | tf_op jit(solution)/shard_map/ppermute | solution.py:23
  26.6 9.8 %collective-permute-start.5 = (bf16[128,256]{1,0:T(8,128)(2,1)S(1)}, bf16[128,256]{1,0:T(8,128)(2,1)S(1)}, u32[]{:S(2)}, u32[]{:S(2)}) collective-permute-start(bf16[128,256]{1,0:T(8,128)(2,1)S(1)} %get-tuple-element.34), channel_id=1, source_target_pairs={{0,1},{1,0},{2,3},{3,2},{4,5},{5,4},{6,7},{7,6},{8,9},{9,8},{10,11... | collective-permute-start | bytes 196616 | tf_op jit(solution)/shard_map/ppermute | solution.py:28
  26.6 9.7 %collective-permute-start.6 = (bf16[128,256]{1,0:T(8,128)(2,1)S(1)}, bf16[128,256]{1,0:T(8,128)(2,1)S(1)}, u32[]{:S(2)}, u32[]{:S(2)}) collective-permute-start(bf16[128,256]{1,0:T(8,128)(2,1)S(1)} %get-tuple-element.35), channel_id=1, source_target_pairs={{0,2},{1,3},{2,0},{3,1},{4,6},{5,7},{6,4},{7,5},{8,10},{9,11},{10,... | collective-permute-start | bytes 196616 | tf_op jit(solution)/shard_map/ppermute | solution.py:28
  29.8 6.5 %collective-permute-start.7 = (bf16[128,256]{1,0:T(8,128)(2,1)S(1)}, bf16[128,256]{1,0:T(8,128)(2,1)S(1)}, u32[]{:S(2)}, u32[]{:S(2)}) collective-permute-start(bf16[128,256]{1,0:T(8,128)(2,1)S(1)} %get-tuple-element.36), channel_id=1, source_target_pairs={{0,3},{1,2},{2,1},{3,0},{4,7},{5,6},{6,5},{7,4},{8,11},{9,10},{10,... | collective-permute-start | bytes 196616 | tf_op jit(solution)/shard_map/ppermute | solution.py:28
  38.8 3.1 %collective-permute-start.10 = (bf16[128,256]{1,0:T(8,128)(2,1)S(1)}, bf16[128,256]{1,0:T(8,128)(2,1)S(1)}, u32[]{:S(2)}, u32[]{:S(2)}) collective-permute-start(bf16[128,256]{1,0:T(8,128)(2,1)S(1)} %get-tuple-element.45), channel_id=1, source_target_pairs={{0,1},{1,0},{2,3},{3,2},{4,5},{5,4},{6,7},{7,6},{8,9},{9,8},{10,11... | collective-permute-start | bytes 196616 | tf_op jit(solution)/shard_map/ppermute | solution.py:28
  38.8 5.0 %collective-permute-start.11 = (bf16[128,256]{1,0:T(8,128)(2,1)S(1)}, bf16[128,256]{1,0:T(8,128)(2,1)S(1)}, u32[]{:S(2)}, u32[]{:S(2)}) collective-permute-start(bf16[128,256]{1,0:T(8,128)(2,1)S(1)} %get-tuple-element.46), channel_id=1, source_target_pairs={{0,2},{1,3},{2,0},{3,1},{4,6},{5,7},{6,4},{7,5},{8,10},{9,11},{10,... | collective-permute-start | bytes 196616 | tf_op jit(solution)/shard_map/ppermute | solution.py:28
  38.9 5.4 %collective-permute-start.12 = (bf16[128,256]{1,0:T(8,128)(2,1)S(1)}, bf16[128,256]{1,0:T(8,128)(2,1)S(1)}, u32[]{:S(2)}, u32[]{:S(2)}) collective-permute-start(bf16[128,256]{1,0:T(8,128)(2,1)S(1)} %get-tuple-element.47), channel_id=1, source_target_pairs={{0,3},{1,2},{2,1},{3,0},{4,7},{5,6},{6,5},{7,4},{8,11},{9,10},{10,... | collective-permute-start | bytes 196616 | tf_op jit(solution)/shard_map/ppermute | solution.py:28

commit v5 on v4

--- a/solution.py
+++ b/solution.py
@@ -11,6 +11,7 @@
 KEY_BLOCK = 256
 CHUNK_TOKENS = 64
 VMEM_LIMIT = 40 * 1024 * 1024
+CUT_LIMIT = 63 * 1024 * 1024
 
 WHOLE = pl.BlockSpec(memory_space=pltpu.VMEM)
 SCALARS = pl.BlockSpec(memory_space=pltpu.SMEM)
@@ -30,6 +31,44 @@
 
 def params(limit=VMEM_LIMIT):
     return pltpu.CompilerParams(vmem_limit_bytes=limit)
+
+
+def cut_kernel(cuts, source_ref, *refs):
+    *out_refs, held, in_sems, out_sems = refs
+    copies = []
+    for i, ((first, size), out_ref) in enumerate(zip(cuts, out_refs)):
+        rows = pl.ds(first, size)
+        copies.append((
+            pltpu.make_async_copy(source_ref.at[rows], held.at[rows], in_sems.at[i]),
+            pltpu.make_async_copy(held.at[rows], out_ref, out_sems.at[i]),
+        ))
+    for fetch, _ in copies:
+        fetch.start()
+    for fetch, store in copies:
+        fetch.wait()
+        store.start()
+    for _, store in copies:
+        store.wait()
+
+
+def cut(source, cuts):
+    return pl.pallas_call(
+        functools.partial(cut_kernel, cuts),
+        out_shape=[
+            jax.ShapeDtypeStruct((size, *source.shape[1:]), source.dtype) for _, size in cuts
+        ],
+        in_specs=[ANYWHERE],
+        out_specs=[ANYWHERE] * len(cuts),
+        scratch_shapes=[
+            pltpu.VMEM(source.shape, source.dtype),
+            pltpu.SemaphoreType.DMA((len(cuts),)),
+            pltpu.SemaphoreType.DMA((len(cuts),)),
+        ],
+        compiler_params=params(CUT_LIMIT),
+        cost_estimate=pl.CostEstimate(
+            flops=0, bytes_accessed=2 * source.size * source.dtype.itemsize, transcendentals=0
+        ),
+    )(source)
 
 
 def sort_keys_kernel(codes, span_rows, head_size, starts_ref, *refs):
@@ -205,12 +244,12 @@
     ]
     per_half = len(chunks) // 2
 
-    cuts = [half * span_rows + first for half, first, _ in chunks]
-    pieces = [grad_held[0, cuts[0] : cuts[0] + CHUNK_TOKENS]]
-    pieces[0], rest = lax.optimization_barrier((pieces[0], grad_held[0]))
-    pieces += [rest[at : at + CHUNK_TOKENS] for at in cuts[1:]]
-    grads = [from_behind(piece, "section", -1) for piece in pieces]
-
+    pieces = cut(
+        grad_held[0], [(half * span_rows + first, size) for half, first, size in chunks]
+    )
+    pieces = list(pieces)
+    grads = [from_behind(pieces[0], "section", -1)]
+    keys, values, pieces[0] = lax.optimization_barrier((keys, values, pieces[0]))
     pair = jnp.concatenate([keys, values], axis=0)
     blocks, codes = [pair], [0]
     step = count // 2
@@ -218,6 +257,10 @@
         blocks = blocks + [with_partner(block, "ctx", step) for block in blocks]
         codes = codes + [code ^ step for code in codes]
         step //= 2
+    gates = [pair, blocks[1]] + grads
+    for number, piece in enumerate(pieces[1:]):
+        piece, _ = lax.optimization_barrier((piece, gates[min(number, 2)]))
+        grads.append(from_behind(piece, "section", -1))
     sorted_keys = sort_keys(span_start, blocks, codes, span_rows, head_size)
 
     q_flat = queries.reshape(row_count * heads, head_size)

time: 45.2 us -> 44.3 us (0.980)
  local copies, waits for them, and re-layouts: 6.37 us -> 1.47 us
  Pallas kernels: 13.8 us -> 16 us
  starting transfers between devices: 17.5 us -> 18.5 us
  waiting for transfers between devices: 6.52 us -> 7.34 us
    ppermute x9, waiting for transfers between devices: 2.46 us -> 7.33 us  [with_partner(): return lax.ppermute(shard, axis, [(i, i ^ step) for i in range(length)])]
    ppermute x4, waiting for transfers between devices: 4.06 us -> 0.01 us  [from_behind(): lax.ppermute(shard, axis, [(i, (i + by) % length) for i in range(length)])]
    ppermute x4, starting transfers between devices: 9.12 us -> 11.7 us  [from_behind(): lax.ppermute(shard, axis, [(i, (i + by) % length) for i in range(length)])]
    pallas_call x0 -> x1, Pallas kernels: none -> 2.02 us  [cut(): pl.pallas_call(functools.partial(cut_kernel, cuts), out_shape=[jax.ShapeD...]
    slice x1 -> x0, local copies, waits for them, and re-layouts: 2.01 us -> none  [body(): pieces += [rest[at:at + CHUNK_TOKENS] for at in cuts[1:]]]
    squeeze x1 -> x0, local copies, waits for them, and re-layouts: 1.68 us -> none  [body(): pieces = [grad_held[0, cuts[0]:cuts[0] + CHUNK_TOKENS]]]
    ppermute x9, starting transfers between devices: 8.35 us -> 6.85 us  [with_partner(): return lax.ppermute(shard, axis, [(i, i ^ step) for i in range(length)])]
    reshape x1, local copies, waits for them, and re-layouts: 1.01 us -> 0.11 us  [body(): lse_flat = lse[0].T.reshape(1, row_count * heads)]
  transfers between devices with their start and end apart: 13 -> 13, of which waited for: 3 -> 5; matrix products, arithmetic and copies ran while one was open for 12% -> 1% of each run, Pallas kernels for 24% -> 25%
where the time goes in v5:
time: 44.3 us; the launch traced here: 44.1 us
  starting transfers between devices  18.5 us (42%)
  Pallas kernels  16 us (36%)
  waiting for transfers between devices  7.34 us (17%)
  local copies, waits for them, and re-layouts  1.47 us (3%)
  between operations  0.81 us (2%)
    ppermute x4, starting transfers between devices, from_behind(): lax.ppermute(shard, axis, [(i, (i + by) % length) for i in range(length)])  11.7 us
    pallas_call x4, Pallas kernels, body(): pl.pallas_call(functools.partial(chunk_kernel, chunk, heads, span_rows, c...  11.3 us
    ppermute x9, waiting for transfers between devices, with_partner(): return lax.ppermute(shard, axis, [(i, i ^ step) for i in range(length)])  7.33 us
    ppermute x9, starting transfers between devices, with_partner(): return lax.ppermute(shard, axis, [(i, i ^ step) for i in range(length)])  6.85 us
    pallas_call x1, Pallas kernels, cut(): pl.pallas_call(functools.partial(cut_kernel, cuts), out_shape=[jax.ShapeD...  2.02 us
    unnamed x13, local copies, waits for them, and re-layouts  1.25 us
    pallas_call x1, Pallas kernels, finish(): pl.pallas_call(functools.partial(finish_kernel, len(terms), places), out_...  1.13 us
  transfers between devices with their start and end apart: 13, of which 5 were waited for; matrix products, arithmetic and copies ran while one was open for 1% of the time, Pallas kernels for 25%

profile of v5, /device:TPU:0, one launch (start us, length us, event | category | flops | bytes accessed | tf_op | source)
XLA Modules:
  0.0 44.1 jit_solution(815360491203677184)
XLA Ops:
  0.7 2.0 %shard_map.94 = (bf16[64,16,128]{2,1,0:T(8,128)(2,1)}, bf16[64,16,128]{2,1,0:T(8,128)(2,1)}, bf16[64,16,128]{2,1,0:T(8,128)(2,1)}, bf16[64,16,128]{2,1,0:T(8,128)(2,1)}) custom-call(bf16[256,16,128]{2,1,0:T(8,128)(2,1)} %bitcast.25), custom_call_target="tpu_custom_call" | custom-call | bytes 2097152 | tf_op jit(solution)/shard_map/pallas_call | solution.py:55
  2.7 0.0 copy-start
  2.7 6.0 %collective-permute-start.4 = (bf16[64,16,128]{2,1,0:T(8,128)(2,1)}, bf16[64,16,128]{2,1,0:T(8,128)(2,1)S(1)}, u32[]{:S(2)}, u32[]{:S(2)}) collective-permute-start(bf16[64,16,128]{2,1,0:T(8,128)(2,1)} %get-tuple-element.35), channel_id=1, source_target_pairs={{0,28},{4,0},{8,4},{12,8},{16,12},{20,16},{24,20},{28,24},{1,29},{... | collective-permute-start | bytes 786440 | tf_op jit(solution)/shard_map/ppermute | solution.py:24
  8.8 1.6 %collective-permute-start.1 = (bf16[2,256,128]{2,1,0:T(8,128)(2,1)S(1)}, bf16[2,256,128]{2,1,0:T(8,128)(2,1)S(1)}, u32[]{:S(2)}, u32[]{:S(2)}) collective-permute-start(bf16[2,256,128]{2,1,0:T(8,128)(2,1)S(1)} %constant_dynamic-update-slice_fusion.refs_0_), channel_id=1, source_target_pairs={{0,2},{1,3},{2,0},{3,1},{4,6},{5,7},{6,4},{7,5},{8,10},{9,11},{10,... | collective-permute-start | bytes 393224 | tf_op jit(solution)/shard_map/ppermute | solution.py:29
  10.4 0.0 collective-permute-start.2
  10.4 3.4 %collective-permute-done.1.refs_1_ = bf16[2,256,128]{2,1,0:T(8,128)(2,1)S(1)} collective-permute-done((bf16[2,256,128]{2,1,0:T(8,128)(2,1)S(1)}, bf16[2,256,128]{2,1,0:T(8,128)(2,1)S(1)}, u32[]{:S(2)}, u32[]{:S(2)}) %collective-permute-start.1) | collective-permute-done | bytes 131104 | tf_op jit(solution)/shard_map/ppermute | solution.py:29
  13.8 0.0 collective-permute-start.3
  13.8 0.5 %collective-permute-start = (bf16[64,16,128]{2,1,0:T(8,128)(2,1)}, bf16[64,16,128]{2,1,0:T(8,128)(2,1)S(1)}, u32[]{:S(2)}, u32[]{:S(2)}) collective-permute-start(bf16[64,16,128]{2,1,0:T(8,128)(2,1)} %get-tuple-element.38), channel_id=1, source_target_pairs={{0,28},{4,0},{8,4},{12,8},{16,12},{20,16},{24,20},{28,24},{1,29},{... | collective-permute-start | bytes 786440 | tf_op jit(solution)/shard_map/ppermute | solution.py:24
  14.4 0.1 copy.11
  14.5 0.1 reshape.33.lse_ref
  14.6 1.4 %collective-permute-start.8 = (bf16[64,16,128]{2,1,0:T(8,128)(2,1)}, bf16[64,16,128]{2,1,0:T(8,128)(2,1)S(1)}, u32[]{:S(2)}, u32[]{:S(2)}) collective-permute-start(bf16[64,16,128]{2,1,0:T(8,128)(2,1)} %get-tuple-element.50), channel_id=1, source_target_pairs={{0,28},{4,0},{8,4},{12,8},{16,12},{20,16},{24,20},{28,24},{1,29},{... | collective-permute-start | bytes 786440 | tf_op jit(solution)/shard_map/ppermute | solution.py:24
  16.0 0.0 collective-permute-done.4
  16.0 3.7 %collective-permute-start.9 = (bf16[64,16,128]{2,1,0:T(8,128)(2,1)}, bf16[64,16,128]{2,1,0:T(8,128)(2,1)S(1)}, u32[]{:S(2)}, u32[]{:S(2)}) collective-permute-start(bf16[64,16,128]{2,1,0:T(8,128)(2,1)} %get-tuple-element.54), channel_id=1, source_target_pairs={{0,28},{4,0},{8,4},{12,8},{16,12},{20,16},{24,20},{28,24},{1,29},{... | collective-permute-start | bytes 786440 | tf_op jit(solution)/shard_map/ppermute | solution.py:24
  19.7 0.8 %shard_map.95 = (bf16[1024,128]{1,0:T(8,128)(2,1)S(1)}, bf16[1024,256]{1,0:T(8,128)(2,1)S(1)}, bf16[128,1024]{1,0:T(8,128)(2,1)S(1)}) custom-call(s32[8]{0:T(128)S(1)} %copy-done.2, bf16[2,256,128]{2,1,0:T(8,128)(2,1)S(1)} %constant_dynamic-update-slice_fusion.refs_0_, bf16[2,256,128]{2,1,0:T(8,128)(2,1)S(1)} %collective-permute-done.1.refs_1_, ...), custom_call_target="tpu_custom_call" | custom-call | tf_op jit(solution)/shard_map/pallas_call | solution.py:97
  20.5 0.0 copy-start.1
  20.5 1.2 %copy-done.1 = bf16[1,256,16,128]{3,2,1,0:T(8,128)(2,1)S(1)} copy-done((bf16[1,256,16,128]{3,2,1,0:T(8,128)(2,1)S(1)}, bf16[1,256,16,128]{3,2,1,0:T(8,128)(2,1)}, u32[]{:S(2)}) %copy-start.1) | copy-done | bytes 1048600
  21.8 3.2 %shard_map.96 = (f32[128,1024]{1,0:T(8,128)S(1)}, f32[1024,256]{1,0:T(8,128)S(1)}) custom-call(s32[8]{0:T(128)S(1)} %copy-done.2, bf16[4096,128]{1,0:T(8,128)(2,1)S(1)} %bitcast.13, bf16[1024,128]{1,0:T(8,128)(2,1)S(1)} %bitcast.23, bf16[4096,128]{1,0:T(8,128)(2,1)S(1)} %bitcast.17, f32[1,4096]{1,0:T(1,128)S(1)} %reshape.33.lse_ref, ...), custom_call_target="tpu_custom_call" | custom-call | flops 2013265920 | bytes 2097152 | tf_op jit(solution)/shard_map/pallas_call | solution.py:292
  25.0 3.3 %shard_map.97 = (f32[128,1024]{1,0:T(8,128)S(1)}, f32[1024,256]{1,0:T(8,128)S(1)}, f32[128,256]{1,0:T(8,128)S(1)}, bf16[128,256]{1,0:T(8,128)(2,1)S(1)}, bf16[12...) custom-call(s32[8]{0:T(128)S(1)} %copy-done.2, bf16[4096,128]{1,0:T(8,128)(2,1)S(1)} %bitcast.14, ...), custom_call_target="tpu_custom_call" | custom-call | flops 2013265920 | bytes 2097152 | tf_op jit(solution)/shard_map/pallas_call | solution.py:292
  28.3 0.1 collective-permute-start.5
  28.3 3.2 %collective-permute-start.6 = (bf16[128,256]{1,0:T(8,128)(2,1)S(1)}, bf16[128,256]{1,0:T(8,128)(2,1)S(1)}, u32[]{:S(2)}, u32[]{:S(2)}) collective-permute-start(bf16[128,256]{1,0:T(8,128)(2,1)S(1)} %get-tuple-element.45), channel_id=1, source_target_pairs={{0,2},{1,3},{2,0},{3,1},{4,6},{5,7},{6,4},{7,5},{8,10},{9,11},{10,... | collective-permute-start | bytes 196616 | tf_op jit(solution)/shard_map/ppermute | solution.py:29
  31.5 0.1 collective-permute-start.7
  31.6 2.4 %shard_map.98 = (f32[128,1024]{1,0:T(8,128)S(1)}, f32[512,256]{1,0:T(8,128)S(1)}) custom-call(s32[8]{0:T(128)S(1)} %copy-done.2, bf16[4096,128]{1,0:T(8,128)(2,1)S(1)} %bitcast.15, bf16[1024,128]{1,0:T(8,128)(2,1)S(1)} %bitcast.22, bf16[4096,128]{1,0:T(8,128)(2,1)S(1)} %bitcast.19, f32[1,4096]{1,0:T(1,128)S(1)} %reshape.33.lse_ref, ...), custom_call_target="tpu_custom_call" | custom-call | flops 671088640 | bytes 2097152 | tf_op jit(solution)/shard_map/pallas_call | solution.py:292
  34.0 0.2 collective-permute-done.6.refs_2_
  34.2 1.4 %collective-permute-done.7.refs_3_ = bf16[128,256]{1,0:T(8,128)(2,1)S(1)} collective-permute-done((bf16[128,256]{1,0:T(8,128)(2,1)S(1)}, bf16[128,256]{1,0:T(8,128)(2,1)S(1)}, u32[]{:S(2)}, u32[]{:S(2)}) %collective-permute-start.7) | collective-permute-done | bytes 65568 | tf_op jit(solution)/shard_map/ppermute | solution.py:29
  35.6 2.4 %shard_map.99 = (f32[128,1024]{1,0:T(8,128)S(1)}, f32[128,256]{1,0:T(8,128)S(1)}, bf16[128,256]{1,0:T(8,128)(2,1)S(1)}, bf16[128,256]{1,0:T(8,128)(2,1)S(1)}, bf16[128,256]{1,0:T(8,128)(2,1)S(1)}) custom-call(s32[8]{0:T(128)S(1)} %copy-done.2, bf16[4096,128]{1,0:T(8,128)(2,1)S(1)} %bitcast.16, bf16[1024,128]{1,0:T(8,128)(2,1)S(1)} %bitcast.21, ...), custom_call_target="tpu_custom_call" | custom-call | flops 671088640 | bytes 2097152 | tf_op jit(solution)/shard_map/pallas_call | solution.py:292
  38.0 0.2 collective-permute-start.10
  38.3 0.7 %collective-permute-start.11 = (bf16[128,256]{1,0:T(8,128)(2,1)S(1)}, bf16[128,256]{1,0:T(8,128)(2,1)S(1)}, u32[]{:S(2)}, u32[]{:S(2)}) collective-permute-start(bf16[128,256]{1,0:T(8,128)(2,1)S(1)} %get-tuple-element.60), channel_id=1, source_target_pairs={{0,2},{1,3},{2,0},{3,1},{4,6},{5,7},{6,4},{7,5},{8,10},{9,11},{10,... | collective-permute-start | bytes 196616 | tf_op jit(solution)/shard_map/ppermute | solution.py:29
  38.9 1.0 %collective-permute-start.12 = (bf16[128,256]{1,0:T(8,128)(2,1)S(1)}, bf16[128,256]{1,0:T(8,128)(2,1)S(1)}, u32[]{:S(2)}, u32[]{:S(2)}) collective-permute-start(bf16[128,256]{1,0:T(8,128)(2,1)S(1)} %get-tuple-element.61), channel_id=1, source_target_pairs={{0,3},{1,2},{2,1},{3,0},{4,7},{5,6},{6,5},{7,4},{8,11},{9,10},{10,... | collective-permute-start | bytes 196616 | tf_op jit(solution)/shard_map/ppermute | solution.py:29
  40.0 1.1 %shard_map.100 = (bf16[128,256]{1,0:T(8,128)(2,1)S(1)}, bf16[4096,128]{1,0:T(8,128)(2,1)}) custom-call(f32[128,256]{1,0:T(8,128)S(1)} %get-tuple-element.43.refs_0_, bf16[128,256]{1,0:T(8,128)(2,1)S(1)} %collective-permute-done.5.refs_1_, bf16[128,256]{1,0:T(8,128)(2,1)S(1)} %collective-permute-done.6.refs_2_, ...), custom_call_target="tpu_custom_call" | custom-call | tf_op jit(solution)/shard_map/pallas_call | solution.py:221
  41.1 2.1 %collective-permute-done.11.refs_2_ = bf16[128,256]{1,0:T(8,128)(2,1)S(1)} collective-permute-done((bf16[128,256]{1,0:T(8,128)(2,1)S(1)}, bf16[128,256]{1,0:T(8,128)(2,1)S(1)}, u32[]{:S(2)}, u32[]{:S(2)}) %collective-permute-start.11) | collective-permute-done | bytes 65568 | tf_op jit(solution)/shard_map/ppermute | solution.py:29
  43.2 0.3 collective-permute-done.12.refs_3_
  43.4 0.7 %shard_map.101 = (bf16[256,128]{1,0:T(8,128)(2,1)}, bf16[256,128]{1,0:T(8,128)(2,1)}) custom-call(f32[128,256]{1,0:T(8,128)S(1)} %get-tuple-element.58.refs_0_, bf16[128,256]{1,0:T(8,128)(2,1)S(1)} %collective-permute-done.10.refs_1_, bf16[128,256]{1,0:T(8,128)(2,1)S(1)} %collective-permute-done.11.refs_2_, ...), custom_call_target="tpu_custom_call" | custom-call | tf_op jit(solution)/shard_map/pallas_call | solution.py:315
  (18 shorter events, 0.1 us)
Async XLA Ops:
  0.6 8.1 %copy-start.3 = (bf16[1,256,128]{2,1,0:T(8,128)(2,1)S(1)}, bf16[1,256,128]{2,1,0:T(8,128)(2,1)}, u32[]{:S(2)}) copy-start(bf16[1,256,128]{2,1,0:T(8,128)(2,1)} %param.8) | copy-start | bytes 196612
  0.6 8.1 %copy-start.4 = (bf16[1,256,128]{2,1,0:T(8,128)(2,1)S(1)}, bf16[1,256,128]{2,1,0:T(8,128)(2,1)}, u32[]{:S(2)}) copy-start(bf16[1,256,128]{2,1,0:T(8,128)(2,1)} %param.9) | copy-start | bytes 196612
  0.7 13.7 %copy-start.5 = (f32[1,16,256]{2,1,0:T(8,128)S(1)}, f32[1,16,256]{2,1,0:T(8,128)}, u32[]{:S(2)}) copy-start(f32[1,16,256]{2,1,0:T(8,128)} %param.12) | copy-start | bytes 49156
  0.7 19.0 %copy-start.2 = (s32[8]{0:T(128)S(1)}, s32[8]{0:T(128)}, u32[]{:S(2)}) copy-start(s32[8]{0:T(128)} %starts_ref.9) | copy-start | bytes 100
  2.7 17.8 %copy-start = (bf16[1,256,16,128]{3,2,1,0:T(8,128)(2,1)S(1)}, bf16[1,256,16,128]{3,2,1,0:T(8,128)(2,1)}, u32[]{:S(2)}) copy-start(bf16[1,256,16,128]{3,2,1,0:T(8,128)(2,1)} %param.7) | copy-start | bytes 3145732
  2.7 13.3 %collective-permute-start.4 = (bf16[64,16,128]{2,1,0:T(8,128)(2,1)}, bf16[64,16,128]{2,1,0:T(8,128)(2,1)S(1)}, u32[]{:S(2)}, u32[]{:S(2)}) collective-permute-start(bf16[64,16,128]{2,1,0:T(8,128)(2,1)} %get-tuple-element.35), channel_id=1, source_target_pairs={{0,28},{4,0},{8,4},{12,8},{16,12},{20,16},{24,20},{28,24},{1,29},{... | collective-permute-start | bytes 786440 | tf_op jit(solution)/shard_map/ppermute | solution.py:24
  8.8 5.0 %collective-permute-start.1 = (bf16[2,256,128]{2,1,0:T(8,128)(2,1)S(1)}, bf16[2,256,128]{2,1,0:T(8,128)(2,1)S(1)}, u32[]{:S(2)}, u32[]{:S(2)}) collective-permute-start(bf16[2,256,128]{2,1,0:T(8,128)(2,1)S(1)} %constant_dynamic-update-slice_fusion.refs_0_), channel_id=1, source_target_pairs={{0,2},{1,3},{2,0},{3,1},{4,6},{5,7},{6,4},{7,5},{8,10},{9,11},{10,... | collective-permute-start | bytes 393224 | tf_op jit(solution)/shard_map/ppermute | solution.py:29
  10.4 9.3 %collective-permute-start.2 = (bf16[2,256,128]{2,1,0:T(8,128)(2,1)S(1)}, bf16[2,256,128]{2,1,0:T(8,128)(2,1)S(1)}, u32[]{:S(2)}, u32[]{:S(2)}) collective-permute-start(bf16[2,256,128]{2,1,0:T(8,128)(2,1)S(1)} %constant_dynamic-update-slice_fusion.refs_0_), channel_id=1, source_target_pairs={{0,1},{1,0},{2,3},{3,2},{4,5},{5,4},{6,7},{7,6},{8,9},{9,8},{10,11... | collective-permute-start | bytes 393224 | tf_op jit(solution)/shard_map/ppermute | solution.py:29
  13.8 5.9 %collective-permute-start.3 = (bf16[2,256,128]{2,1,0:T(8,128)(2,1)S(1)}, bf16[2,256,128]{2,1,0:T(8,128)(2,1)S(1)}, u32[]{:S(2)}, u32[]{:S(2)}) collective-permute-start(bf16[2,256,128]{2,1,0:T(8,128)(2,1)S(1)} %collective-permute-done.1.refs_1_), channel_id=1, source_target_pairs={{0,1},{1,0},{2,3},{3,2},{4,5},{5,4},{6,7},{7,6},{8,9},{9,8},{10,11... | collective-permute-start | bytes 393224 | tf_op jit(solution)/shard_map/ppermute | solution.py:29
  13.8 11.2 %collective-permute-start = (bf16[64,16,128]{2,1,0:T(8,128)(2,1)}, bf16[64,16,128]{2,1,0:T(8,128)(2,1)S(1)}, u32[]{:S(2)}, u32[]{:S(2)}) collective-permute-start(bf16[64,16,128]{2,1,0:T(8,128)(2,1)} %get-tuple-element.38), channel_id=1, source_target_pairs={{0,28},{4,0},{8,4},{12,8},{16,12},{20,16},{24,20},{28,24},{1,29},{... | collective-permute-start | bytes 786440 | tf_op jit(solution)/shard_map/ppermute | solution.py:24
  14.6 17.0 %collective-permute-start.8 = (bf16[64,16,128]{2,1,0:T(8,128)(2,1)}, bf16[64,16,128]{2,1,0:T(8,128)(2,1)S(1)}, u32[]{:S(2)}, u32[]{:S(2)}) collective-permute-start(bf16[64,16,128]{2,1,0:T(8,128)(2,1)} %get-tuple-element.50), channel_id=1, source_target_pairs={{0,28},{4,0},{8,4},{12,8},{16,12},{20,16},{24,20},{28,24},{1,29},{... | collective-permute-start | bytes 786440 | tf_op jit(solution)/shard_map/ppermute | solution.py:24
  16.0 19.6 %collective-permute-start.9 = (bf16[64,16,128]{2,1,0:T(8,128)(2,1)}, bf16[64,16,128]{2,1,0:T(8,128)(2,1)S(1)}, u32[]{:S(2)}, u32[]{:S(2)}) collective-permute-start(bf16[64,16,128]{2,1,0:T(8,128)(2,1)} %get-tuple-element.54), channel_id=1, source_target_pairs={{0,28},{4,0},{8,4},{12,8},{16,12},{20,16},{24,20},{28,24},{1,29},{... | collective-permute-start | bytes 786440 | tf_op jit(solution)/shard_map/ppermute | solution.py:24
  20.5 1.2 %copy-start.1 = (bf16[1,256,16,128]{3,2,1,0:T(8,128)(2,1)S(1)}, bf16[1,256,16,128]{3,2,1,0:T(8,128)(2,1)}, u32[]{:S(2)}) copy-start(bf16[1,256,16,128]{3,2,1,0:T(8,128)(2,1)} %param.10) | copy-start | bytes 3145732
  28.3 5.8 %collective-permute-start.5 = (bf16[128,256]{1,0:T(8,128)(2,1)S(1)}, bf16[128,256]{1,0:T(8,128)(2,1)S(1)}, u32[]{:S(2)}, u32[]{:S(2)}) collective-permute-start(bf16[128,256]{1,0:T(8,128)(2,1)S(1)} %get-tuple-element.44), channel_id=1, source_target_pairs={{0,1},{1,0},{2,3},{3,2},{4,5},{5,4},{6,7},{7,6},{8,9},{9,8},{10,11... | collective-permute-start | bytes 196616 | tf_op jit(solution)/shard_map/ppermute | solution.py:29
  28.3 5.9 %collective-permute-start.6 = (bf16[128,256]{1,0:T(8,128)(2,1)S(1)}, bf16[128,256]{1,0:T(8,128)(2,1)S(1)}, u32[]{:S(2)}, u32[]{:S(2)}) collective-permute-start(bf16[128,256]{1,0:T(8,128)(2,1)S(1)} %get-tuple-element.45), channel_id=1, source_target_pairs={{0,2},{1,3},{2,0},{3,1},{4,6},{5,7},{6,4},{7,5},{8,10},{9,11},{10,... | collective-permute-start | bytes 196616 | tf_op jit(solution)/shard_map/ppermute | solution.py:29
  31.5 4.0 %collective-permute-start.7 = (bf16[128,256]{1,0:T(8,128)(2,1)S(1)}, bf16[128,256]{1,0:T(8,128)(2,1)S(1)}, u32[]{:S(2)}, u32[]{:S(2)}) collective-permute-start(bf16[128,256]{1,0:T(8,128)(2,1)S(1)} %get-tuple-element.46), channel_id=1, source_target_pairs={{0,3},{1,2},{2,1},{3,0},{4,7},{5,6},{6,5},{7,4},{8,11},{9,10},{10,... | collective-permute-start | bytes 196616 | tf_op jit(solution)/shard_map/ppermute | solution.py:29
  38.0 3.1 %collective-permute-start.10 = (bf16[128,256]{1,0:T(8,128)(2,1)S(1)}, bf16[128,256]{1,0:T(8,128)(2,1)S(1)}, u32[]{:S(2)}, u32[]{:S(2)}) collective-permute-start(bf16[128,256]{1,0:T(8,128)(2,1)S(1)} %get-tuple-element.59), channel_id=1, source_target_pairs={{0,1},{1,0},{2,3},{3,2},{4,5},{5,4},{6,7},{7,6},{8,9},{9,8},{10,11... | collective-permute-start | bytes 196616 | tf_op jit(solution)/shard_map/ppermute | solution.py:29
  38.3 4.9 %collective-permute-start.11 = (bf16[128,256]{1,0:T(8,128)(2,1)S(1)}, bf16[128,256]{1,0:T(8,128)(2,1)S(1)}, u32[]{:S(2)}, u32[]{:S(2)}) collective-permute-start(bf16[128,256]{1,0:T(8,128)(2,1)S(1)} %get-tuple-element.60), channel_id=1, source_target_pairs={{0,2},{1,3},{2,0},{3,1},{4,6},{5,7},{6,4},{7,5},{8,10},{9,11},{10,... | collective-permute-start | bytes 196616 | tf_op jit(solution)/shard_map/ppermute | solution.py:29
  38.9 4.5 %collective-permute-start.12 = (bf16[128,256]{1,0:T(8,128)(2,1)S(1)}, bf16[128,256]{1,0:T(8,128)(2,1)S(1)}, u32[]{:S(2)}, u32[]{:S(2)}) collective-permute-start(bf16[128,256]{1,0:T(8,128)(2,1)S(1)} %get-tuple-element.61), channel_id=1, source_target_pairs={{0,3},{1,2},{2,1},{3,0},{4,7},{5,6},{6,5},{7,4},{8,11},{9,10},{10,... | collective-permute-start | bytes 196616 | tf_op jit(solution)/shard_map/ppermute | solution.py:29

commit v6 on v5

--- a/solution.py
+++ b/solution.py
@@ -11,7 +11,9 @@
 KEY_BLOCK = 256
 CHUNK_TOKENS = 64
 VMEM_LIMIT = 40 * 1024 * 1024
-CUT_LIMIT = 63 * 1024 * 1024
+CUT_LIMIT = 62 * 1024 * 1024
+SORT_FLOPS = 10**9
+WIDEN_FLOPS = 4 * 10**9
 
 WHOLE = pl.BlockSpec(memory_space=pltpu.VMEM)
 SCALARS = pl.BlockSpec(memory_space=pltpu.SMEM)
@@ -33,15 +35,21 @@
     return pltpu.CompilerParams(vmem_limit_bytes=limit)
 
 
-def cut_kernel(cuts, source_ref, *refs):
-    *out_refs, held, in_sems, out_sems = refs
-    copies = []
-    for i, ((first, size), out_ref) in enumerate(zip(cuts, out_refs)):
+def cut_kernel(cuts, source_ref, keys_ref, values_ref, *refs):
+    pair_ref, *out_refs, held, held_pair, in_sems, out_sems = refs
+    moves = []
+    for (first, size), out_ref in zip(cuts, out_refs):
         rows = pl.ds(first, size)
-        copies.append((
-            pltpu.make_async_copy(source_ref.at[rows], held.at[rows], in_sems.at[i]),
-            pltpu.make_async_copy(held.at[rows], out_ref, out_sems.at[i]),
-        ))
+        moves.append((source_ref.at[rows], held.at[rows], out_ref))
+    for i, part_ref in enumerate((keys_ref, values_ref)):
+        moves.append((part_ref.at[0], held_pair.at[i], pair_ref.at[i]))
+    copies = [
+        (
+            pltpu.make_async_copy(source, stage, in_sems.at[i]),
+            pltpu.make_async_copy(stage, target, out_sems.at[i]),
+        )
+        for i, (source, stage, target) in enumerate(moves)
+    ]
     for fetch, _ in copies:
         fetch.start()
     for fetch, store in copies:
@@ -51,24 +59,50 @@
         store.wait()
 
 
-def cut(source, cuts):
+def cut(source, keys, values, cuts):
+    pair = (2, *keys.shape[1:])
     return pl.pallas_call(
         functools.partial(cut_kernel, cuts),
-        out_shape=[
-            jax.ShapeDtypeStruct((size, *source.shape[1:]), source.dtype) for _, size in cuts
-        ],
-        in_specs=[ANYWHERE],
-        out_specs=[ANYWHERE] * len(cuts),
+        out_shape=[jax.ShapeDtypeStruct(pair, keys.dtype)]
+        + [jax.ShapeDtypeStruct((size, *source.shape[1:]), source.dtype) for _, size in cuts],
+        in_specs=[ANYWHERE] * 3,
+        out_specs=[ANYWHERE] * (len(cuts) + 1),
         scratch_shapes=[
             pltpu.VMEM(source.shape, source.dtype),
-            pltpu.SemaphoreType.DMA((len(cuts),)),
-            pltpu.SemaphoreType.DMA((len(cuts),)),
+            pltpu.VMEM(pair, keys.dtype),
+            pltpu.SemaphoreType.DMA((len(cuts) + 2,)),
+            pltpu.SemaphoreType.DMA((len(cuts) + 2,)),
         ],
         compiler_params=params(CUT_LIMIT),
         cost_estimate=pl.CostEstimate(
             flops=0, bytes_accessed=2 * source.size * source.dtype.itemsize, transcendentals=0
         ),
-    )(source)
+    )(source, keys, values)
+
+
+def widen_kernel(rows, g_ref, o_ref, wide_ref):
+    head_size = g_ref.shape[1]
+    g = g_ref[...]
+    wide_ref[:, :head_size] = g
+    wide_ref[:, head_size:] = times(g, o_ref[rows, :])
+
+
+def widen(grad, outputs, first):
+    row_count, head_size = grad.shape
+    return pl.pallas_call(
+        functools.partial(widen_kernel, slice(first, first + row_count)),
+        out_shape=jax.ShapeDtypeStruct((row_count, 2 * head_size), grad.dtype),
+        in_specs=[WHOLE] * 2,
+        out_specs=WHOLE,
+        compiler_params=params(),
+        cost_estimate=pl.CostEstimate(
+            flops=WIDEN_FLOPS, bytes_accessed=grad.size * 8, transcendentals=0
+        ),
+    )(grad, outputs)
+
+
+def times(g, o):
+    return (g.astype(jnp.float32) * o.astype(jnp.float32)).astype(jnp.bfloat16)
 
 
 def sort_keys_kernel(codes, span_rows, head_size, starts_ref, *refs):
@@ -104,6 +138,9 @@
         in_specs=[SCALARS] + [WHOLE] * count,
         out_specs=(WHOLE,) * 3,
         compiler_params=params(),
+        cost_estimate=pl.CostEstimate(
+            flops=SORT_FLOPS, bytes_accessed=8 * total * head_size, transcendentals=0
+        ),
     )(span_start, *blocks)
 
 
@@ -124,8 +161,10 @@
 
     q = q_ref[rows, :]
     g = g_ref[...]
-    products = (g.astype(jnp.float32) * o_ref[rows, :].astype(jnp.float32)).astype(jnp.bfloat16)
-    g_wide = jnp.concatenate([g, products], axis=1)
+    if g.shape[1] == head_size:
+        g_wide = jnp.concatenate([g, times(g, o_ref[rows, :])], axis=1)
+    else:
+        g, g_wide = g[:, :head_size], g
     lse2 = lse_ref[0:1, rows] * to_log2
     dq_ref[...] = jnp.zeros_like(dq_ref)
 
@@ -154,24 +193,27 @@
     block(full_blocks, True)
 
 
-def hand_out(half, count, span_rows, starts_ref, total_ref, own_ref, send_refs):
+def hand_out(half, count, span_rows, starts_ref, total_ref, own_ref, send_ref):
     head_size = total_ref.shape[1] // 2
     scale = head_size**-0.5
     me = lax.axis_index("ctx")
-    for step in range(count):
-        owner = lax.bitwise_xor(me, step)
+    for owner in range(count):
         start = pl.multiple_of(starts_ref[2 * owner + half], span_rows)
         rows = pl.ds(start, span_rows)
-        target = own_ref if step == 0 else send_refs[step - 1]
-        target[:, :head_size] = (total_ref[rows, :head_size] * scale).astype(target.dtype)
-        target[:, head_size:] = total_ref[rows, head_size:].astype(target.dtype)
-
-
-def add_terms(term_refs):
-    total = term_refs[0][...]
-    for term_ref in term_refs[1:]:
-        total = total + term_ref[...].astype(jnp.float32)
-    return total
+        send_ref[owner, :, :head_size] = (total_ref[rows, :head_size] * scale).astype(jnp.bfloat16)
+        send_ref[owner, :, head_size:] = total_ref[rows, head_size:].astype(jnp.bfloat16)
+    rows = pl.ds(pl.multiple_of(starts_ref[2 * me + half], span_rows), span_rows)
+    own_ref[:, :head_size] = total_ref[rows, :head_size] * scale
+    own_ref[:, head_size:] = total_ref[rows, head_size:]
+
+
+def add_terms(own_ref, terms_ref):
+    me = lax.axis_index("ctx")
+    total = own_ref[...]
+    for owner in range(terms_ref.shape[0]):
+        term = terms_ref[owner].astype(jnp.float32)
+        total = total + jnp.where(me == owner, 0.0, term)
+    return total.astype(jnp.bfloat16)
 
 
 def chunk_kernel(
@@ -191,19 +233,17 @@
         keys_t_ref, total_ref, dq_ref,
     )
     if hands_out:
-        hand_out(chunk[0], count, span_rows, starts_ref, total_ref, handed[0], handed[1:])
-
-
-def add_kernel(count, span_rows, head_size, *refs):
-    term_refs, upper_ref, (key_ref, value_ref) = refs[:count], refs[count], refs[count + 1 :]
-    lower = add_terms(term_refs).astype(jnp.bfloat16)
+        hand_out(chunk[0], count, span_rows, starts_ref, total_ref, *handed)
+
+
+def add_kernel(span_rows, head_size, own_ref, terms_ref, upper_ref, key_ref, value_ref):
+    lower = add_terms(own_ref, terms_ref)
     for out_ref, columns in ((key_ref, slice(0, head_size)), (value_ref, slice(head_size, None))):
         out_ref[:span_rows, :] = lower[:, columns]
         out_ref[span_rows:, :] = upper_ref[:, columns]
 
 
-def finish_kernel(count, places, *refs):
-    term_refs, refs = refs[:count], refs[count:]
+def finish_kernel(places, own_ref, terms_ref, *refs):
     part_refs, (upper_ref, out_ref, held, sems) = refs[: len(places)], refs[len(places) :]
     scale = out_ref.shape[1] ** -0.5
     copies = []
@@ -212,14 +252,14 @@
         held[rows, :] = (part_ref[...] * scale).T.astype(jnp.bfloat16)
         copies.append(pltpu.make_async_copy(held.at[rows], out_ref.at[rows], sems.at[i]))
         copies[-1].start()
-    upper_ref[...] = add_terms(term_refs).astype(jnp.bfloat16)
+    upper_ref[...] = add_terms(own_ref, terms_ref)
     for copy in copies:
         copy.wait()
 
 
 def finish(terms, parts, places, shape):
     return pl.pallas_call(
-        functools.partial(finish_kernel, len(terms), places),
+        functools.partial(finish_kernel, places),
         out_shape=(
             jax.ShapeDtypeStruct(terms[0].shape, jnp.bfloat16),
             jax.ShapeDtypeStruct(shape, jnp.bfloat16),
@@ -244,22 +284,20 @@
     ]
     per_half = len(chunks) // 2
 
-    pieces = cut(
-        grad_held[0], [(half * span_rows + first, size) for half, first, size in chunks]
-    )
-    pieces = list(pieces)
+    pair, *pieces = cut(
+        grad_held[0], keys, values,
+        [(half * span_rows + first, size) for half, first, size in chunks],
+    )
     grads = [from_behind(pieces[0], "section", -1)]
-    keys, values, pieces[0] = lax.optimization_barrier((keys, values, pieces[0]))
-    pair = jnp.concatenate([keys, values], axis=0)
     blocks, codes = [pair], [0]
     step = count // 2
     while step:
         blocks = blocks + [with_partner(block, "ctx", step) for block in blocks]
         codes = codes + [code ^ step for code in codes]
         step //= 2
-    gates = [pair, blocks[1]] + grads
-    for number, piece in enumerate(pieces[1:]):
-        piece, _ = lax.optimization_barrier((piece, gates[min(number, 2)]))
+    for piece, gate in zip(pieces[1:], [None, None] + [blocks[1]] * len(pieces)):
+        if gate is not None:
+            piece, _ = lax.optimization_barrier((piece, gate))
         grads.append(from_behind(piece, "section", -1))
     sorted_keys = sort_keys(span_start, blocks, codes, span_rows, head_size)
 
@@ -277,8 +315,11 @@
         after = received if is_last else []
         if after:
             upper_terms = received
+        grad = grads[number].reshape(rows, head_size)
+        if is_first:
+            grad = widen(grad, o_flat, (half * span_rows + chunk[1]) * heads)
         operands = [
-            q_flat, grads[number].reshape(rows, head_size), o_flat, lse_flat, *sorted_keys, *after,
+            q_flat, grad, o_flat, lse_flat, *sorted_keys, *after,
             *running,
         ]
         total_shape = (total if half else total // 2, 2 * head_size)
@@ -287,7 +328,7 @@
             out_shape.append(jax.ShapeDtypeStruct(total_shape, jnp.float32))
         if hands_out:
             out_shape.append(jax.ShapeDtypeStruct(span_wide, jnp.float32))
-            out_shape += [jax.ShapeDtypeStruct(span_wide, jnp.bfloat16)] * (count - 1)
+            out_shape.append(jax.ShapeDtypeStruct((count, *span_wide), jnp.bfloat16))
         pairs = rows * (3 * total // 4 if half == 1 else total // 4)
         dq, *handed = pl.pallas_call(
             functools.partial(
@@ -306,16 +347,14 @@
         dq_parts.append(dq)
         running = [] if is_last else [handed.pop(0)]
         if hands_out:
-            received = [handed[0]] + [
-                with_partner(send, "ctx", step) for step, send in enumerate(handed[1:], start=1)
-            ]
+            received = [handed[0], lax.all_to_all(handed[1], "ctx", 0, 0)]
 
     places = [(half * span_rows + first) * heads for half, first, _ in chunks]
     upper_sum, dq = finish(upper_terms, dq_parts, places, q_flat.shape)
     key_out, value_out = pl.pallas_call(
-        functools.partial(add_kernel, count, span_rows, head_size),
+        functools.partial(add_kernel, span_rows, head_size),
         out_shape=(jax.ShapeDtypeStruct((row_count, head_size), jnp.bfloat16),) * 2,
-        in_specs=[WHOLE] * (count + 1),
+        in_specs=[WHOLE] * 3,
         out_specs=(WHOLE,) * 2,
         compiler_params=params(),
     )(*received, upper_sum)

time: 44.3 us -> 56.1 us (1.27); the launches traced: 44.1 us -> 55 us
  local copies, waits for them, and re-layouts: 1.47 us -> 13.2 us
  waiting for transfers between devices: 7.34 us -> 5.09 us
  Pallas kernels: 16 us -> 18.2 us
  starting transfers between devices: 18.5 us -> 17.7 us
    unnamed x13 -> x44, local copies, waits for them, and re-layouts: 1.25 us -> 13 us
    all_to_all x0 -> x2, starting transfers between devices: none -> 7.66 us  [body(): received = [handed[0], lax.all_to_all(handed[1], 'ctx', 0, 0)]]
    ppermute x9 -> x3, starting transfers between devices: 6.85 us -> 1.52 us  [with_partner(): return lax.ppermute(shard, axis, [(i, i ^ step) for i in range(length)])]
    ppermute x9 -> x3, waiting for transfers between devices: 7.33 us -> 2.04 us  [with_partner(): return lax.ppermute(shard, axis, [(i, i ^ step) for i in range(length)])]
    ppermute x4, starting transfers between devices: 11.7 us -> 8.48 us  [from_behind(): lax.ppermute(shard, axis, [(i, (i + by) % length) for i in range(length)])]
    pallas_call x4, Pallas kernels: 11.3 us -> 13.3 us  [body(): pl.pallas_call(functools.partial(chunk_kernel, chunk, heads, span_rows, c...]
    all_to_all x0 -> x2, waiting for transfers between devices: none -> 1.73 us  [body(): received = [handed[0], lax.all_to_all(handed[1], 'ctx', 0, 0)]]
    ppermute x4, waiting for transfers between devices: 0.01 us -> 1.32 us  [from_behind(): lax.ppermute(shard, axis, [(i, (i + by) % length) for i in range(length)])]
  transfers between devices with their start and end apart: 13 -> 9, of which waited for: 5 -> 4; matrix products, arithmetic and copies ran while one was open for 1% -> 0% of each run, Pallas kernels for 25% -> 22%
where the time goes in v6:
time: 56.1 us; the launch traced here: 55 us
  Pallas kernels  18.2 us (32%)
  starting transfers between devices  17.7 us (32%)
  local copies, waits for them, and re-layouts  13.2 us (24%)
  waiting for transfers between devices  5.09 us (9%)
  between operations  0.83 us (1%)
    pallas_call x4, Pallas kernels, body(): pl.pallas_call(functools.partial(chunk_kernel, chunk, heads, span_rows, c...  13.3 us
    unnamed x44, local copies, waits for them, and re-layouts  13 us
    ppermute x4, starting transfers between devices, from_behind(): lax.ppermute(shard, axis, [(i, (i + by) % length) for i in range(length)])  8.48 us
    all_to_all x2, starting transfers between devices, body(): received = [handed[0], lax.all_to_all(handed[1], 'ctx', 0, 0)]  7.66 us
    pallas_call x1, Pallas kernels, cut(): pl.pallas_call(functools.partial(cut_kernel, cuts), out_shape=[jax.ShapeD...  2.14 us
    ppermute x3, waiting for transfers between devices, with_partner(): return lax.ppermute(shard, axis, [(i, i ^ step) for i in range(length)])  2.04 us
    all_to_all x2, waiting for transfers between devices, body(): received = [handed[0], lax.all_to_all(handed[1], 'ctx', 0, 0)]  1.73 us
    ppermute x3, starting transfers between devices, with_partner(): return lax.ppermute(shard, axis, [(i, i ^ step) for i in range(length)])  1.52 us
  transfers between devices with their start and end apart: 9, of which 4 were waited for; matrix products, arithmetic and copies ran while one was open for 0% of the time, Pallas kernels for 22%

profile of v6, /device:TPU:0, one launch (start us, length us, event | category | flops | bytes accessed | tf_op | source)
XLA Modules:
  0.0 55.0 jit_solution(12613356635843925628)
XLA Ops:
  0.7 2.1 %shard_map.94 = (bf16[2,256,128]{2,1,0:T(8,128)(2,1)}, bf16[64,16,128]{2,1,0:T(8,128)(2,1)}, bf16[64,16,128]{2,1,0:T(8,128)(2,1)}, bf16[64,16,128]{2,1,0:T(8,128)(2,1)}, bf16[64,16,128]{2,1,0:T(8,128)(2,1)}) custom-call(bf16[256,16,128]{2,1,0:T(8,128)(2,1)} %bitcast.24, bf16[1,256,128]{2,1,0:T(8,128)(2,1)} %keys_ref.1, bf16[1,256,128]{2,1,0:T(8,128)(2,1)} %values_ref.1), custom_call_target="tpu_custom_call" | custom-call | bytes 2097152 | tf_op jit(solution)/shard_map/pallas_call | solution.py:64
  2.8 6.0 %collective-permute-start.4 = (bf16[64,16,128]{2,1,0:T(8,128)(2,1)}, bf16[64,16,128]{2,1,0:T(8,128)(2,1)S(1)}, u32[]{:S(2)}, u32[]{:S(2)}) collective-permute-start(bf16[64,16,128]{2,1,0:T(8,128)(2,1)} %get-tuple-element.32), channel_id=1, source_target_pairs={{0,28},{4,0},{8,4},{12,8},{16,12},{20,16},{24,20},{28,24},{1,29},{... | collective-permute-start | bytes 786440 | tf_op jit(solution)/shard_map/ppermute | solution.py:26
  8.8 1.5 %collective-permute-start.1 = (bf16[2,256,128]{2,1,0:T(8,128)(2,1)}, bf16[2,256,128]{2,1,0:T(8,128)(2,1)S(1)}, u32[]{:S(2)}, u32[]{:S(2)}) collective-permute-start(bf16[2,256,128]{2,1,0:T(8,128)(2,1)} %get-tuple-element.28.refs_0_), channel_id=1, source_target_pairs={{0,2},{1,3},{2,0},{3,1},{4,6},{5,7},{6,4},{7,5},{8,10},{9,11},{10,... | collective-permute-start | bytes 393224 | tf_op jit(solution)/shard_map/ppermute | solution.py:31
  10.4 0.5 collective-permute-start
  10.9 1.4 %collective-permute-start.5 = (bf16[64,16,128]{2,1,0:T(8,128)(2,1)}, bf16[64,16,128]{2,1,0:T(8,128)(2,1)}, u32[]{:S(2)}, u32[]{:S(2)}) collective-permute-start(bf16[64,16,128]{2,1,0:T(8,128)(2,1)} %get-tuple-element.38), channel_id=1, source_target_pairs={{0,28},{4,0},{8,4},{12,8},{16,12},{20,16},{24,20},{28,24},{1,29},{... | collective-permute-start | bytes 786440 | tf_op jit(solution)/shard_map/ppermute | solution.py:26
  12.5 1.5 %collective-permute-done.1.refs_1_ = bf16[2,256,128]{2,1,0:T(8,128)(2,1)S(1)} collective-permute-done((bf16[2,256,128]{2,1,0:T(8,128)(2,1)}, bf16[2,256,128]{2,1,0:T(8,128)(2,1)S(1)}, u32[]{:S(2)}, u32[]{:S(2)}) %collective-permute-start.1) | collective-permute-done | bytes 131104 | tf_op jit(solution)/shard_map/ppermute | solution.py:31
  14.0 0.5 collective-permute-start.6
  14.5 1.3 %collective-permute-done.4 = bf16[64,16,128]{2,1,0:T(8,128)(2,1)S(1)} collective-permute-done((bf16[64,16,128]{2,1,0:T(8,128)(2,1)}, bf16[64,16,128]{2,1,0:T(8,128)(2,1)S(1)}, u32[]{:S(2)}, u32[]{:S(2)}) %collective-permute-start.4) | collective-permute-done | bytes 262176 | tf_op jit(solution)/shard_map/ppermute | solution.py:26
  16.0 0.6 %copy-done.19 = bf16[2,256,128]{2,1,0:T(8,128)(2,1)} copy-done((bf16[2,256,128]{2,1,0:T(8,128)(2,1)}, bf16[2,256,128]{2,1,0:T(8,128)(2,1)S(1)}, u32[]{:S(2)}) %copy-start.19) | copy-done | bytes 131096
  17.2 0.9 %copy-done.20 = bf16[2,256,128]{2,1,0:T(8,128)(2,1)S(1)} copy-done((bf16[2,256,128]{2,1,0:T(8,128)(2,1)S(1)}, bf16[2,256,128]{2,1,0:T(8,128)(2,1)}, u32[]{:S(2)}) %copy-start.20) | copy-done | bytes 131096
  18.1 0.8 %shard_map.95 = (bf16[1024,128]{1,0:T(8,128)(2,1)S(1)}, bf16[1024,256]{1,0:T(8,128)(2,1)S(1)}, bf16[128,1024]{1,0:T(8,128)(2,1)S(1)}) custom-call(s32[8]{0:T(128)S(1)} %copy-done.17, bf16[2,256,128]{2,1,0:T(8,128)(2,1)S(1)} %copy-done.18, bf16[2,256,128]{2,1,0:T(8,128)(2,1)S(1)} %collective-permute-done.1.refs_1_, bf16[2,256,128]{2,1,0:T(8,128)(2,1)S(1)} %copy-done.20, ...), custom_call_target="tpu_custom_call" | custom-call | flops 1000000000 | bytes 1048576 | tf_op jit(solution)/shard_map/pallas_call | solution.py:131
  18.9 3.1 %shard_map.97 = (f32[128,1024]{1,0:T(8,128)S(1)}, f32[1024,256]{1,0:T(8,128)S(1)}) custom-call(s32[8]{0:T(128)S(1)} %copy-done.17, bf16[4096,128]{1,0:T(8,128)(2,1)S(1)} %bitcast.13, bf16[1024,256]{1,0:T(8,128)(2,1)S(1)} %shard_map.96.g_ref, bf16[4096,128]{1,0:T(8,128)(2,1)S(1)} %bitcast.18, f32[1,4096]{1,0:T(1,128)S(1)} %reshape.33.lse_ref, ...), custom_call_target="tpu_custom_call" | custom-call | flops 2013265920 | bytes 2097152 | tf_op jit(solution)/shard_map/pallas_call | solution.py:333
  22.1 3.9 %shard_map.98 = (f32[128,1024]{1,0:T(8,128)S(1)}, f32[1024,256]{1,0:T(8,128)S(1)}, f32[128,256]{1,0:T(8,128)S(1)}, bf16[4,128,256]{2,1,0:T(8,128)(2,1)}) custom-call(s32[8]{0:T(128)S(1)} %copy-done.17, bf16[4096,128]{1,0:T(8,128)(2,1)S(1)} %bitcast.14, bf16[1024,128]{1,0:T(8,128)(2,1)S(1)} %bitcast.22, bf16[4096,128]{1,0:T(8,128)(2,1)S(1)} %bitcast.19, ...), custom_call_target="tpu_custom_call" | custom-call | flops 2013265920 | bytes 2097152 | tf_op jit(solution)/shard_map/pallas_call | solution.py:333
  26.0 1.0 %copy-done.2 = f32[1024,256]{1,0:T(8,128)} copy-done((f32[1024,256]{1,0:T(8,128)}, f32[1024,256]{1,0:T(8,128)S(1)}, u32[]{:S(2)}) %copy-start.2) | copy-done | bytes 1048600
  27.0 0.8 %copy-done.9 = f32[128,1024]{1,0:T(8,128)} copy-done((f32[128,1024]{1,0:T(8,128)}, f32[128,1024]{1,0:T(8,128)S(1)}, u32[]{:S(2)}) %copy-start.9) | copy-done | bytes 524312
  27.8 4.1 %all-to-all-start = ((bf16[4,128,256]{2,1,0:T(8,128)(2,1)}), bf16[4,128,256]{2,1,0:T(8,128)(2,1)S(1)}, u32[]{:S(2)}, u32[]{:S(2)}) async-start(bf16[4,128,256]{2,1,0:T(8,128)(2,1)} %get-tuple-element.35), calls=%async_computation | async-start | bytes 524288 | tf_op jit(solution)/shard_map/all_to_all | solution.py:350
  31.9 1.2 %copy-done.3 = f32[1024,256]{1,0:T(8,128)S(1)} copy-done((f32[1024,256]{1,0:T(8,128)S(1)}, f32[1024,256]{1,0:T(8,128)}, u32[]{:S(2)}) %copy-start.3) | copy-done | bytes 1048600
  33.2 0.9 %copy-done.5 = bf16[128,1024]{1,0:T(8,128)(2,1)S(1)} copy-done((bf16[128,1024]{1,0:T(8,128)(2,1)S(1)}, bf16[128,1024]{1,0:T(8,128)(2,1)}, u32[]{:S(2)}) %copy-start.5) | copy-done | bytes 262168
  34.1 2.8 %shard_map.99 = (f32[128,1024]{1,0:T(8,128)S(1)}, f32[512,256]{1,0:T(8,128)S(1)}) custom-call(s32[8]{0:T(128)S(1)} %copy-done.17, bf16[4096,128]{1,0:T(8,128)(2,1)S(1)} %bitcast.15, bf16[1024,128]{1,0:T(8,128)(2,1)} %bitcast.7.g_ref, bf16[4096,128]{1,0:T(8,128)(2,1)S(1)} %bitcast.20, f32[1,4096]{1,0:T(1,128)S(1)} %reshape.33.lse_ref, ...), custom_call_target="tpu_custom_call" | custom-call | flops 671088640 | bytes 2097152 | tf_op jit(solution)/shard_map/pallas_call | solution.py:333
  36.9 0.8 %copy-done.11 = f32[128,1024]{1,0:T(8,128)} copy-done((f32[128,1024]{1,0:T(8,128)}, f32[128,1024]{1,0:T(8,128)S(1)}, u32[]{:S(2)}) %copy-start.11) | copy-done | bytes 524312
  37.7 0.8 %copy-done.15 = f32[512,256]{1,0:T(8,128)} copy-done((f32[512,256]{1,0:T(8,128)}, f32[512,256]{1,0:T(8,128)S(1)}, u32[]{:S(2)}) %copy-start.15) | copy-done | bytes 524312
  38.5 0.9 %copy-done.6 = bf16[128,1024]{1,0:T(8,128)(2,1)S(1)} copy-done((bf16[128,1024]{1,0:T(8,128)(2,1)S(1)}, bf16[128,1024]{1,0:T(8,128)(2,1)}, u32[]{:S(2)}) %copy-start.6) | copy-done | bytes 262168
  39.5 1.0 %copy-done.16 = f32[512,256]{1,0:T(8,128)S(1)} copy-done((f32[512,256]{1,0:T(8,128)S(1)}, f32[512,256]{1,0:T(8,128)}, u32[]{:S(2)}) %copy-start.16) | copy-done | bytes 524312
  40.5 3.5 %shard_map.100 = (f32[128,1024]{1,0:T(8,128)S(1)}, f32[128,256]{1,0:T(8,128)S(1)}, bf16[4,128,256]{2,1,0:T(8,128)(2,1)}) custom-call(s32[8]{0:T(128)S(1)} %copy-done.17, bf16[4096,128]{1,0:T(8,128)(2,1)S(1)} %bitcast.16, bf16[1024,128]{1,0:T(8,128)(2,1)} %bitcast.8.g_ref, bf16[4096,128]{1,0:T(8,128)(2,1)S(1)} %bitcast.21, f32[1,4096]{1,0:T(1,128)S(1)} %reshape.33.lse_ref, ...), custom_call_target="tpu_custom_call" | custom-call | flops 671088640 | bytes 2097152 | tf_op jit(solution)/shard_map/pallas_call | solution.py:333
  44.0 0.8 %copy-done.13 = f32[128,1024]{1,0:T(8,128)} copy-done((f32[128,1024]{1,0:T(8,128)}, f32[128,1024]{1,0:T(8,128)S(1)}, u32[]{:S(2)}) %copy-start.13) | copy-done | bytes 524312
  44.8 3.5 %all-to-all-start.1 = ((bf16[4,128,256]{2,1,0:T(8,128)(2,1)}), bf16[4,128,256]{2,1,0:T(8,128)(2,1)S(1)}, u32[]{:S(2)}, u32[]{:S(2)}) async-start(bf16[4,128,256]{2,1,0:T(8,128)(2,1)} %get-tuple-element.47), calls=%async_computation.1 | async-start | bytes 524288 | tf_op jit(solution)/shard_map/all_to_all | solution.py:350
  48.4 1.0 %copy-done.10 = f32[128,1024]{1,0:T(8,128)S(1)} copy-done((f32[128,1024]{1,0:T(8,128)S(1)}, f32[128,1024]{1,0:T(8,128)}, u32[]{:S(2)}) %copy-start.10) | copy-done | bytes 524312
  49.4 1.0 %copy-done.12 = f32[128,1024]{1,0:T(8,128)S(1)} copy-done((f32[128,1024]{1,0:T(8,128)S(1)}, f32[128,1024]{1,0:T(8,128)}, u32[]{:S(2)}) %copy-start.12) | copy-done | bytes 524312
  50.4 1.0 %copy-done.14 = f32[128,1024]{1,0:T(8,128)S(1)} copy-done((f32[128,1024]{1,0:T(8,128)S(1)}, f32[128,1024]{1,0:T(8,128)}, u32[]{:S(2)}) %copy-start.14) | copy-done | bytes 524312
  51.5 1.1 %shard_map.101 = (bf16[128,256]{1,0:T(8,128)(2,1)S(1)}, bf16[4096,128]{1,0:T(8,128)(2,1)}) custom-call(f32[128,256]{1,0:T(8,128)S(1)} %get-tuple-element.34.refs_0_.own_ref, bf16[4,128,256]{2,1,0:T(8,128)(2,1)S(1)} %all-to-all-done.refs_1_.terms_ref, f32[128,1024]{1,0:T(8,128)S(1)} %copy-done.8, f32[128,1024]{1,0:T(8,128)S(1)} %copy-done.10, ...), custom_call_target="tpu_custom_call" | custom-call | tf_op jit(solution)/shard_map/pallas_call | solution.py:261
  52.6 1.7 %all-to-all-done.1.terms_ref = bf16[4,128,256]{2,1,0:T(8,128)(2,1)S(1)} async-done(((bf16[4,128,256]{2,1,0:T(8,128)(2,1)}), bf16[4,128,256]{2,1,0:T(8,128)(2,1)S(1)}, u32[]{:S(2)}, u32[]{:S(2)}) %all-to-all-start.1) | async-done | bytes 262176 | tf_op jit(solution)/shard_map/all_to_all | solution.py:350
  54.3 0.7 %shard_map.102 = (bf16[256,128]{1,0:T(8,128)(2,1)}, bf16[256,128]{1,0:T(8,128)(2,1)}) custom-call(f32[128,256]{1,0:T(8,128)S(1)} %get-tuple-element.46.own_ref, bf16[4,128,256]{2,1,0:T(8,128)(2,1)S(1)} %all-to-all-done.1.terms_ref, bf16[128,256]{1,0:T(8,128)(2,1)S(1)} %get-tuple-element.48.upper_ref), custom_call_target="tpu_custom_call" | custom-call | tf_op jit(solution)/shard_map/pallas_call | solution.py:354
  (41 shorter events, 0.9 us)
Async XLA Ops:
  0.6 15.2 %copy-start.1 = (bf16[1,256,16,128]{3,2,1,0:T(8,128)(2,1)S(1)}, bf16[1,256,16,128]{3,2,1,0:T(8,128)(2,1)}, u32[]{:S(2)}) copy-start(bf16[1,256,16,128]{3,2,1,0:T(8,128)(2,1)} %param.10) | copy-start | bytes 3145732
  0.6 11.6 %copy-start.21 = (f32[1,16,256]{2,1,0:T(8,128)S(1)}, f32[1,16,256]{2,1,0:T(8,128)}, u32[]{:S(2)}) copy-start(f32[1,16,256]{2,1,0:T(8,128)} %param.12) | copy-start | bytes 49156
  2.8 13.1 %collective-permute-start.4 = (bf16[64,16,128]{2,1,0:T(8,128)(2,1)}, bf16[64,16,128]{2,1,0:T(8,128)(2,1)S(1)}, u32[]{:S(2)}, u32[]{:S(2)}) collective-permute-start(bf16[64,16,128]{2,1,0:T(8,128)(2,1)} %get-tuple-element.32), channel_id=1, source_target_pairs={{0,28},{4,0},{8,4},{12,8},{16,12},{20,16},{24,20},{28,24},{1,29},{... | collective-permute-start | bytes 786440 | tf_op jit(solution)/shard_map/ppermute | solution.py:26
  8.8 5.2 %collective-permute-start.1 = (bf16[2,256,128]{2,1,0:T(8,128)(2,1)}, bf16[2,256,128]{2,1,0:T(8,128)(2,1)S(1)}, u32[]{:S(2)}, u32[]{:S(2)}) collective-permute-start(bf16[2,256,128]{2,1,0:T(8,128)(2,1)} %get-tuple-element.28.refs_0_), channel_id=1, source_target_pairs={{0,2},{1,3},{2,0},{3,1},{4,6},{5,7},{6,4},{7,5},{8,10},{9,11},{10,... | collective-permute-start | bytes 393224 | tf_op jit(solution)/shard_map/ppermute | solution.py:31
  10.3 5.7 %collective-permute-start.2 = (bf16[2,256,128]{2,1,0:T(8,128)(2,1)}, bf16[2,256,128]{2,1,0:T(8,128)(2,1)S(1)}, u32[]{:S(2)}, u32[]{:S(2)}) collective-permute-start(bf16[2,256,128]{2,1,0:T(8,128)(2,1)} %get-tuple-element.28.refs_0_), channel_id=1, source_target_pairs={{0,1},{1,0},{2,3},{3,2},{4,5},{5,4},{6,7},{7,6},{8,9},{9,8},{10,11... | collective-permute-start | bytes 393224 | tf_op jit(solution)/shard_map/ppermute | solution.py:31
  10.4 11.7 %collective-permute-start = (bf16[64,16,128]{2,1,0:T(8,128)(2,1)}, bf16[64,16,128]{2,1,0:T(8,128)(2,1)S(1)}, u32[]{:S(2)}, u32[]{:S(2)}) collective-permute-start(bf16[64,16,128]{2,1,0:T(8,128)(2,1)} %get-tuple-element.27), channel_id=1, source_target_pairs={{0,28},{4,0},{8,4},{12,8},{16,12},{20,16},{24,20},{28,24},{1,29},{... | collective-permute-start | bytes 786440 | tf_op jit(solution)/shard_map/ppermute | solution.py:26
  10.9 21.0 %collective-permute-start.5 = (bf16[64,16,128]{2,1,0:T(8,128)(2,1)}, bf16[64,16,128]{2,1,0:T(8,128)(2,1)}, u32[]{:S(2)}, u32[]{:S(2)}) collective-permute-start(bf16[64,16,128]{2,1,0:T(8,128)(2,1)} %get-tuple-element.38), channel_id=1, source_target_pairs={{0,28},{4,0},{8,4},{12,8},{16,12},{20,16},{24,20},{28,24},{1,29},{... | collective-permute-start | bytes 786440 | tf_op jit(solution)/shard_map/ppermute | solution.py:26
  14.0 24.5 %collective-permute-start.6 = (bf16[64,16,128]{2,1,0:T(8,128)(2,1)}, bf16[64,16,128]{2,1,0:T(8,128)(2,1)}, u32[]{:S(2)}, u32[]{:S(2)}) collective-permute-start(bf16[64,16,128]{2,1,0:T(8,128)(2,1)} %get-tuple-element.42), channel_id=1, source_target_pairs={{0,28},{4,0},{8,4},{12,8},{16,12},{20,16},{24,20},{28,24},{1,29},{... | collective-permute-start | bytes 786440 | tf_op jit(solution)/shard_map/ppermute | solution.py:26
  15.9 1.3 %collective-permute-start.3 = (bf16[2,256,128]{2,1,0:T(8,128)(2,1)S(1)}, bf16[2,256,128]{2,1,0:T(8,128)(2,1)S(1)}, u32[]{:S(2)}, u32[]{:S(2)}) collective-permute-start(bf16[2,256,128]{2,1,0:T(8,128)(2,1)S(1)} %collective-permute-done.1.refs_1_), channel_id=1, source_target_pairs={{0,1},{1,0},{2,3},{3,2},{4,5},{5,4},{6,7},{7,6},{8,9},{9,8},{10,11... | collective-permute-start | bytes 393224 | tf_op jit(solution)/shard_map/ppermute | solution.py:31
  15.9 1.3 %copy-start.17 = (s32[8]{0:T(128)S(1)}, s32[8]{0:T(128)}, u32[]{:S(2)}) copy-start(s32[8]{0:T(128)} %starts_ref.9) | copy-start | bytes 100
  15.9 1.3 %copy-start.18 = (bf16[2,256,128]{2,1,0:T(8,128)(2,1)S(1)}, bf16[2,256,128]{2,1,0:T(8,128)(2,1)}, u32[]{:S(2)}) copy-start(bf16[2,256,128]{2,1,0:T(8,128)(2,1)} %get-tuple-element.28.refs_0_) | copy-start | bytes 393220
  16.0 2.9 %copy-start = (bf16[1,256,16,128]{3,2,1,0:T(8,128)(2,1)S(1)}, bf16[1,256,16,128]{3,2,1,0:T(8,128)(2,1)}, u32[]{:S(2)}) copy-start(bf16[1,256,16,128]{3,2,1,0:T(8,128)(2,1)} %param.7) | copy-start | bytes 3145732
  16.0 0.7 %copy-start.19 = (bf16[2,256,128]{2,1,0:T(8,128)(2,1)}, bf16[2,256,128]{2,1,0:T(8,128)(2,1)S(1)}, u32[]{:S(2)}) copy-start(bf16[2,256,128]{2,1,0:T(8,128)(2,1)S(1)} %collective-permute-done.2.refs_2_) | copy-start | bytes 393220
  17.2 0.9 %copy-start.20 = (bf16[2,256,128]{2,1,0:T(8,128)(2,1)S(1)}, bf16[2,256,128]{2,1,0:T(8,128)(2,1)}, u32[]{:S(2)}) copy-start(bf16[2,256,128]{2,1,0:T(8,128)(2,1)} %copy-done.19) | copy-start | bytes 393220
  18.9 3.2 %copy-start.4 = (bf16[128,1024]{1,0:T(8,128)(2,1)}, bf16[128,1024]{1,0:T(8,128)(2,1)S(1)}, u32[]{:S(2)}) copy-start(bf16[128,1024]{1,0:T(8,128)(2,1)S(1)} %get-tuple-element.31.keys_t_ref) | copy-start | bytes 786436
  22.1 4.0 %copy-start.7 = (f32[128,1024]{1,0:T(8,128)}, f32[128,1024]{1,0:T(8,128)S(1)}, u32[]{:S(2)}) copy-start(f32[128,1024]{1,0:T(8,128)S(1)} %get-tuple-element.36.refs_0_) | copy-start | bytes 1572868
  26.0 1.0 %copy-start.2 = (f32[1024,256]{1,0:T(8,128)}, f32[1024,256]{1,0:T(8,128)S(1)}, u32[]{:S(2)}) copy-start(f32[1024,256]{1,0:T(8,128)S(1)} %get-tuple-element.39.refs_0_) | copy-start | bytes 3145732
  27.0 0.8 %copy-start.9 = (f32[128,1024]{1,0:T(8,128)}, f32[128,1024]{1,0:T(8,128)S(1)}, u32[]{:S(2)}) copy-start(f32[128,1024]{1,0:T(8,128)S(1)} %get-tuple-element.37.refs_1_) | copy-start | bytes 1572868
  27.8 10.7 %all-to-all-start = ((bf16[4,128,256]{2,1,0:T(8,128)(2,1)}), bf16[4,128,256]{2,1,0:T(8,128)(2,1)S(1)}, u32[]{:S(2)}, u32[]{:S(2)}) async-start(bf16[4,128,256]{2,1,0:T(8,128)(2,1)} %get-tuple-element.35), calls=%async_computation | async-start | bytes 524288 | tf_op jit(solution)/shard_map/all_to_all | solution.py:350
  31.9 1.2 %copy-start.3 = (f32[1024,256]{1,0:T(8,128)S(1)}, f32[1024,256]{1,0:T(8,128)}, u32[]{:S(2)}) copy-start(f32[1024,256]{1,0:T(8,128)} %copy-done.2) | copy-start | bytes 3145732
  33.1 0.9 %copy-start.5 = (bf16[128,1024]{1,0:T(8,128)(2,1)S(1)}, bf16[128,1024]{1,0:T(8,128)(2,1)}, u32[]{:S(2)}) copy-start(bf16[128,1024]{1,0:T(8,128)(2,1)} %copy-done.4) | copy-start | bytes 786436
  36.9 0.8 %copy-start.11 = (f32[128,1024]{1,0:T(8,128)}, f32[128,1024]{1,0:T(8,128)S(1)}, u32[]{:S(2)}) copy-start(f32[128,1024]{1,0:T(8,128)S(1)} %get-tuple-element.40.refs_2_) | copy-start | bytes 1572868
  37.7 0.8 %copy-start.15 = (f32[512,256]{1,0:T(8,128)}, f32[512,256]{1,0:T(8,128)S(1)}, u32[]{:S(2)}) copy-start(f32[512,256]{1,0:T(8,128)S(1)} %get-tuple-element.43.refs_2_) | copy-start | bytes 1572868
  38.5 1.0 %copy-start.6 = (bf16[128,1024]{1,0:T(8,128)(2,1)S(1)}, bf16[128,1024]{1,0:T(8,128)(2,1)}, u32[]{:S(2)}) copy-start(bf16[128,1024]{1,0:T(8,128)(2,1)} %copy-done.4) | copy-start | bytes 786436
  39.5 1.0 %copy-start.16 = (f32[512,256]{1,0:T(8,128)S(1)}, f32[512,256]{1,0:T(8,128)}, u32[]{:S(2)}) copy-start(f32[512,256]{1,0:T(8,128)} %copy-done.15) | copy-start | bytes 1572868
  44.0 0.8 %copy-start.13 = (f32[128,1024]{1,0:T(8,128)}, f32[128,1024]{1,0:T(8,128)S(1)}, u32[]{:S(2)}) copy-start(f32[128,1024]{1,0:T(8,128)S(1)} %get-tuple-element.44.refs_3_) | copy-start | bytes 1572868
  44.8 3.5 %copy-start.8 = (f32[128,1024]{1,0:T(8,128)S(1)}, f32[128,1024]{1,0:T(8,128)}, u32[]{:S(2)}) copy-start(f32[128,1024]{1,0:T(8,128)} %copy-done.7) | copy-start | bytes 1572868
  44.8 9.5 %all-to-all-start.1 = ((bf16[4,128,256]{2,1,0:T(8,128)(2,1)}), bf16[4,128,256]{2,1,0:T(8,128)(2,1)S(1)}, u32[]{:S(2)}, u32[]{:S(2)}) async-start(bf16[4,128,256]{2,1,0:T(8,128)(2,1)} %get-tuple-element.47), calls=%async_computation.1 | async-start | bytes 524288 | tf_op jit(solution)/shard_map/all_to_all | solution.py:350
  48.4 1.0 %copy-start.10 = (f32[128,1024]{1,0:T(8,128)S(1)}, f32[128,1024]{1,0:T(8,128)}, u32[]{:S(2)}) copy-start(f32[128,1024]{1,0:T(8,128)} %copy-done.9) | copy-start | bytes 1572868
  49.4 1.0 %copy-start.12 = (f32[128,1024]{1,0:T(8,128)S(1)}, f32[128,1024]{1,0:T(8,128)}, u32[]{:S(2)}) copy-start(f32[128,1024]{1,0:T(8,128)} %copy-done.11) | copy-start | bytes 1572868
  50.4 1.0 %copy-start.14 = (f32[128,1024]{1,0:T(8,128)S(1)}, f32[128,1024]{1,0:T(8,128)}, u32[]{:S(2)}) copy-start(f32[128,1024]{1,0:T(8,128)} %copy-done.13) | copy-start | bytes 1572868

commit v7 on v4

--- a/solution.py
+++ b/solution.py
@@ -11,6 +11,8 @@
 KEY_BLOCK = 256
 CHUNK_TOKENS = 64
 VMEM_LIMIT = 40 * 1024 * 1024
+SORT_FLOPS = 10**9
+WIDEN_FLOPS = 4 * 10**9
 
 WHOLE = pl.BlockSpec(memory_space=pltpu.VMEM)
 SCALARS = pl.BlockSpec(memory_space=pltpu.SMEM)
@@ -30,6 +32,60 @@
 
 def params(limit=VMEM_LIMIT):
     return pltpu.CompilerParams(vmem_limit_bytes=limit)
+
+
+def cut_kernel(cuts, source_ref, starts_ref, *refs):
+    *out_refs, sems = refs
+    copies = [
+        pltpu.make_async_copy(source_ref.at[pl.ds(first, size)], out_ref, sems.at[i])
+        for i, ((first, size), out_ref) in enumerate(zip(cuts, out_refs))
+    ]
+    for copy in copies:
+        copy.start()
+    for copy in copies:
+        copy.wait()
+
+
+def cut(source, span_start, cuts):
+    return pl.pallas_call(
+        functools.partial(cut_kernel, cuts),
+        out_shape=[
+            jax.ShapeDtypeStruct((size, *source.shape[1:]), source.dtype) for _, size in cuts
+        ],
+        in_specs=[ANYWHERE, WHOLE],
+        out_specs=[ANYWHERE] * len(cuts),
+        scratch_shapes=[pltpu.SemaphoreType.DMA((len(cuts),))],
+        compiler_params=params(),
+        cost_estimate=pl.CostEstimate(
+            flops=0, bytes_accessed=2 * source.size * source.dtype.itemsize, transcendentals=0
+        ),
+    )(source, span_start)
+
+
+def widen_kernel(rows, g_ref, o_ref, *refs):
+    wide_ref = refs[-1]
+    head_size = g_ref.shape[1]
+    g = g_ref[...]
+    wide_ref[:, :head_size] = g
+    wide_ref[:, head_size:] = times(g, o_ref[rows, :])
+
+
+def widen(grad, outputs, first, *others):
+    row_count, head_size = grad.shape
+    return pl.pallas_call(
+        functools.partial(widen_kernel, slice(first, first + row_count)),
+        out_shape=jax.ShapeDtypeStruct((row_count, 2 * head_size), grad.dtype),
+        in_specs=[WHOLE] * (2 + len(others)),
+        out_specs=WHOLE,
+        compiler_params=params(),
+        cost_estimate=pl.CostEstimate(
+            flops=WIDEN_FLOPS, bytes_accessed=grad.size * 8, transcendentals=0
+        ),
+    )(grad, outputs, *others)
+
+
+def times(g, o):
+    return (g.astype(jnp.float32) * o.astype(jnp.float32)).astype(jnp.bfloat16)
 
 
 def sort_keys_kernel(codes, span_rows, head_size, starts_ref, *refs):
@@ -65,6 +121,9 @@
         in_specs=[SCALARS] + [WHOLE] * count,
         out_specs=(WHOLE,) * 3,
         compiler_params=params(),
+        cost_estimate=pl.CostEstimate(
+            flops=SORT_FLOPS, bytes_accessed=8 * total * head_size, transcendentals=0
+        ),
     )(span_start, *blocks)
 
 
@@ -85,8 +144,10 @@
 
     q = q_ref[rows, :]
     g = g_ref[...]
-    products = (g.astype(jnp.float32) * o_ref[rows, :].astype(jnp.float32)).astype(jnp.bfloat16)
-    g_wide = jnp.concatenate([g, products], axis=1)
+    if g.shape[1] == head_size:
+        g_wide = jnp.concatenate([g, times(g, o_ref[rows, :])], axis=1)
+    else:
+        g, g_wide = g[:, :head_size], g
     lse2 = lse_ref[0:1, rows] * to_log2
     dq_ref[...] = jnp.zeros_like(dq_ref)
 
@@ -205,19 +266,21 @@
     ]
     per_half = len(chunks) // 2
 
-    cuts = [half * span_rows + first for half, first, _ in chunks]
-    pieces = [grad_held[0, cuts[0] : cuts[0] + CHUNK_TOKENS]]
-    pieces[0], rest = lax.optimization_barrier((pieces[0], grad_held[0]))
-    pieces += [rest[at : at + CHUNK_TOKENS] for at in cuts[1:]]
-    grads = [from_behind(piece, "section", -1) for piece in pieces]
-
-    pair = jnp.concatenate([keys, values], axis=0)
+    pieces = cut(
+        grad_held[0], span_start, [(half * span_rows + first, size) for half, first, size in chunks]
+    )
+    grads = [from_behind(pieces[0], "section", -1)]
+    pair = jnp.concatenate(lax.optimization_barrier((keys, values, pieces[0]))[:2], axis=0)
     blocks, codes = [pair], [0]
     step = count // 2
     while step:
         blocks = blocks + [with_partner(block, "ctx", step) for block in blocks]
         codes = codes + [code ^ step for code in codes]
         step //= 2
+    for piece, gate in zip(pieces[1:], [None, None] + [blocks[1]] * len(pieces)):
+        if gate is not None:
+            piece, _ = lax.optimization_barrier((piece, gate))
+        grads.append(from_behind(piece, "section", -1))
     sorted_keys = sort_keys(span_start, blocks, codes, span_rows, head_size)
 
     q_flat = queries.reshape(row_count * heads, head_size)
@@ -234,8 +297,11 @@
         after = received if is_last else []
         if after:
             upper_terms = received
+        grad = grads[number].reshape(rows, head_size)
+        if is_first:
+            grad = widen(grad, o_flat, (half * span_rows + chunk[1]) * heads)
         operands = [
-            q_flat, grads[number].reshape(rows, head_size), o_flat, lse_flat, *sorted_keys, *after,
+            q_flat, grad, o_flat, lse_flat, *sorted_keys, *after,
             *running,
         ]
         total_shape = (total if half else total // 2, 2 * head_size)

time: 45.2 us -> 40.5 us (0.90)
  local copies, waits for them, and re-layouts: 6.37 us -> 3.05 us
  starting transfers between devices: 17.5 us -> 15 us
  waiting for transfers between devices: 6.52 us -> 7.13 us
    ppermute x9, waiting for transfers between devices: 2.46 us -> 6.56 us  [with_partner(): return lax.ppermute(shard, axis, [(i, i ^ step) for i in range(length)])]
    ppermute x4, waiting for transfers between devices: 4.06 us -> 0.57 us  [from_behind(): lax.ppermute(shard, axis, [(i, (i + by) % length) for i in range(length)])]
    slice x1 -> x0, local copies, waits for them, and re-layouts: 2.01 us -> none  [body(): pieces += [rest[at:at + CHUNK_TOKENS] for at in cuts[1:]]]
    unnamed x11 -> x15, local copies, waits for them, and re-layouts: 0.9 us -> 2.83 us
    ppermute x9, starting transfers between devices: 8.35 us -> 6.57 us  [with_partner(): return lax.ppermute(shard, axis, [(i, i ^ step) for i in range(length)])]
    squeeze x1 -> x0, local copies, waits for them, and re-layouts: 1.68 us -> none  [body(): pieces = [grad_held[0, cuts[0]:cuts[0] + CHUNK_TOKENS]]]
    reshape x1, local copies, waits for them, and re-layouts: 1.01 us -> 0.11 us  [body(): lse_flat = lse[0].T.reshape(1, row_count * heads)]
    transpose x1, local copies, waits for them, and re-layouts: 0.76 us -> 0.1 us  [body(): lse_flat = lse[0].T.reshape(1, row_count * heads)]
  transfers between devices with their start and end apart: 13 -> 13, of which waited for: 3 -> 8; matrix products, arithmetic and copies ran while one was open for 12% -> 3% of each run, Pallas kernels for 24% -> 27%
where the time goes in v7:
time: 40.5 us; the launch traced here: 40.1 us
  starting transfers between devices  15 us (37%)
  Pallas kernels  14.1 us (35%)
  waiting for transfers between devices  7.13 us (18%)
  local copies, waits for them, and re-layouts  3.05 us (8%)
  between operations  0.79 us (2%)
    pallas_call x4, Pallas kernels, body(): pl.pallas_call(functools.partial(chunk_kernel, chunk, heads, span_rows, c...  11.3 us
    ppermute x4, starting transfers between devices, from_behind(): lax.ppermute(shard, axis, [(i, (i + by) % length) for i in range(length)])  8.48 us
    ppermute x9, starting transfers between devices, with_partner(): return lax.ppermute(shard, axis, [(i, i ^ step) for i in range(length)])  6.57 us
    ppermute x9, waiting for transfers between devices, with_partner(): return lax.ppermute(shard, axis, [(i, i ^ step) for i in range(length)])  6.56 us
    unnamed x15, local copies, waits for them, and re-layouts  2.83 us
    pallas_call x1, Pallas kernels, finish(): pl.pallas_call(functools.partial(finish_kernel, len(terms), places), out_...  1.13 us
  transfers between devices with their start and end apart: 13, of which 8 were waited for; matrix products, arithmetic and copies ran while one was open for 3% of the time, Pallas kernels for 27%

profile of v7, /device:TPU:0, one launch (start us, length us, event | category | flops | bytes accessed | tf_op | source)
XLA Modules:
  0.0 40.1 jit_solution(7342537785424238947)
XLA Ops:
  0.7 1.3 %copy-done.2 = bf16[1,256,16,128]{3,2,1,0:T(8,128)(2,1)S(1)} copy-done((bf16[1,256,16,128]{3,2,1,0:T(8,128)(2,1)S(1)}, bf16[1,256,16,128]{3,2,1,0:T(8,128)(2,1)}, u32[]{:S(2)}) %copy-start.2) | copy-done | bytes 1048600
  2.0 0.7 %copy-done.3 = s32[8]{0:T(128)S(1)} copy-done((s32[8]{0:T(128)S(1)}, s32[8]{0:T(128)}, u32[]{:S(2)}) %copy-start.3) | copy-done | bytes 56
  2.6 0.1 shard_map.94
  2.7 6.0 %collective-permute-start.4 = (bf16[64,16,128]{2,1,0:T(8,128)(2,1)S(1)}, bf16[64,16,128]{2,1,0:T(8,128)(2,1)S(1)}, u32[]{:S(2)}, u32[]{:S(2)}) collective-permute-start(bf16[64,16,128]{2,1,0:T(8,128)(2,1)S(1)} %get-tuple-element.33), channel_id=1, source_target_pairs={{0,28},{4,0},{8,4},{12,8},{16,12},{20,16},{24,20},{28,24},{1,29},{... | collective-permute-start | bytes 786440 | tf_op jit(solution)/shard_map/ppermute | solution.py:25
  8.8 0.8 %constant_dynamic-update-slice_fusion.1 = bf16[2,256,128]{2,1,0:T(8,128)(2,1)S(1)} fusion(bf16[1,256,128]{2,1,0:T(8,128)(2,1)} %param.8), kind=kLoop, calls=%fused_computation.1 | loop fusion | bytes 131072
  9.6 1.6 %collective-permute-start.1 = (bf16[2,256,128]{2,1,0:T(8,128)(2,1)S(1)}, bf16[2,256,128]{2,1,0:T(8,128)(2,1)S(1)}, u32[]{:S(2)}, u32[]{:S(2)}) collective-permute-start(bf16[2,256,128]{2,1,0:T(8,128)(2,1)S(1)} %constant_dynamic-update-slice_fusion.refs_0_), channel_id=1, source_target_pairs={{0,2},{1,3},{2,0},{3,1},{4,6},{5,7},{6,4},{7,5},{8,10},{9,11},{10,... | collective-permute-start | bytes 393224 | tf_op jit(solution)/shard_map/ppermute | solution.py:30
  11.2 0.5 %collective-permute-start = (bf16[64,16,128]{2,1,0:T(8,128)(2,1)S(1)}, bf16[64,16,128]{2,1,0:T(8,128)(2,1)S(1)}, u32[]{:S(2)}, u32[]{:S(2)}) collective-permute-start(bf16[64,16,128]{2,1,0:T(8,128)(2,1)S(1)} %get-tuple-element.32), channel_id=1, source_target_pairs={{0,28},{4,0},{8,4},{12,8},{16,12},{20,16},{24,20},{28,24},{1,29},{... | collective-permute-start | bytes 786440 | tf_op jit(solution)/shard_map/ppermute | solution.py:25
  11.8 1.4 %collective-permute-start.8 = (bf16[64,16,128]{2,1,0:T(8,128)(2,1)S(1)}, bf16[64,16,128]{2,1,0:T(8,128)(2,1)S(1)}, u32[]{:S(2)}, u32[]{:S(2)}) collective-permute-start(bf16[64,16,128]{2,1,0:T(8,128)(2,1)S(1)} %get-tuple-element.46), channel_id=1, source_target_pairs={{0,28},{4,0},{8,4},{12,8},{16,12},{20,16},{24,20},{28,24},{1,29},{... | collective-permute-start | bytes 786440 | tf_op jit(solution)/shard_map/ppermute | solution.py:25
  13.1 0.1 copy.11
  13.2 0.1 reshape.33.lse_ref
  13.4 1.3 %collective-permute-done.1.refs_1_ = bf16[2,256,128]{2,1,0:T(8,128)(2,1)S(1)} collective-permute-done((bf16[2,256,128]{2,1,0:T(8,128)(2,1)S(1)}, bf16[2,256,128]{2,1,0:T(8,128)(2,1)S(1)}, u32[]{:S(2)}, u32[]{:S(2)}) %collective-permute-start.1) | collective-permute-done | bytes 131104 | tf_op jit(solution)/shard_map/ppermute | solution.py:30
  14.7 0.5 %collective-permute-start.9 = (bf16[64,16,128]{2,1,0:T(8,128)(2,1)S(1)}, bf16[64,16,128]{2,1,0:T(8,128)(2,1)S(1)}, u32[]{:S(2)}, u32[]{:S(2)}) collective-permute-start(bf16[64,16,128]{2,1,0:T(8,128)(2,1)S(1)} %get-tuple-element.50), channel_id=1, source_target_pairs={{0,28},{4,0},{8,4},{12,8},{16,12},{20,16},{24,20},{28,24},{1,29},{... | collective-permute-start | bytes 786440 | tf_op jit(solution)/shard_map/ppermute | solution.py:25
  15.2 0.3 collective-permute-done.4
  15.5 0.1 shard_map.96.g_ref
  15.6 1.2 %collective-permute-done.3.refs_3_ = bf16[2,256,128]{2,1,0:T(8,128)(2,1)S(1)} collective-permute-done((bf16[2,256,128]{2,1,0:T(8,128)(2,1)S(1)}, bf16[2,256,128]{2,1,0:T(8,128)(2,1)S(1)}, u32[]{:S(2)}, u32[]{:S(2)}) %collective-permute-start.3) | collective-permute-done | bytes 131104 | tf_op jit(solution)/shard_map/ppermute | solution.py:30
  16.8 0.8 %shard_map.95 = (bf16[1024,128]{1,0:T(8,128)(2,1)S(1)}, bf16[1024,256]{1,0:T(8,128)(2,1)S(1)}, bf16[128,1024]{1,0:T(8,128)(2,1)S(1)}) custom-call(s32[8]{0:T(128)S(1)} %copy-done.4, bf16[2,256,128]{2,1,0:T(8,128)(2,1)S(1)} %constant_dynamic-update-slice_fusion.refs_0_, bf16[2,256,128]{2,1,0:T(8,128)(2,1)S(1)} %collective-permute-done.1.refs_1_, ...), custom_call_target="tpu_custom_call" | custom-call | flops 1000000000 | bytes 1048576 | tf_op jit(solution)/shard_map/pallas_call | solution.py:114
  17.6 3.2 %shard_map.97 = (f32[128,1024]{1,0:T(8,128)S(1)}, f32[1024,256]{1,0:T(8,128)S(1)}) custom-call(s32[8]{0:T(128)S(1)} %copy-done.4, bf16[4096,128]{1,0:T(8,128)(2,1)S(1)} %bitcast.13, bf16[1024,256]{1,0:T(8,128)(2,1)S(1)} %shard_map.96.g_ref, bf16[4096,128]{1,0:T(8,128)(2,1)S(1)} %bitcast.18, f32[1,4096]{1,0:T(1,128)S(1)} %reshape.33.lse_ref, ...), custom_call_target="tpu_custom_call" | custom-call | flops 2013265920 | bytes 2097152 | tf_op jit(solution)/shard_map/pallas_call | solution.py:315
  20.8 0.3 collective-permute-done
  21.1 3.3 %shard_map.98 = (f32[128,1024]{1,0:T(8,128)S(1)}, f32[1024,256]{1,0:T(8,128)S(1)}, f32[128,256]{1,0:T(8,128)S(1)}, bf16[128,256]{1,0:T(8,128)(2,1)S(1)}, bf16[12...) custom-call(s32[8]{0:T(128)S(1)} %copy-done.4, bf16[4096,128]{1,0:T(8,128)(2,1)S(1)} %bitcast.14, ...), custom_call_target="tpu_custom_call" | custom-call | flops 2013265920 | bytes 2097152 | tf_op jit(solution)/shard_map/pallas_call | solution.py:315
  24.4 0.1 collective-permute-start.5
  24.4 3.0 %collective-permute-start.6 = (bf16[128,256]{1,0:T(8,128)(2,1)S(1)}, bf16[128,256]{1,0:T(8,128)(2,1)S(1)}, u32[]{:S(2)}, u32[]{:S(2)}) collective-permute-start(bf16[128,256]{1,0:T(8,128)(2,1)S(1)} %get-tuple-element.42), channel_id=1, source_target_pairs={{0,2},{1,3},{2,0},{3,1},{4,6},{5,7},{6,4},{7,5},{8,10},{9,11},{10,... | collective-permute-start | bytes 196616 | tf_op jit(solution)/shard_map/ppermute | solution.py:30
  27.4 2.4 %shard_map.99 = (f32[128,1024]{1,0:T(8,128)S(1)}, f32[512,256]{1,0:T(8,128)S(1)}) custom-call(s32[8]{0:T(128)S(1)} %copy-done.4, bf16[4096,128]{1,0:T(8,128)(2,1)S(1)} %bitcast.15, bf16[1024,128]{1,0:T(8,128)(2,1)S(1)} %bitcast.24, bf16[4096,128]{1,0:T(8,128)(2,1)S(1)} %bitcast.20, f32[1,4096]{1,0:T(1,128)S(1)} %reshape.33.lse_ref, ...), custom_call_target="tpu_custom_call" | custom-call | flops 671088640 | bytes 2097152 | tf_op jit(solution)/shard_map/pallas_call | solution.py:315
  29.9 0.2 collective-permute-done.6.refs_2_
  30.0 1.5 %collective-permute-done.7.refs_3_ = bf16[128,256]{1,0:T(8,128)(2,1)S(1)} collective-permute-done((bf16[128,256]{1,0:T(8,128)(2,1)S(1)}, bf16[128,256]{1,0:T(8,128)(2,1)S(1)}, u32[]{:S(2)}, u32[]{:S(2)}) %collective-permute-start.7) | collective-permute-done | bytes 65568 | tf_op jit(solution)/shard_map/ppermute | solution.py:30
  31.6 2.4 %shard_map.100 = (f32[128,1024]{1,0:T(8,128)S(1)}, f32[128,256]{1,0:T(8,128)S(1)}, bf16[128,256]{1,0:T(8,128)(2,1)S(1)}, bf16[128,256]{1,0:T(8,128)(2,1)S(1)}, bf16[128,256]{1,0:T(8,128)(2,1)S(1)}) custom-call(s32[8]{0:T(128)S(1)} %copy-done.4, bf16[4096,128]{1,0:T(8,128)(2,1)S(1)} %bitcast.16, bf16[1024,128]{1,0:T(8,128)(2,1)S(1)} %bitcast.23, ...), custom_call_target="tpu_custom_call" | custom-call | flops 671088640 | bytes 2097152 | tf_op jit(solution)/shard_map/pallas_call | solution.py:315
  34.0 0.2 collective-permute-start.10
  34.2 0.5 %collective-permute-start.11 = (bf16[128,256]{1,0:T(8,128)(2,1)S(1)}, bf16[128,256]{1,0:T(8,128)(2,1)S(1)}, u32[]{:S(2)}, u32[]{:S(2)}) collective-permute-start(bf16[128,256]{1,0:T(8,128)(2,1)S(1)} %get-tuple-element.56), channel_id=1, source_target_pairs={{0,2},{1,3},{2,0},{3,1},{4,6},{5,7},{6,4},{7,5},{8,10},{9,11},{10,... | collective-permute-start | bytes 196616 | tf_op jit(solution)/shard_map/ppermute | solution.py:30
  34.7 1.2 %collective-permute-start.12 = (bf16[128,256]{1,0:T(8,128)(2,1)S(1)}, bf16[128,256]{1,0:T(8,128)(2,1)S(1)}, u32[]{:S(2)}, u32[]{:S(2)}) collective-permute-start(bf16[128,256]{1,0:T(8,128)(2,1)S(1)} %get-tuple-element.57), channel_id=1, source_target_pairs={{0,3},{1,2},{2,1},{3,0},{4,7},{5,6},{6,5},{7,4},{8,11},{9,10},{10,... | collective-permute-start | bytes 196616 | tf_op jit(solution)/shard_map/ppermute | solution.py:30
  35.9 1.1 %shard_map.101 = (bf16[128,256]{1,0:T(8,128)(2,1)S(1)}, bf16[4096,128]{1,0:T(8,128)(2,1)}) custom-call(f32[128,256]{1,0:T(8,128)S(1)} %get-tuple-element.40.refs_0_, bf16[128,256]{1,0:T(8,128)(2,1)S(1)} %collective-permute-done.5.refs_1_, bf16[128,256]{1,0:T(8,128)(2,1)S(1)} %collective-permute-done.6.refs_2_, ...), custom_call_target="tpu_custom_call" | custom-call | tf_op jit(solution)/shard_map/pallas_call | solution.py:243
  37.1 2.0 %collective-permute-done.11.refs_2_ = bf16[128,256]{1,0:T(8,128)(2,1)S(1)} collective-permute-done((bf16[128,256]{1,0:T(8,128)(2,1)S(1)}, bf16[128,256]{1,0:T(8,128)(2,1)S(1)}, u32[]{:S(2)}, u32[]{:S(2)}) %collective-permute-start.11) | collective-permute-done | bytes 65568 | tf_op jit(solution)/shard_map/ppermute | solution.py:30
  39.1 0.3 collective-permute-done.12.refs_3_
  39.4 0.7 %shard_map.102 = (bf16[256,128]{1,0:T(8,128)(2,1)}, bf16[256,128]{1,0:T(8,128)(2,1)}) custom-call(f32[128,256]{1,0:T(8,128)S(1)} %get-tuple-element.54.refs_0_, bf16[128,256]{1,0:T(8,128)(2,1)S(1)} %collective-permute-done.10.refs_1_, bf16[128,256]{1,0:T(8,128)(2,1)S(1)} %collective-permute-done.11.refs_2_, ...), custom_call_target="tpu_custom_call" | custom-call | tf_op jit(solution)/shard_map/pallas_call | solution.py:338
  (21 shorter events, 0.1 us)
Async XLA Ops:
  0.6 14.9 %copy-start.1 = (bf16[1,256,16,128]{3,2,1,0:T(8,128)(2,1)S(1)}, bf16[1,256,16,128]{3,2,1,0:T(8,128)(2,1)}, u32[]{:S(2)}) copy-start(bf16[1,256,16,128]{3,2,1,0:T(8,128)(2,1)} %param.10) | copy-start | bytes 3145732
  0.6 1.3 %copy-start.2 = (bf16[1,256,16,128]{3,2,1,0:T(8,128)(2,1)S(1)}, bf16[1,256,16,128]{3,2,1,0:T(8,128)(2,1)}, u32[]{:S(2)}) copy-start(bf16[1,256,16,128]{3,2,1,0:T(8,128)(2,1)} %param.11) | copy-start | bytes 3145732
  2.0 0.7 %copy-start.3 = (s32[8]{0:T(128)S(1)}, s32[8]{0:T(128)}, u32[]{:S(2)}) copy-start(s32[8]{0:T(128)} %starts_ref.11) | copy-start | bytes 100
  2.7 6.9 %copy-start.5 = (bf16[1,256,128]{2,1,0:T(8,128)(2,1)S(1)}, bf16[1,256,128]{2,1,0:T(8,128)(2,1)}, u32[]{:S(2)}) copy-start(bf16[1,256,128]{2,1,0:T(8,128)(2,1)} %param.9) | copy-start | bytes 196612
  2.7 12.7 %collective-permute-start.4 = (bf16[64,16,128]{2,1,0:T(8,128)(2,1)S(1)}, bf16[64,16,128]{2,1,0:T(8,128)(2,1)S(1)}, u32[]{:S(2)}, u32[]{:S(2)}) collective-permute-start(bf16[64,16,128]{2,1,0:T(8,128)(2,1)S(1)} %get-tuple-element.33), channel_id=1, source_target_pairs={{0,28},{4,0},{8,4},{12,8},{16,12},{20,16},{24,20},{28,24},{1,29},{... | collective-permute-start | bytes 786440 | tf_op jit(solution)/shard_map/ppermute | solution.py:25
  9.6 3.5 %copy-start.6 = (f32[1,16,256]{2,1,0:T(8,128)S(1)}, f32[1,16,256]{2,1,0:T(8,128)}, u32[]{:S(2)}) copy-start(f32[1,16,256]{2,1,0:T(8,128)} %param.12) | copy-start | bytes 49156
  9.6 5.0 %collective-permute-start.1 = (bf16[2,256,128]{2,1,0:T(8,128)(2,1)S(1)}, bf16[2,256,128]{2,1,0:T(8,128)(2,1)S(1)}, u32[]{:S(2)}, u32[]{:S(2)}) collective-permute-start(bf16[2,256,128]{2,1,0:T(8,128)(2,1)S(1)} %constant_dynamic-update-slice_fusion.refs_0_), channel_id=1, source_target_pairs={{0,2},{1,3},{2,0},{3,1},{4,6},{5,7},{6,4},{7,5},{8,10},{9,11},{10,... | collective-permute-start | bytes 393224 | tf_op jit(solution)/shard_map/ppermute | solution.py:30
  11.2 4.4 %collective-permute-start.2 = (bf16[2,256,128]{2,1,0:T(8,128)(2,1)S(1)}, bf16[2,256,128]{2,1,0:T(8,128)(2,1)S(1)}, u32[]{:S(2)}, u32[]{:S(2)}) collective-permute-start(bf16[2,256,128]{2,1,0:T(8,128)(2,1)S(1)} %constant_dynamic-update-slice_fusion.refs_0_), channel_id=1, source_target_pairs={{0,1},{1,0},{2,3},{3,2},{4,5},{5,4},{6,7},{7,6},{8,9},{9,8},{10,11... | collective-permute-start | bytes 393224 | tf_op jit(solution)/shard_map/ppermute | solution.py:30
  11.2 9.9 %collective-permute-start = (bf16[64,16,128]{2,1,0:T(8,128)(2,1)S(1)}, bf16[64,16,128]{2,1,0:T(8,128)(2,1)S(1)}, u32[]{:S(2)}, u32[]{:S(2)}) collective-permute-start(bf16[64,16,128]{2,1,0:T(8,128)(2,1)S(1)} %get-tuple-element.32), channel_id=1, source_target_pairs={{0,28},{4,0},{8,4},{12,8},{16,12},{20,16},{24,20},{28,24},{1,29},{... | collective-permute-start | bytes 786440 | tf_op jit(solution)/shard_map/ppermute | solution.py:25
  11.8 15.7 %collective-permute-start.8 = (bf16[64,16,128]{2,1,0:T(8,128)(2,1)S(1)}, bf16[64,16,128]{2,1,0:T(8,128)(2,1)S(1)}, u32[]{:S(2)}, u32[]{:S(2)}) collective-permute-start(bf16[64,16,128]{2,1,0:T(8,128)(2,1)S(1)} %get-tuple-element.46), channel_id=1, source_target_pairs={{0,28},{4,0},{8,4},{12,8},{16,12},{20,16},{24,20},{28,24},{1,29},{... | collective-permute-start | bytes 786440 | tf_op jit(solution)/shard_map/ppermute | solution.py:25
  14.7 16.9 %collective-permute-start.9 = (bf16[64,16,128]{2,1,0:T(8,128)(2,1)S(1)}, bf16[64,16,128]{2,1,0:T(8,128)(2,1)S(1)}, u32[]{:S(2)}, u32[]{:S(2)}) collective-permute-start(bf16[64,16,128]{2,1,0:T(8,128)(2,1)S(1)} %get-tuple-element.50), channel_id=1, source_target_pairs={{0,28},{4,0},{8,4},{12,8},{16,12},{20,16},{24,20},{28,24},{1,29},{... | collective-permute-start | bytes 786440 | tf_op jit(solution)/shard_map/ppermute | solution.py:25
  15.5 1.3 %collective-permute-start.3 = (bf16[2,256,128]{2,1,0:T(8,128)(2,1)S(1)}, bf16[2,256,128]{2,1,0:T(8,128)(2,1)S(1)}, u32[]{:S(2)}, u32[]{:S(2)}) collective-permute-start(bf16[2,256,128]{2,1,0:T(8,128)(2,1)S(1)} %collective-permute-done.1.refs_1_), channel_id=1, source_target_pairs={{0,1},{1,0},{2,3},{3,2},{4,5},{5,4},{6,7},{7,6},{8,9},{9,8},{10,11... | collective-permute-start | bytes 393224 | tf_op jit(solution)/shard_map/ppermute | solution.py:30
  15.5 1.3 %copy-start.4 = (s32[8]{0:T(128)S(1)}, s32[8]{0:T(128)}, u32[]{:S(2)}) copy-start(s32[8]{0:T(128)} %starts_ref.11) | copy-start | bytes 100
  15.6 2.0 %copy-start = (bf16[1,256,16,128]{3,2,1,0:T(8,128)(2,1)S(1)}, bf16[1,256,16,128]{3,2,1,0:T(8,128)(2,1)}, u32[]{:S(2)}) copy-start(bf16[1,256,16,128]{3,2,1,0:T(8,128)(2,1)} %param.7) | copy-start | bytes 3145732
  24.4 5.5 %collective-permute-start.5 = (bf16[128,256]{1,0:T(8,128)(2,1)S(1)}, bf16[128,256]{1,0:T(8,128)(2,1)S(1)}, u32[]{:S(2)}, u32[]{:S(2)}) collective-permute-start(bf16[128,256]{1,0:T(8,128)(2,1)S(1)} %get-tuple-element.41), channel_id=1, source_target_pairs={{0,1},{1,0},{2,3},{3,2},{4,5},{5,4},{6,7},{7,6},{8,9},{9,8},{10,11... | collective-permute-start | bytes 196616 | tf_op jit(solution)/shard_map/ppermute | solution.py:30
  24.4 5.6 %collective-permute-start.6 = (bf16[128,256]{1,0:T(8,128)(2,1)S(1)}, bf16[128,256]{1,0:T(8,128)(2,1)S(1)}, u32[]{:S(2)}, u32[]{:S(2)}) collective-permute-start(bf16[128,256]{1,0:T(8,128)(2,1)S(1)} %get-tuple-element.42), channel_id=1, source_target_pairs={{0,2},{1,3},{2,0},{3,1},{4,6},{5,7},{6,4},{7,5},{8,10},{9,11},{10,... | collective-permute-start | bytes 196616 | tf_op jit(solution)/shard_map/ppermute | solution.py:30
  27.4 4.1 %collective-permute-start.7 = (bf16[128,256]{1,0:T(8,128)(2,1)S(1)}, bf16[128,256]{1,0:T(8,128)(2,1)S(1)}, u32[]{:S(2)}, u32[]{:S(2)}) collective-permute-start(bf16[128,256]{1,0:T(8,128)(2,1)S(1)} %get-tuple-element.43), channel_id=1, source_target_pairs={{0,3},{1,2},{2,1},{3,0},{4,7},{5,6},{6,5},{7,4},{8,11},{9,10},{10,... | collective-permute-start | bytes 196616 | tf_op jit(solution)/shard_map/ppermute | solution.py:30
  34.0 3.1 %collective-permute-start.10 = (bf16[128,256]{1,0:T(8,128)(2,1)S(1)}, bf16[128,256]{1,0:T(8,128)(2,1)S(1)}, u32[]{:S(2)}, u32[]{:S(2)}) collective-permute-start(bf16[128,256]{1,0:T(8,128)(2,1)S(1)} %get-tuple-element.55), channel_id=1, source_target_pairs={{0,1},{1,0},{2,3},{3,2},{4,5},{5,4},{6,7},{7,6},{8,9},{9,8},{10,11... | collective-permute-start | bytes 196616 | tf_op jit(solution)/shard_map/ppermute | solution.py:30
  34.2 4.9 %collective-permute-start.11 = (bf16[128,256]{1,0:T(8,128)(2,1)S(1)}, bf16[128,256]{1,0:T(8,128)(2,1)S(1)}, u32[]{:S(2)}, u32[]{:S(2)}) collective-permute-start(bf16[128,256]{1,0:T(8,128)(2,1)S(1)} %get-tuple-element.56), channel_id=1, source_target_pairs={{0,2},{1,3},{2,0},{3,1},{4,6},{5,7},{6,4},{7,5},{8,10},{9,11},{10,... | collective-permute-start | bytes 196616 | tf_op jit(solution)/shard_map/ppermute | solution.py:30
  34.7 4.7 %collective-permute-start.12 = (bf16[128,256]{1,0:T(8,128)(2,1)S(1)}, bf16[128,256]{1,0:T(8,128)(2,1)S(1)}, u32[]{:S(2)}, u32[]{:S(2)}) collective-permute-start(bf16[128,256]{1,0:T(8,128)(2,1)S(1)} %get-tuple-element.57), channel_id=1, source_target_pairs={{0,3},{1,2},{2,1},{3,0},{4,7},{5,6},{6,5},{7,4},{8,11},{9,10},{10,... | collective-permute-start | bytes 196616 | tf_op jit(solution)/shard_map/ppermute | solution.py:30

commit v8 on v7

--- a/solution.py
+++ b/solution.py
@@ -12,7 +12,7 @@
 CHUNK_TOKENS = 64
 VMEM_LIMIT = 40 * 1024 * 1024
 SORT_FLOPS = 10**9
-WIDEN_FLOPS = 4 * 10**9
+WIDEN_FLOPS = 4*10**9
 
 WHOLE = pl.BlockSpec(memory_space=pltpu.VMEM)
 SCALARS = pl.BlockSpec(memory_space=pltpu.SMEM)
@@ -34,7 +34,7 @@
     return pltpu.CompilerParams(vmem_limit_bytes=limit)
 
 
-def cut_kernel(cuts, source_ref, starts_ref, *refs):
+def cut_kernel(cuts, source_ref, *refs):
     *out_refs, sems = refs
     copies = [
         pltpu.make_async_copy(source_ref.at[pl.ds(first, size)], out_ref, sems.at[i])
@@ -46,20 +46,20 @@
         copy.wait()
 
 
-def cut(source, span_start, cuts):
+def cut(source, cuts):
     return pl.pallas_call(
         functools.partial(cut_kernel, cuts),
         out_shape=[
             jax.ShapeDtypeStruct((size, *source.shape[1:]), source.dtype) for _, size in cuts
         ],
-        in_specs=[ANYWHERE, WHOLE],
+        in_specs=[ANYWHERE],
         out_specs=[ANYWHERE] * len(cuts),
         scratch_shapes=[pltpu.SemaphoreType.DMA((len(cuts),))],
         compiler_params=params(),
         cost_estimate=pl.CostEstimate(
             flops=0, bytes_accessed=2 * source.size * source.dtype.itemsize, transcendentals=0
         ),
-    )(source, span_start)
+    )(source)
 
 
 def widen_kernel(rows, g_ref, o_ref, *refs):
@@ -89,28 +89,27 @@
 
 
 def sort_keys_kernel(codes, span_rows, head_size, starts_ref, *refs):
-    count = len(codes)
-    blocks = refs[:count]
-    keys_ref, values_ref, keys_t_ref = refs[count:]
+    held_ref, got_ref, keys_ref, values_ref, keys_t_ref = refs
+    half_count = len(codes) // 2
+    blocks = [(ref, 2 * i) for ref in (held_ref, got_ref) for i in range(half_count)]
     me = lax.axis_index("ctx")
     values_ref[:, head_size:] = jnp.full(
         (values_ref.shape[0], values_ref.shape[1] - head_size), -1.0, values_ref.dtype
     )
-    for block, code in zip(blocks, codes):
+    for (block, at), code in zip(blocks, codes):
         owner = lax.bitwise_xor(me, code)
         for half in range(2):
             start = pl.multiple_of(starts_ref[2 * owner + half], span_rows)
             rows = pl.ds(start, span_rows)
             part = slice(half * span_rows, (half + 1) * span_rows)
-            keys = block[0, part, :]
+            keys = block[at, part, :]
             keys_ref[rows, :] = keys
-            values_ref[rows, :head_size] = block[1, part, :]
+            values_ref[rows, :head_size] = block[at + 1, part, :]
             keys_t_ref[:, rows] = keys.astype(jnp.float32).T.astype(jnp.bfloat16)
 
 
 def sort_keys(span_start, blocks, codes, span_rows, head_size):
-    count = len(blocks)
-    total = count * 2 * span_rows
+    total = len(codes) * 2 * span_rows
     return pl.pallas_call(
         functools.partial(sort_keys_kernel, codes, span_rows, head_size),
         out_shape=(
@@ -118,7 +117,7 @@
             jax.ShapeDtypeStruct((total, 2 * head_size), jnp.bfloat16),
             jax.ShapeDtypeStruct((head_size, total), jnp.bfloat16),
         ),
-        in_specs=[SCALARS] + [WHOLE] * count,
+        in_specs=[SCALARS] + [WHOLE] * len(blocks),
         out_specs=(WHOLE,) * 3,
         compiler_params=params(),
         cost_estimate=pl.CostEstimate(
@@ -266,22 +265,21 @@
     ]
     per_half = len(chunks) // 2
 
-    pieces = cut(
-        grad_held[0], span_start, [(half * span_rows + first, size) for half, first, size in chunks]
-    )
+    pieces = cut(grad_held[0], [(half * span_rows + first, size) for half, first, size in chunks])
     grads = [from_behind(pieces[0], "section", -1)]
     pair = jnp.concatenate(lax.optimization_barrier((keys, values, pieces[0]))[:2], axis=0)
-    blocks, codes = [pair], [0]
-    step = count // 2
+    gathered, codes, step = pair, [0], count // 2
     while step:
-        blocks = blocks + [with_partner(block, "ctx", step) for block in blocks]
+        held, gathered = gathered, with_partner(gathered, "ctx", step)
         codes = codes + [code ^ step for code in codes]
+        if step > 1:
+            gathered = jnp.concatenate([held, gathered], axis=0)
         step //= 2
-    for piece, gate in zip(pieces[1:], [None, None] + [blocks[1]] * len(pieces)):
+    for piece, gate in zip(pieces[1:], [None] * (len(pieces) - 2) + [pair]):
         if gate is not None:
             piece, _ = lax.optimization_barrier((piece, gate))
         grads.append(from_behind(piece, "section", -1))
-    sorted_keys = sort_keys(span_start, blocks, codes, span_rows, head_size)
+    sorted_keys = sort_keys(span_start, [held, gathered], codes, span_rows, head_size)
 
     q_flat = queries.reshape(row_count * heads, head_size)
     o_flat = outputs.reshape(row_count * heads, head_size)
@@ -294,8 +292,8 @@
         rows = tokens * heads
         is_first, is_last = number == 0, number == len(chunks) - 1
         hands_out = number % per_half == per_half - 1
-        after = received if is_last else []
-        if after:
+        after = received[:2] if is_last else []
+        if is_last:
             upper_terms = received
         grad = grads[number].reshape(rows, head_size)
         if is_first:

time: 40.5 us -> 39.9 us (0.985)
  waiting for transfers between devices: 7.13 us -> 5.33 us
  local copies, waits for them, and re-layouts: 3.05 us -> 4.59 us
  starting transfers between devices: 15 us -> 14.5 us
    ppermute x9 -> x8, waiting for transfers between devices: 6.56 us -> 5.25 us  [with_partner(): return lax.ppermute(shard, axis, [(i, i ^ step) for i in range(length)])]
    concatenate x0 -> x1, local copies, waits for them, and re-layouts: none -> 0.92 us  [body(): gathered = jnp.concatenate([held, gathered], axis=0)]
    concatenate x1, local copies, waits for them, and re-layouts: 0.01 us -> 0.64 us  [body(): jnp.concatenate(lax.optimization_barrier((keys, values, pieces[0]))[:2],...]
    ppermute x9 -> x8, starting transfers between devices: 6.57 us -> 6.04 us  [with_partner(): return lax.ppermute(shard, axis, [(i, i ^ step) for i in range(length)])]
    ppermute x4, waiting for transfers between devices: 0.57 us -> 0.08 us  [from_behind(): lax.ppermute(shard, axis, [(i, (i + by) % length) for i in range(length)])]
    unnamed x15 -> x13, local copies, waits for them, and re-layouts: 2.83 us -> 2.82 us
  transfers between devices with their start and end apart: 13 -> 12, of which waited for: 8 -> 5; matrix products, arithmetic and copies ran while one was open for 3% -> 8% of each run, Pallas kernels for 27% -> 34%
where the time goes in v8:
time: 39.9 us; the launch traced here: 39.4 us
  starting transfers between devices  14.5 us (36%)
  Pallas kernels  14.1 us (35%)
  waiting for transfers between devices  5.33 us (13%)
  local copies, waits for them, and re-layouts  4.59 us (12%)
  between operations  0.81 us (2%)
    pallas_call x4, Pallas kernels, body(): pl.pallas_call(functools.partial(chunk_kernel, chunk, heads, span_rows, c...  11.3 us
    ppermute x4, starting transfers between devices, from_behind(): lax.ppermute(shard, axis, [(i, (i + by) % length) for i in range(length)])  8.49 us
    ppermute x8, starting transfers between devices, with_partner(): return lax.ppermute(shard, axis, [(i, i ^ step) for i in range(length)])  6.04 us
    ppermute x8, waiting for transfers between devices, with_partner(): return lax.ppermute(shard, axis, [(i, i ^ step) for i in range(length)])  5.25 us
    unnamed x13, local copies, waits for them, and re-layouts  2.82 us
    pallas_call x1, Pallas kernels, finish(): pl.pallas_call(functools.partial(finish_kernel, len(terms), places), out_...  1.13 us
    concatenate x1, local copies, waits for them, and re-layouts, body(): gathered = jnp.concatenate([held, gathered], axis=0)  0.92 us
  transfers between devices with their start and end apart: 12, of which 5 were waited for; matrix products, arithmetic and copies ran while one was open for 8% of the time, Pallas kernels for 34%

profile of v8, /device:TPU:0, one launch (start us, length us, event | category | flops | bytes accessed | tf_op | source)
XLA Modules:
  0.0 39.4 jit_solution(8124995941272394443)
XLA Ops:
  0.7 1.3 %copy-done.2 = bf16[1,256,16,128]{3,2,1,0:T(8,128)(2,1)S(1)} copy-done((bf16[1,256,16,128]{3,2,1,0:T(8,128)(2,1)S(1)}, bf16[1,256,16,128]{3,2,1,0:T(8,128)(2,1)}, u32[]{:S(2)}) %copy-start.2) | copy-done | bytes 1048600
  2.0 0.1 shard_map.94
  2.1 6.0 %collective-permute-start.3 = (bf16[64,16,128]{2,1,0:T(8,128)(2,1)S(1)}, bf16[64,16,128]{2,1,0:T(8,128)(2,1)S(1)}, u32[]{:S(2)}, u32[]{:S(2)}) collective-permute-start(bf16[64,16,128]{2,1,0:T(8,128)(2,1)S(1)} %get-tuple-element.33), channel_id=1, source_target_pairs={{0,28},{4,0},{8,4},{12,8},{16,12},{20,16},{24,20},{28,24},{1,29},{... | collective-permute-start | bytes 786440 | tf_op jit(solution)/shard_map/ppermute | solution.py:25
  8.1 1.5 %constant_dynamic-update-slice_fusion.1 = (bf16[2,256,128]{2,1,0:T(8,128)(2,1)}, bf16[4,256,128]{2,1,0:T(8,128)(2,1)S(1)}) fusion(bf16[1,256,128]{2,1,0:T(8,128)(2,1)} %param.8), kind=kLoop, calls=%fused_computation.1 | loop fusion | bytes 196608
  9.6 0.6 %constant_dynamic-update-slice_fusion = (bf16[2,256,128]{2,1,0:T(8,128)(2,1)}, bf16[4,256,128]{2,1,0:T(8,128)(2,1)S(1)}) fusion(bf16[2,256,128]{2,1,0:T(8,128)(2,1)} %get-tuple-element.63, bf16[1,256,128]{2,1,0:T(8,128)(2,1)S(1)} %copy-done.4, bf16[4,256,128]{2,1,0:T(8,128)(2,1)S(1)} %get-tuple-element.64), kind=kLoop, calls=%fused_computation | loop fusion | bytes 196608 | tf_op jit(solution)/shard_map/concatenate | solution.py:270
  10.3 1.5 %collective-permute-start.1 = (bf16[2,256,128]{2,1,0:T(8,128)(2,1)}, bf16[2,256,128]{2,1,0:T(8,128)(2,1)}, u32[]{:S(2)}, u32[]{:S(2)}) collective-permute-start(bf16[2,256,128]{2,1,0:T(8,128)(2,1)} %get-tuple-element.61), channel_id=1, source_target_pairs={{0,2},{1,3},{2,0},{3,1},{4,6},{5,7},{6,4},{7,5},{8,10},{9,11},{10,... | collective-permute-start | bytes 393224 | tf_op jit(solution)/shard_map/ppermute | solution.py:30
  11.8 0.5 %collective-permute-start = (bf16[64,16,128]{2,1,0:T(8,128)(2,1)S(1)}, bf16[64,16,128]{2,1,0:T(8,128)(2,1)S(1)}, u32[]{:S(2)}, u32[]{:S(2)}) collective-permute-start(bf16[64,16,128]{2,1,0:T(8,128)(2,1)S(1)} %get-tuple-element.32), channel_id=1, source_target_pairs={{0,28},{4,0},{8,4},{12,8},{16,12},{20,16},{24,20},{28,24},{1,29},{... | collective-permute-start | bytes 786440 | tf_op jit(solution)/shard_map/ppermute | solution.py:25
  12.3 1.4 %collective-permute-start.7 = (bf16[64,16,128]{2,1,0:T(8,128)(2,1)S(1)}, bf16[64,16,128]{2,1,0:T(8,128)(2,1)S(1)}, u32[]{:S(2)}, u32[]{:S(2)}) collective-permute-start(bf16[64,16,128]{2,1,0:T(8,128)(2,1)S(1)} %get-tuple-element.46), channel_id=1, source_target_pairs={{0,28},{4,0},{8,4},{12,8},{16,12},{20,16},{24,20},{28,24},{1,29},{... | collective-permute-start | bytes 786440 | tf_op jit(solution)/shard_map/ppermute | solution.py:25
  13.7 0.5 %collective-permute-start.8 = (bf16[64,16,128]{2,1,0:T(8,128)(2,1)S(1)}, bf16[64,16,128]{2,1,0:T(8,128)(2,1)S(1)}, u32[]{:S(2)}, u32[]{:S(2)}) collective-permute-start(bf16[64,16,128]{2,1,0:T(8,128)(2,1)S(1)} %get-tuple-element.50), channel_id=1, source_target_pairs={{0,28},{4,0},{8,4},{12,8},{16,12},{20,16},{24,20},{28,24},{1,29},{... | collective-permute-start | bytes 786440 | tf_op jit(solution)/shard_map/ppermute | solution.py:25
  14.2 0.1 copy.11
  14.3 0.1 reshape.33.lse_ref
  14.5 1.1 %collective-permute-done.1 = bf16[2,256,128]{2,1,0:T(8,128)(2,1)} collective-permute-done((bf16[2,256,128]{2,1,0:T(8,128)(2,1)}, bf16[2,256,128]{2,1,0:T(8,128)(2,1)}, u32[]{:S(2)}, u32[]{:S(2)}) %collective-permute-start.1) | collective-permute-done | bytes 131104 | tf_op jit(solution)/shard_map/ppermute | solution.py:30
  15.5 0.9 %constant_dynamic-update-slice_fusion.2.refs_0_ = bf16[4,256,128]{2,1,0:T(8,128)(2,1)S(1)} fusion(bf16[4,256,128]{2,1,0:T(8,128)(2,1)S(1)} %get-tuple-element.62, bf16[2,256,128]{2,1,0:T(8,128)(2,1)} %collective-permute-done.1), kind=kLoop, calls=%fused_computation.2 | loop fusion | bytes 262144 | tf_op jit(solution)/shard_map/concatenate | solution.py:276
  16.5 0.1 collective-permute-start.2
  16.6 0.0 copy-start.3
  16.6 0.1 shard_map.96.g_ref
  16.7 1.3 %collective-permute-done.2.refs_1_ = bf16[4,256,128]{2,1,0:T(8,128)(2,1)S(1)} collective-permute-done((bf16[4,256,128]{2,1,0:T(8,128)(2,1)S(1)}, bf16[4,256,128]{2,1,0:T(8,128)(2,1)S(1)}, u32[]{:S(2)}, u32[]{:S(2)}) %collective-permute-start.2) | collective-permute-done | bytes 262176 | tf_op jit(solution)/shard_map/ppermute | solution.py:30
  18.1 0.8 %shard_map.95 = (bf16[1024,128]{1,0:T(8,128)(2,1)S(1)}, bf16[1024,256]{1,0:T(8,128)(2,1)S(1)}, bf16[128,1024]{1,0:T(8,128)(2,1)S(1)}) custom-call(s32[8]{0:T(128)S(1)} %copy-done.3, bf16[4,256,128]{2,1,0:T(8,128)(2,1)S(1)} %constant_dynamic-update-slice_fusion.2.refs_0_, bf16[4,256,128]{2,1,0:T(8,128)(2,1)S(1)} %collective-permute-done.2.refs_1_), custom_call_target="tpu_custom_call" | custom-call | flops 1000000000 | bytes 1048576 | tf_op jit(solution)/shard_map/pallas_call | solution.py:113
  18.9 4.0 %shard_map.97 = (f32[128,1024]{1,0:T(8,128)S(1)}, f32[1024,256]{1,0:T(8,128)S(1)}) custom-call(s32[8]{0:T(128)S(1)} %copy-done.3, bf16[4096,128]{1,0:T(8,128)(2,1)S(1)} %bitcast.13, bf16[1024,256]{1,0:T(8,128)(2,1)S(1)} %shard_map.96.g_ref, bf16[4096,128]{1,0:T(8,128)(2,1)S(1)} %bitcast.18, f32[1,4096]{1,0:T(1,128)S(1)} %reshape.33.lse_ref, ...), custom_call_target="tpu_custom_call" | custom-call | flops 2013265920 | bytes 2097152 | tf_op jit(solution)/shard_map/pallas_call | solution.py:313
  22.8 4.1 %shard_map.98 = (f32[128,1024]{1,0:T(8,128)S(1)}, f32[1024,256]{1,0:T(8,128)S(1)}, f32[128,256]{1,0:T(8,128)S(1)}, bf16[128,256]{1,0:T(8,128)(2,1)S(1)}, bf16[12...) custom-call(s32[8]{0:T(128)S(1)} %copy-done.3, bf16[4096,128]{1,0:T(8,128)(2,1)S(1)} %bitcast.14, ...), custom_call_target="tpu_custom_call" | custom-call | flops 2013265920 | bytes 2097152 | tf_op jit(solution)/shard_map/pallas_call | solution.py:313
  26.9 0.2 collective-permute-start.4
  27.1 1.7 %collective-permute-start.6 = (bf16[128,256]{1,0:T(8,128)(2,1)S(1)}, bf16[128,256]{1,0:T(8,128)(2,1)S(1)}, u32[]{:S(2)}, u32[]{:S(2)}) collective-permute-start(bf16[128,256]{1,0:T(8,128)(2,1)S(1)} %get-tuple-element.43), channel_id=1, source_target_pairs={{0,3},{1,2},{2,1},{3,0},{4,7},{5,6},{6,5},{7,4},{8,11},{9,10},{10,... | collective-permute-start | bytes 196616 | tf_op jit(solution)/shard_map/ppermute | solution.py:30
  28.8 1.6 %shard_map.99 = (f32[128,1024]{1,0:T(8,128)S(1)}, f32[512,256]{1,0:T(8,128)S(1)}) custom-call(s32[8]{0:T(128)S(1)} %copy-done.3, bf16[4096,128]{1,0:T(8,128)(2,1)S(1)} %bitcast.15, bf16[1024,128]{1,0:T(8,128)(2,1)S(1)} %bitcast.24, bf16[4096,128]{1,0:T(8,128)(2,1)S(1)} %bitcast.20, f32[1,4096]{1,0:T(1,128)S(1)} %reshape.33.lse_ref, ...), custom_call_target="tpu_custom_call" | custom-call | flops 671088640 | bytes 2097152 | tf_op jit(solution)/shard_map/pallas_call | solution.py:313
  30.5 0.1 collective-permute-done.8
  30.5 1.6 %shard_map.100 = (f32[128,1024]{1,0:T(8,128)S(1)}, f32[128,256]{1,0:T(8,128)S(1)}, bf16[128,256]{1,0:T(8,128)(2,1)S(1)}, bf16[128,256]{1,0:T(8,128)(2,1)S(1)}, bf16[128,256]{1,0:T(8,128)(2,1)S(1)}) custom-call(s32[8]{0:T(128)S(1)} %copy-done.3, bf16[4096,128]{1,0:T(8,128)(2,1)S(1)} %bitcast.16, bf16[1024,128]{1,0:T(8,128)(2,1)S(1)} %bitcast.23, ...), custom_call_target="tpu_custom_call" | custom-call | flops 671088640 | bytes 2097152 | tf_op jit(solution)/shard_map/pallas_call | solution.py:313
  32.2 0.5 %collective-permute-start.9 = (bf16[128,256]{1,0:T(8,128)(2,1)S(1)}, bf16[128,256]{1,0:T(8,128)(2,1)S(1)}, u32[]{:S(2)}, u32[]{:S(2)}) collective-permute-start(bf16[128,256]{1,0:T(8,128)(2,1)S(1)} %get-tuple-element.55), channel_id=1, source_target_pairs={{0,1},{1,0},{2,3},{3,2},{4,5},{5,4},{6,7},{7,6},{8,9},{9,8},{10,11... | collective-permute-start | bytes 196616 | tf_op jit(solution)/shard_map/ppermute | solution.py:30
  32.6 2.0 %collective-permute-start.10 = (bf16[128,256]{1,0:T(8,128)(2,1)S(1)}, bf16[128,256]{1,0:T(8,128)(2,1)S(1)}, u32[]{:S(2)}, u32[]{:S(2)}) collective-permute-start(bf16[128,256]{1,0:T(8,128)(2,1)S(1)} %get-tuple-element.56), channel_id=1, source_target_pairs={{0,2},{1,3},{2,0},{3,1},{4,6},{5,7},{6,4},{7,5},{8,10},{9,11},{10,... | collective-permute-start | bytes 196616 | tf_op jit(solution)/shard_map/ppermute | solution.py:30
  34.6 0.1 collective-permute-start.11
  34.7 1.1 %shard_map.101 = (bf16[128,256]{1,0:T(8,128)(2,1)S(1)}, bf16[4096,128]{1,0:T(8,128)(2,1)}) custom-call(f32[128,256]{1,0:T(8,128)S(1)} %get-tuple-element.40.refs_0_, bf16[128,256]{1,0:T(8,128)(2,1)S(1)} %collective-permute-done.4.refs_1_, bf16[128,256]{1,0:T(8,128)(2,1)S(1)} %collective-permute-done.5.refs_2_, ...), custom_call_target="tpu_custom_call" | custom-call | tf_op jit(solution)/shard_map/pallas_call | solution.py:242
  35.9 1.5 %collective-permute-done.10.refs_2_ = bf16[128,256]{1,0:T(8,128)(2,1)S(1)} collective-permute-done((bf16[128,256]{1,0:T(8,128)(2,1)S(1)}, bf16[128,256]{1,0:T(8,128)(2,1)S(1)}, u32[]{:S(2)}, u32[]{:S(2)}) %collective-permute-start.10) | collective-permute-done | bytes 65568 | tf_op jit(solution)/shard_map/ppermute | solution.py:30
  37.3 1.4 %collective-permute-done.11.refs_3_ = bf16[128,256]{1,0:T(8,128)(2,1)S(1)} collective-permute-done((bf16[128,256]{1,0:T(8,128)(2,1)S(1)}, bf16[128,256]{1,0:T(8,128)(2,1)S(1)}, u32[]{:S(2)}, u32[]{:S(2)}) %collective-permute-start.11) | collective-permute-done | bytes 65568 | tf_op jit(solution)/shard_map/ppermute | solution.py:30
  38.7 0.7 %shard_map.102 = (bf16[256,128]{1,0:T(8,128)(2,1)}, bf16[256,128]{1,0:T(8,128)(2,1)}) custom-call(f32[128,256]{1,0:T(8,128)S(1)} %get-tuple-element.54.refs_0_, bf16[128,256]{1,0:T(8,128)(2,1)S(1)} %collective-permute-done.9.refs_1_, bf16[128,256]{1,0:T(8,128)(2,1)S(1)} %collective-permute-done.10.refs_2_, ...), custom_call_target="tpu_custom_call" | custom-call | tf_op jit(solution)/shard_map/pallas_call | solution.py:336
  (18 shorter events, 0.0 us)
Async XLA Ops:
  0.6 15.9 %copy-start.1 = (bf16[1,256,16,128]{3,2,1,0:T(8,128)(2,1)S(1)}, bf16[1,256,16,128]{3,2,1,0:T(8,128)(2,1)}, u32[]{:S(2)}) copy-start(bf16[1,256,16,128]{3,2,1,0:T(8,128)(2,1)} %param.10) | copy-start | bytes 3145732
  0.6 1.3 %copy-start.2 = (bf16[1,256,16,128]{3,2,1,0:T(8,128)(2,1)S(1)}, bf16[1,256,16,128]{3,2,1,0:T(8,128)(2,1)}, u32[]{:S(2)}) copy-start(bf16[1,256,16,128]{3,2,1,0:T(8,128)(2,1)} %param.11) | copy-start | bytes 3145732
  2.1 7.5 %copy-start.4 = (bf16[1,256,128]{2,1,0:T(8,128)(2,1)S(1)}, bf16[1,256,128]{2,1,0:T(8,128)(2,1)}, u32[]{:S(2)}) copy-start(bf16[1,256,128]{2,1,0:T(8,128)(2,1)} %param.9) | copy-start | bytes 196612
  2.1 14.5 %collective-permute-start.3 = (bf16[64,16,128]{2,1,0:T(8,128)(2,1)S(1)}, bf16[64,16,128]{2,1,0:T(8,128)(2,1)S(1)}, u32[]{:S(2)}, u32[]{:S(2)}) collective-permute-start(bf16[64,16,128]{2,1,0:T(8,128)(2,1)S(1)} %get-tuple-element.33), channel_id=1, source_target_pairs={{0,28},{4,0},{8,4},{12,8},{16,12},{20,16},{24,20},{28,24},{1,29},{... | collective-permute-start | bytes 786440 | tf_op jit(solution)/shard_map/ppermute | solution.py:25
  9.6 4.6 %copy-start.5 = (f32[1,16,256]{2,1,0:T(8,128)S(1)}, f32[1,16,256]{2,1,0:T(8,128)}, u32[]{:S(2)}) copy-start(f32[1,16,256]{2,1,0:T(8,128)} %param.12) | copy-start | bytes 49156
  10.3 5.3 %collective-permute-start.1 = (bf16[2,256,128]{2,1,0:T(8,128)(2,1)}, bf16[2,256,128]{2,1,0:T(8,128)(2,1)}, u32[]{:S(2)}, u32[]{:S(2)}) collective-permute-start(bf16[2,256,128]{2,1,0:T(8,128)(2,1)} %get-tuple-element.61), channel_id=1, source_target_pairs={{0,2},{1,3},{2,0},{3,1},{4,6},{5,7},{6,4},{7,5},{8,10},{9,11},{10,... | collective-permute-start | bytes 393224 | tf_op jit(solution)/shard_map/ppermute | solution.py:30
  11.8 11.1 %collective-permute-start = (bf16[64,16,128]{2,1,0:T(8,128)(2,1)S(1)}, bf16[64,16,128]{2,1,0:T(8,128)(2,1)S(1)}, u32[]{:S(2)}, u32[]{:S(2)}) collective-permute-start(bf16[64,16,128]{2,1,0:T(8,128)(2,1)S(1)} %get-tuple-element.32), channel_id=1, source_target_pairs={{0,28},{4,0},{8,4},{12,8},{16,12},{20,16},{24,20},{28,24},{1,29},{... | collective-permute-start | bytes 786440 | tf_op jit(solution)/shard_map/ppermute | solution.py:25
  12.3 16.5 %collective-permute-start.7 = (bf16[64,16,128]{2,1,0:T(8,128)(2,1)S(1)}, bf16[64,16,128]{2,1,0:T(8,128)(2,1)S(1)}, u32[]{:S(2)}, u32[]{:S(2)}) collective-permute-start(bf16[64,16,128]{2,1,0:T(8,128)(2,1)S(1)} %get-tuple-element.46), channel_id=1, source_target_pairs={{0,28},{4,0},{8,4},{12,8},{16,12},{20,16},{24,20},{28,24},{1,29},{... | collective-permute-start | bytes 786440 | tf_op jit(solution)/shard_map/ppermute | solution.py:25
  13.7 16.9 %collective-permute-start.8 = (bf16[64,16,128]{2,1,0:T(8,128)(2,1)S(1)}, bf16[64,16,128]{2,1,0:T(8,128)(2,1)S(1)}, u32[]{:S(2)}, u32[]{:S(2)}) collective-permute-start(bf16[64,16,128]{2,1,0:T(8,128)(2,1)S(1)} %get-tuple-element.50), channel_id=1, source_target_pairs={{0,28},{4,0},{8,4},{12,8},{16,12},{20,16},{24,20},{28,24},{1,29},{... | collective-permute-start | bytes 786440 | tf_op jit(solution)/shard_map/ppermute | solution.py:25
  16.5 1.6 %collective-permute-start.2 = (bf16[4,256,128]{2,1,0:T(8,128)(2,1)S(1)}, bf16[4,256,128]{2,1,0:T(8,128)(2,1)S(1)}, u32[]{:S(2)}, u32[]{:S(2)}) collective-permute-start(bf16[4,256,128]{2,1,0:T(8,128)(2,1)S(1)} %constant_dynamic-update-slice_fusion.2.refs_0_), channel_id=1, source_target_pairs={{0,1},{1,0},{2,3},{3,2},{4,5},{5,4},{6,7},{7,6},{8,9},{9,8},{10,11... | collective-permute-start | bytes 786440 | tf_op jit(solution)/shard_map/ppermute | solution.py:30
  16.6 1.5 %copy-start.3 = (s32[8]{0:T(128)S(1)}, s32[8]{0:T(128)}, u32[]{:S(2)}) copy-start(s32[8]{0:T(128)} %starts_ref.9) | copy-start | bytes 100
  16.7 2.2 %copy-start = (bf16[1,256,16,128]{3,2,1,0:T(8,128)(2,1)S(1)}, bf16[1,256,16,128]{3,2,1,0:T(8,128)(2,1)}, u32[]{:S(2)}) copy-start(bf16[1,256,16,128]{3,2,1,0:T(8,128)(2,1)} %param.7) | copy-start | bytes 3145732
  26.9 3.6 %collective-permute-start.4 = (bf16[128,256]{1,0:T(8,128)(2,1)S(1)}, bf16[128,256]{1,0:T(8,128)(2,1)S(1)}, u32[]{:S(2)}, u32[]{:S(2)}) collective-permute-start(bf16[128,256]{1,0:T(8,128)(2,1)S(1)} %get-tuple-element.41), channel_id=1, source_target_pairs={{0,1},{1,0},{2,3},{3,2},{4,5},{5,4},{6,7},{7,6},{8,9},{9,8},{10,11... | collective-permute-start | bytes 196616 | tf_op jit(solution)/shard_map/ppermute | solution.py:30
  27.1 7.6 %collective-permute-start.5 = (bf16[128,256]{1,0:T(8,128)(2,1)S(1)}, bf16[128,256]{1,0:T(8,128)(2,1)S(1)}, u32[]{:S(2)}, u32[]{:S(2)}) collective-permute-start(bf16[128,256]{1,0:T(8,128)(2,1)S(1)} %get-tuple-element.42), channel_id=1, source_target_pairs={{0,2},{1,3},{2,0},{3,1},{4,6},{5,7},{6,4},{7,5},{8,10},{9,11},{10,... | collective-permute-start | bytes 196616 | tf_op jit(solution)/shard_map/ppermute | solution.py:30
  27.1 7.6 %collective-permute-start.6 = (bf16[128,256]{1,0:T(8,128)(2,1)S(1)}, bf16[128,256]{1,0:T(8,128)(2,1)S(1)}, u32[]{:S(2)}, u32[]{:S(2)}) collective-permute-start(bf16[128,256]{1,0:T(8,128)(2,1)S(1)} %get-tuple-element.43), channel_id=1, source_target_pairs={{0,3},{1,2},{2,1},{3,0},{4,7},{5,6},{6,5},{7,4},{8,11},{9,10},{10,... | collective-permute-start | bytes 196616 | tf_op jit(solution)/shard_map/ppermute | solution.py:30
  32.2 3.7 %collective-permute-start.9 = (bf16[128,256]{1,0:T(8,128)(2,1)S(1)}, bf16[128,256]{1,0:T(8,128)(2,1)S(1)}, u32[]{:S(2)}, u32[]{:S(2)}) collective-permute-start(bf16[128,256]{1,0:T(8,128)(2,1)S(1)} %get-tuple-element.55), channel_id=1, source_target_pairs={{0,1},{1,0},{2,3},{3,2},{4,5},{5,4},{6,7},{7,6},{8,9},{9,8},{10,11... | collective-permute-start | bytes 196616 | tf_op jit(solution)/shard_map/ppermute | solution.py:30
  32.6 4.7 %collective-permute-start.10 = (bf16[128,256]{1,0:T(8,128)(2,1)S(1)}, bf16[128,256]{1,0:T(8,128)(2,1)S(1)}, u32[]{:S(2)}, u32[]{:S(2)}) collective-permute-start(bf16[128,256]{1,0:T(8,128)(2,1)S(1)} %get-tuple-element.56), channel_id=1, source_target_pairs={{0,2},{1,3},{2,0},{3,1},{4,6},{5,7},{6,4},{7,5},{8,10},{9,11},{10,... | collective-permute-start | bytes 196616 | tf_op jit(solution)/shard_map/ppermute | solution.py:30
  34.6 4.0 %collective-permute-start.11 = (bf16[128,256]{1,0:T(8,128)(2,1)S(1)}, bf16[128,256]{1,0:T(8,128)(2,1)S(1)}, u32[]{:S(2)}, u32[]{:S(2)}) collective-permute-start(bf16[128,256]{1,0:T(8,128)(2,1)S(1)} %get-tuple-element.57), channel_id=1, source_target_pairs={{0,3},{1,2},{2,1},{3,0},{4,7},{5,6},{6,5},{7,4},{8,11},{9,10},{10,... | collective-permute-start | bytes 196616 | tf_op jit(solution)/shard_map/ppermute | solution.py:30
